TPU v7x, 128 devices: a whole 4x4x4 slice. The times are simulated.
128 devices in a mesh: grp: 2 (over z_lo), seq: 8 (over z_hi, y), shard: 8 (over x, core).
Axes of the slice: x: 4, y: 4, z: 4 (z_hi: 2, z_lo: 2; z = z_hi * 2 + z_lo), core: 2. Of those that a mesh axis runs over, the one named last changes fastest.
Arguments:
- tokens: bfloat16 [8, 2048, 2048], P('shard', ('grp', 'seq')), may hold values from -6 to 6
- adapter_ids: int32 [8, 5], P('shard'), may hold values from 0 to 7
- norm_gain_attn: bfloat16 [2048], P(('grp', 'seq', 'shard')), may hold values from 0.5 to 1.5
- norm_gain_mlp: bfloat16 [2048], P(('grp', 'seq', 'shard')), may hold values from 0.5 to 1.5
- qkv_weight: bfloat16 [2048, 3072], P(('grp', 'seq', 'shard')), may hold values from -0.4375 to 0.4375
- output_projection_weight: bfloat16 [2048, 2048], P(('grp', 'seq', 'shard')), may hold values from -1 to 1
- gate_up_weight: bfloat16 [2048, 16384], P(('grp', 'seq', 'shard')), may hold values from -0.125 to 0.125
- down_projection_weight: bfloat16 [8192, 2048], P(('grp', 'seq', 'shard')), may hold values from -0.25 to 0.25
- qkv_adapter_in: bfloat16 [2048, 384], P(('grp', 'seq', 'shard')), may hold values from -0.125 to 0.125
- q_adapter_out: bfloat16 [128, 2048], P(('grp', 'seq', 'shard')), may hold values from -0.75 to 0.75
- kv_adapter_out: bfloat16 [128, 1024], P(('grp', 'seq', 'shard')), may hold values from -0.75 to 0.75
- out_adapter_in: bfloat16 [2048, 128], P(('grp', 'seq', 'shard')), may hold values from -0.125 to 0.125
- out_adapter_out: bfloat16 [128, 2048], P(('grp', 'seq', 'shard')), may hold values from -0.75 to 0.75
- gate_up_adapter_in: bfloat16 [2048, 256], P(('grp', 'seq', 'shard')), may hold values from -0.125 to 0.125
- gate_up_adapter_out: bfloat16 [128, 16384], P(('grp', 'seq', 'shard')), may hold values from -0.75 to 0.75
- down_adapter_in: bfloat16 [8192, 128], P(('grp', 'seq', 'shard')), may hold values from -0.0625 to 0.0625
- down_adapter_out: bfloat16 [128, 2048], P(('grp', 'seq', 'shard')), may hold values from -0.75 to 0.75
- cotangent: bfloat16 [8, 2048, 2048], P('shard', ('grp', 'seq')), may hold values from -6 to 6
Outputs:
- output: bfloat16 [8, 2048, 2048], P('shard', ('grp', 'seq'))
- input_grad: bfloat16 [8, 2048, 2048], P('shard', ('grp', 'seq'))
- grad_qkv_adapter_in: float32 [2048, 384], P(('grp', 'seq', 'shard'))
- grad_q_adapter_out: float32 [128, 2048], P(('grp', 'seq', 'shard'))
- grad_kv_adapter_out: float32 [128, 1024], P(('grp', 'seq', 'shard'))
- grad_out_adapter_in: float32 [2048, 128], P(('grp', 'seq', 'shard'))
- grad_out_adapter_out: float32 [128, 2048], P(('grp', 'seq', 'shard'))
- grad_gate_up_adapter_in: float32 [2048, 256], P(('grp', 'seq', 'shard'))
- grad_gate_up_adapter_out: float32 [128, 16384], P(('grp', 'seq', 'shard'))
- grad_down_adapter_in: float32 [8192, 128], P(('grp', 'seq', 'shard'))
- grad_down_adapter_out: float32 [128, 2048], P(('grp', 'seq', 'shard'))
All inputs are finite; a program needn't handle non-finite values.
Results may differ from a plain program's by a relative error of at most 0.022.
Values may be sent and summed in bfloat16 or wider, within the bound.
No kernel may reach another device: no remote copies, remote signals or barrier semaphores. Data moves between devices by JAX's collectives and lax.ppermute only.
A program may use at most 384 MiB of HBM per device.

v0:
```python
import jax
import jax.numpy as jnp
from jax import lax
from jax.sharding import PartitionSpec as P

HEADS = 32
KVH = 8
HDIM = 64
FEEDFWD_UNITS = 8192
NAD = 8
RANK = 16
PROMPT = 1024
CONTS = 4
CLEN = 256
GTOK = 2048


EPSILON = 1e-05
ATTN_SCALE = 1.0 / 64.0
SKIP_PATH_SCALE = 0.22
ADAPTER_SCALE = 2.0
ROPE_BASE = 10000000.0
NEG_FILL = -1e30


def side_by_side(arrays, axis, dim, along):
    widths = [a.shape[along] for a in arrays]
    both = jnp.concatenate(arrays, axis=along)
    result = lax.all_gather(both, axis, axis=dim, tiled=True)
    return tuple(jnp.split(result, [sum(widths[:k]) for k in range(1, len(widths))], axis=along))


def in_blocks(shard, dim, length):
    before, after = (shard.shape[:dim], shard.shape[dim + 1 :])
    return jnp.moveaxis(shard.reshape(*before, length, -1, *after), dim, 0)


def one_scatter(arrays, axis, dims):
    length = lax.axis_size(axis)
    parts = [in_blocks(a, dim, length) for a, dim in zip(arrays, dims)]
    lines = jnp.concatenate([b.reshape(length, -1) for b in parts], axis=1)
    rows = max(16, -(-lines.shape[1] // 1024) * 8)
    lines = jnp.pad(lines, ((0, 0), (0, rows * 128 - lines.shape[1]))).reshape(-1, 128)
    ravelled, at, done = (lax.psum_scatter(lines, axis, tiled=True).reshape(-1), 0, [])
    for b in parts:
        part = b[0]
        done.append(ravelled[at : at + part.size].reshape(part.shape))
        at += part.size
    return tuple(done)


def matrix_product(left, right):
    return jnp.dot(left, right, preferred_element_type=jnp.float32)


def product_with_transpose(left, right):
    return lax.dot_general(
        left, right, (((1,), (1,)), ((), ())), preferred_element_type=jnp.float32
    )


def transpose_product(left, right):
    return lax.dot_general(
        left, right, (((0,), (0,)), ((), ())), preferred_element_type=jnp.float32
    )


def token_table(token_index):
    offset_after = jnp.maximum(token_index - PROMPT, 0)
    segment_ids = jnp.where(token_index < PROMPT, 0, 1 + offset_after // CLEN)
    positions = jnp.where(token_index < PROMPT, token_index, PROMPT + offset_after % CLEN)
    return (segment_ids, positions)


def rope_tables(positions):
    half_dim = HDIM // 2
    frequency = ROPE_BASE ** (-(jnp.arange(half_dim, dtype=jnp.float32) * 2.0) / HDIM)
    angles = positions.astype(jnp.float32)[:, None] * frequency[None, :]
    return (jnp.cos(angles), jnp.sin(angles))


def rotate(value_rows, cosine, sine_rows):
    half_dim = HDIM // 2
    first_half = value_rows[..., :half_dim]
    second_half = value_rows[..., half_dim:]
    cos_part = cosine[:, None, :]
    sin_part = sine_rows[:, None, :]
    return jnp.concatenate(
        [
            first_half * cos_part - second_half * sin_part,
            second_half * cos_part + first_half * sin_part,
        ],
        axis=-1,
    )


def rms_factor(value_rows):
    return lax.rsqrt(jnp.mean(value_rows * value_rows, axis=1, keepdims=True) + EPSILON)


def rms_back(value_rows, factor, gain_row, upstream):
    weighted = gain_row * upstream
    return factor * weighted - value_rows * factor**3 * jnp.mean(
        value_rows * weighted, axis=1, keepdims=True
    )


def head_forward(allowed):

    def compute(packed):
        query_head, key_head, value_head = packed
        scores = (
            jnp.einsum("qrd,kd->rqk", query_head, key_head, preferred_element_type=jnp.float32)
            * ATTN_SCALE
        )
        scores = jnp.where(allowed[None], scores, NEG_FILL)
        row_max = jnp.max(scores, axis=2, keepdims=True)
        exponent = jnp.exp(scores - row_max)
        row_total = jnp.sum(exponent, axis=2, keepdims=True)
        probs_low = (exponent / row_total).astype(jnp.bfloat16)
        attention_output = jnp.einsum(
            "rqk,kd->qrd", probs_low, value_head, preferred_element_type=jnp.float32
        )
        return (attention_output, (row_max + jnp.log(row_total))[..., 0])

    return compute


def head_backward(allowed):

    def compute(packed):
        query_head, key_head, value_head, d_head, log_total = packed
        scores = (
            jnp.einsum("qrd,kd->rqk", query_head, key_head, preferred_element_type=jnp.float32)
            * ATTN_SCALE
        )
        scores = jnp.where(allowed[None], scores, NEG_FILL)
        probs = jnp.exp(scores - log_total[..., None])
        probs_low = probs.astype(jnp.bfloat16)
        d_probs = jnp.einsum("qrd,kd->rqk", d_head, value_head, preferred_element_type=jnp.float32)
        row_inner = jnp.sum(probs * d_probs, axis=2, keepdims=True)
        d_scores = (probs * (d_probs - row_inner)).astype(jnp.bfloat16)
        d_query = (
            jnp.einsum("rqk,kd->qrd", d_scores, key_head, preferred_element_type=jnp.float32)
            * ATTN_SCALE
        )
        d_key = (
            jnp.einsum("rqk,qrd->kd", d_scores, query_head, preferred_element_type=jnp.float32)
            * ATTN_SCALE
        )
        d_value = jnp.einsum("rqk,qrd->kd", probs_low, d_head, preferred_element_type=jnp.float32)
        return (d_query, d_key, d_value)

    return compute


def local(
    tokens,
    adapter_ids,
    norm_gain_attn,
    norm_gain_mlp,
    qkv_weight,
    output_projection_weight,
    gate_up_weight,
    down_projection_weight,
    qkv_adapter_in,
    q_adapter_out,
    kv_adapter_out,
    out_adapter_in,
    out_adapter_out,
    gate_up_adapter_in,
    gate_up_adapter_out,
    down_adapter_in,
    down_adapter_out,
    cotangent,
):
    groups_here, block_len, model_width = tokens.shape
    row_count = groups_here * block_len
    key_value_width = KVH * HDIM
    rank_columns = NAD * RANK
    rep_heads = HEADS // KVH
    gathered_small = (
        lax.all_gather(norm_gain_attn, ("grp", "seq", "shard"), axis=0, tiled=True),
        lax.all_gather(norm_gain_mlp, ("grp", "seq", "shard"), axis=0, tiled=True),
        *side_by_side(
            (q_adapter_out, kv_adapter_out, out_adapter_out, gate_up_adapter_out, down_adapter_out),
            ("grp", "seq", "shard"),
            0,
            1,
        ),
    )
    (
        gain_attn,
        gain_mlp,
        query_raise,
        key_value_raise,
        output_raise,
        gate_up_raise,
        down_adapter_raise,
    ) = gathered_small
    dense_set = side_by_side(
        (
            qkv_weight,
            qkv_adapter_in,
            output_projection_weight,
            out_adapter_in,
            gate_up_weight,
            gate_up_adapter_in,
        ),
        ("grp", "seq", "shard"),
        0,
        1,
    )
    down_set = side_by_side(
        (down_projection_weight, down_adapter_in), ("grp", "seq", "shard"), 0, 1
    )
    block_index = lax.axis_index(("grp", "seq"))
    local_index = block_index * block_len + jnp.arange(block_len, dtype=jnp.int32)
    segment_ids, positions = token_table(local_index)
    key_index = jnp.arange(GTOK, dtype=jnp.int32)
    key_segments, key_positions = token_table(key_index)
    allowed = (key_index[None, :] <= local_index[:, None]) & (
        (key_segments[None, :] == 0) | (key_segments[None, :] == segment_ids[:, None])
    )
    cos_block, sin_block = rope_tables(positions)
    cosine = jnp.tile(cos_block, (groups_here, 1))
    sine_rows = jnp.tile(sin_block, (groups_here, 1))
    chosen = jnp.sum(
        jnp.where(
            segment_ids[None, :, None] == jnp.arange(CONTS + 1, dtype=jnp.int32)[None, None, :],
            adapter_ids[:, None, :],
            0,
        ),
        axis=2,
    ).reshape(row_count)
    select_adapter = (
        jnp.arange(rank_columns, dtype=jnp.int32)[None, :] // RANK == chosen[:, None]
    ).astype(jnp.bfloat16)
    layer_input_rows = tokens.reshape(row_count, model_width).astype(jnp.float32)
    first_factor = rms_factor(layer_input_rows)
    normed_attn = (layer_input_rows * first_factor * gain_attn).astype(jnp.bfloat16)
    combined_query_key_value = matrix_product(normed_attn, dense_set[0])
    joint_small = matrix_product(normed_attn, dense_set[1])
    query_key_value_rank_factor = joint_small.astype(jnp.bfloat16) * jnp.tile(
        select_adapter, (1, 3)
    )
    query_before_rotation = combined_query_key_value[
        :, :model_width
    ] + ADAPTER_SCALE * matrix_product(query_key_value_rank_factor[:, :rank_columns], query_raise)
    key_before_rotation = combined_query_key_value[
        :, model_width : model_width + key_value_width
    ] + ADAPTER_SCALE * matrix_product(
        query_key_value_rank_factor[:, rank_columns : 2 * rank_columns],
        key_value_raise[:, :key_value_width],
    )
    value_rows = (
        combined_query_key_value[:, model_width + key_value_width :]
        + ADAPTER_SCALE
        * matrix_product(
            query_key_value_rank_factor[:, 2 * rank_columns :], key_value_raise[:, key_value_width:]
        )
    ).astype(jnp.bfloat16)
    queries = rotate(
        query_before_rotation.reshape(row_count, HEADS, HDIM), cosine, sine_rows
    ).astype(jnp.bfloat16)
    keys_local = rotate(
        key_before_rotation.reshape(row_count, KVH, HDIM), cosine, sine_rows
    ).astype(jnp.bfloat16)
    local_kv = jnp.concatenate(
        [
            keys_local.reshape(groups_here, block_len, key_value_width),
            value_rows.reshape(groups_here, block_len, key_value_width),
        ],
        axis=2,
    )
    group_kv = lax.all_gather(local_kv, ("grp", "seq"), axis=1, tiled=True)
    query_groups = queries.reshape(groups_here, block_len, KVH, rep_heads, HDIM)
    group_number = 0
    key_heads = (
        group_kv[group_number, :, :key_value_width].reshape(GTOK, KVH, HDIM).transpose(1, 0, 2)
    )
    value_heads = (
        group_kv[group_number, :, key_value_width:].reshape(GTOK, KVH, HDIM).transpose(1, 0, 2)
    )
    query_heads = query_groups[group_number].transpose(1, 0, 2, 3)
    attended_heads, log_total = lax.map(
        head_forward(allowed), (query_heads, key_heads, value_heads)
    )
    attended_list = attended_heads.transpose(1, 0, 2, 3).reshape(block_len, model_width)
    log_totals = [log_total]
    head_keys = [key_heads]
    head_values = [value_heads]
    attention_output = attended_list.astype(jnp.bfloat16)
    attention_projection = matrix_product(attention_output, dense_set[2])
    proj_small = matrix_product(attention_output, dense_set[3])
    output_rank_factor = proj_small.astype(jnp.bfloat16) * select_adapter
    hidden_state = layer_input_rows + SKIP_PATH_SCALE * (
        attention_projection + ADAPTER_SCALE * matrix_product(output_rank_factor, output_raise)
    )
    second_factor = rms_factor(hidden_state)
    normed_mlp = (hidden_state * second_factor * gain_mlp).astype(jnp.bfloat16)
    combined_perceptron = matrix_product(normed_mlp, dense_set[4])
    joint_gu_small = matrix_product(normed_mlp, dense_set[5])
    gate_up_rank_factor = joint_gu_small.astype(jnp.bfloat16) * jnp.tile(select_adapter, (1, 2))
    gate_activation_value = combined_perceptron[:, :FEEDFWD_UNITS] + ADAPTER_SCALE * matrix_product(
        gate_up_rank_factor[:, :rank_columns], gate_up_raise[:, :FEEDFWD_UNITS]
    )
    up_projection_value = combined_perceptron[:, FEEDFWD_UNITS:] + ADAPTER_SCALE * matrix_product(
        gate_up_rank_factor[:, rank_columns:], gate_up_raise[:, FEEDFWD_UNITS:]
    )
    sigmoid_gate = jax.nn.sigmoid(gate_activation_value)
    mlp_activation = (gate_activation_value * sigmoid_gate * up_projection_value).astype(
        jnp.bfloat16
    )
    down_projection = matrix_product(mlp_activation, down_set[0])
    down_small = matrix_product(mlp_activation, down_set[1])
    down_rank_factor = down_small.astype(jnp.bfloat16) * select_adapter
    output = (
        hidden_state
        + SKIP_PATH_SCALE
        * (down_projection + ADAPTER_SCALE * matrix_product(down_rank_factor, down_adapter_raise))
    ).astype(jnp.bfloat16)
    upstream = cotangent.reshape(row_count, model_width).astype(jnp.float32)
    grad_perceptron = (SKIP_PATH_SCALE * upstream).astype(jnp.bfloat16)
    grad_down_adapter_rank = (
        ADAPTER_SCALE * product_with_transpose(grad_perceptron, down_adapter_raise) * select_adapter
    ).astype(jnp.bfloat16)
    d_activation = product_with_transpose(grad_perceptron, down_set[0]) + product_with_transpose(
        grad_down_adapter_rank, down_set[1]
    )
    d_gate = (
        d_activation
        * up_projection_value
        * sigmoid_gate
        * (1.0 + gate_activation_value * (1.0 - sigmoid_gate))
    ).astype(jnp.bfloat16)
    d_up = (d_activation * gate_activation_value * sigmoid_gate).astype(jnp.bfloat16)
    d_small_gu = (
        ADAPTER_SCALE
        * jnp.concatenate(
            [
                product_with_transpose(d_gate, gate_up_raise[:, :FEEDFWD_UNITS]),
                product_with_transpose(d_up, gate_up_raise[:, FEEDFWD_UNITS:]),
            ],
            axis=1,
        )
        * jnp.tile(select_adapter, (1, 2))
    ).astype(jnp.bfloat16)
    d_gate_up = jnp.concatenate([d_gate, d_up], axis=1)
    d_normed_mlp = product_with_transpose(d_gate_up, dense_set[4]) + product_with_transpose(
        d_small_gu, dense_set[5]
    )
    d_hidden = upstream + rms_back(hidden_state, second_factor, gain_mlp, d_normed_mlp)
    grad_attention = (SKIP_PATH_SCALE * d_hidden).astype(jnp.bfloat16)
    grad_output_adapter_rank = (
        ADAPTER_SCALE * product_with_transpose(grad_attention, output_raise) * select_adapter
    ).astype(jnp.bfloat16)
    d_attended = product_with_transpose(grad_attention, dense_set[2]) + product_with_transpose(
        grad_output_adapter_rank, dense_set[3]
    )
    d_attended = d_attended.astype(jnp.bfloat16).reshape(
        groups_here, block_len, KVH, rep_heads, HDIM
    )
    group_number = 0
    query_heads = query_groups[group_number].transpose(1, 0, 2, 3)
    d_heads = d_attended[group_number].transpose(1, 0, 2, 3)
    d_query, d_key, d_value = lax.map(
        head_backward(allowed),
        (
            query_heads,
            head_keys[group_number],
            head_values[group_number],
            d_heads,
            log_totals[group_number],
        ),
    )
    d_query_list = d_query.transpose(1, 0, 2, 3).reshape(block_len, HEADS, HDIM)
    d_kv_list = [
        jnp.concatenate(
            [
                d_key.transpose(1, 0, 2).reshape(GTOK, key_value_width),
                d_value.transpose(1, 0, 2).reshape(GTOK, key_value_width),
            ],
            axis=1,
        )
    ]
    d_kv_local = lax.psum_scatter(
        jnp.stack(d_kv_list, axis=0).astype(jnp.bfloat16),
        ("grp", "seq"),
        scatter_dimension=1,
        tiled=True,
    ).astype(jnp.float32)
    d_kv_local = d_kv_local.reshape(row_count, 2 * key_value_width)
    grad_query_before_rotation = (
        rotate(d_query_list, cosine, -sine_rows)
        .reshape(row_count, model_width)
        .astype(jnp.bfloat16)
    )
    d_k_pre = (
        rotate(d_kv_local[:, :key_value_width].reshape(row_count, KVH, HDIM), cosine, -sine_rows)
        .reshape(row_count, key_value_width)
        .astype(jnp.bfloat16)
    )
    d_v = d_kv_local[:, key_value_width:].astype(jnp.bfloat16)
    d_small_qkv = (
        ADAPTER_SCALE
        * jnp.concatenate(
            [
                product_with_transpose(grad_query_before_rotation, query_raise),
                product_with_transpose(d_k_pre, key_value_raise[:, :key_value_width]),
                product_with_transpose(d_v, key_value_raise[:, key_value_width:]),
            ],
            axis=1,
        )
        * jnp.tile(select_adapter, (1, 3))
    ).astype(jnp.bfloat16)
    d_joint = jnp.concatenate([grad_query_before_rotation, d_k_pre, d_v], axis=1)
    d_normed_attn = product_with_transpose(d_joint, dense_set[0]) + product_with_transpose(
        d_small_qkv, dense_set[1]
    )
    input_grad = (
        d_hidden + rms_back(layer_input_rows, first_factor, gain_attn, d_normed_attn)
    ).astype(jnp.bfloat16)
    gradient_down_result = ADAPTER_SCALE * transpose_product(down_rank_factor, grad_perceptron)
    grad_down_in = transpose_product(mlp_activation, grad_down_adapter_rank)
    gradient_gate_up_result = ADAPTER_SCALE * jnp.concatenate(
        [
            transpose_product(gate_up_rank_factor[:, :rank_columns], d_gate),
            transpose_product(gate_up_rank_factor[:, rank_columns:], d_up),
        ],
        axis=1,
    )
    grad_gu_in = transpose_product(normed_mlp, d_small_gu)
    gradient_output_result = ADAPTER_SCALE * transpose_product(output_rank_factor, grad_attention)
    grad_o_in = transpose_product(attention_output, grad_output_adapter_rank)
    gradient_query_result = ADAPTER_SCALE * transpose_product(
        query_key_value_rank_factor[:, :rank_columns], grad_query_before_rotation
    )
    gradient_key_value_result = ADAPTER_SCALE * jnp.concatenate(
        [
            transpose_product(
                query_key_value_rank_factor[:, rank_columns : 2 * rank_columns], d_k_pre
            ),
            transpose_product(query_key_value_rank_factor[:, 2 * rank_columns :], d_v),
        ],
        axis=1,
    )
    grad_qkv_in = transpose_product(normed_attn, d_small_qkv)
    summed = one_scatter(
        (
            grad_qkv_in,
            gradient_query_result,
            gradient_key_value_result,
            grad_o_in,
            gradient_output_result,
            grad_gu_in,
            gradient_gate_up_result,
            grad_down_in,
            gradient_down_result,
        ),
        ("grp", "seq", "shard"),
        (0, 0, 0, 0, 0, 0, 0, 0, 0),
    )
    return (
        output.reshape(groups_here, block_len, model_width),
        input_grad.reshape(groups_here, block_len, model_width),
        summed[0],
        summed[1],
        summed[2],
        summed[3],
        summed[4],
        summed[5],
        summed[6],
        summed[7],
        summed[8],
    )


def solution(mesh):
    placed = (
        P("shard", ("grp", "seq"), None),
        P("shard", None),
        P(("grp", "seq", "shard")),
        P(("grp", "seq", "shard")),
        P(("grp", "seq", "shard"), None),
        P(("grp", "seq", "shard"), None),
        P(("grp", "seq", "shard"), None),
        P(("grp", "seq", "shard"), None),
        P(("grp", "seq", "shard"), None),
        P(("grp", "seq", "shard"), None),
        P(("grp", "seq", "shard"), None),
        P(("grp", "seq", "shard"), None),
        P(("grp", "seq", "shard"), None),
        P(("grp", "seq", "shard"), None),
        P(("grp", "seq", "shard"), None),
        P(("grp", "seq", "shard"), None),
        P(("grp", "seq", "shard"), None),
        P("shard", ("grp", "seq"), None),
    )
    return jax.shard_map(
        local,
        mesh=mesh,
        in_specs=placed,
        out_specs=(
            P("shard", ("grp", "seq"), None),
            P("shard", ("grp", "seq"), None),
            P(("grp", "seq", "shard"), None),
            P(("grp", "seq", "shard"), None),
            P(("grp", "seq", "shard"), None),
            P(("grp", "seq", "shard"), None),
            P(("grp", "seq", "shard"), None),
            P(("grp", "seq", "shard"), None),
            P(("grp", "seq", "shard"), None),
            P(("grp", "seq", "shard"), None),
            P(("grp", "seq", "shard"), None),
        ),
        check_vma=False,
    )
```

profile of v0, /device:TPU:1, one launch (start us, length us, event | category | flops | bytes accessed | tf_op | source)
XLA Modules:
  0.0 1708.8 jit_solution(17920923251206734323)
XLA Ops:
  21.1 68.9 %all-reduce.3 = (bf16[2048]{0:T(1024)(128)(2,1)S(1)}, bf16[2048]{0:T(1024)(128)(2,1)S(1)}) all-reduce(bf16[2048]{0:T(1024)(128)(2,1)S(1)} %dynamic-update-slice, bf16[2048]{0:T(1024)(128)(2,1)S(1)} %dynamic-update-slice.1), channel_id=1, replica_groups=mesh['grp'=2,'seq'=8,'shard'=8] {'grp','seq','shard'}, use_global_device_ids=true, to_apply=%add | all-reduce | flops 4096 | bytes 16384
  93.6 129.9 %all-gather.12.cloned.1.call-done = bf16[128,1,23552]{2,1,0:T(2,128)(2,1)} async-done(((bf16[1,1,23552]{2,1,0:T(2,128)(2,1)}), bf16[128,1,23552]{2,1,0:T(2,128)(2,1)}) %all-gather.12.cloned.1.call-update) | async-done | bytes 6029328 | tf_op jit(solution)/shard_map/all_gather | solution.py:29
  223.5 8.8 copy.112
  232.3 487.1 %all-gather.6.cloned.1.call-done = bf16[2048,22272]{1,0:T(8,128)(2,1)} async-done(((bf16[16,22272]{1,0:T(8,128)(2,1)}), bf16[2048,22272]{1,0:T(8,128)(2,1)}) %all-gather.6.cloned.1.call-update) | async-done | bytes 91226128 | tf_op jit(solution)/shard_map/all_gather | solution.py:29
  721.4 5.7 fusion.61
  733.7 227.7 %all-gather.10.cloned.1.call-done = bf16[8192,2176]{1,0:T(8,128)(2,1)} async-done(((bf16[64,2176]{1,0:T(8,128)(2,1)}), bf16[8192,2176]{1,0:T(8,128)(2,1)}) %all-gather.10.cloned.1.call-update) | async-done | bytes 35651600 | tf_op jit(solution)/shard_map/all_gather | solution.py:29
  961.5 16.2 fusion.55
  977.7 4.5 convolution_add_fusion
  984.1 51.1 %all-gather.8.cloned.1.call-done = bf16[1,2048,1024]{2,1,0:T(8,128)(2,1)} async-done(((bf16[1,128,1024]{2,1,0:T(8,128)(2,1)}), bf16[1,2048,1024]{2,1,0:T(8,128)(2,1)}) %all-gather.8.cloned.1.call-update) | async-done | bytes 4194320 | tf_op jit(solution)/shard_map/all_gather | solution.py:276
  1035.2 4.5 fusion.219
  1039.7 4.0 copy.86
  1043.6 4.0 copy.87
  1047.6 44.5 %while.30 = (s32[]{:T(128)}, bf16[8,128,4,64]{1,3,2,0:T(8,128)(2,1)S(1)}, f32[8,4,128]{2,1,0:T(4,128)S(1)}, bf16[8,2048,64]{1,2,0:T(8,128)(2,1)}, bf16[8,2048,64...) while((s32[]{:T(128)}, ...), condition=%wide.region_5.6_spmd.clone.clone, body=%wide.region_2.5_spmd.clone.sunk.clone | while | flops 277872128 | bytes 13857905 | solution.py:286
  1092.1 4.9 fusion.68
  1100.1 26.3 %fusion.53 = f32[128,16384]{1,0:T(8,128)} fusion(bf16[128,2048]{1,0:T(8,128)(2,1)S(1)} %multiply_convert_fusion.4, bf16[2048,22272]{1,0:T(8,128)(2,1)} %all-gather.6.cloned.1.call-done), kind=kOutput, calls=%fused_computation.64 | convolution fusion | flops 8589934592 | bytes 76021760 | tf_op jit(solution)/shard_map/dot_general | solution.py:53
  1128.1 3.7 fusion.63
  1132.1 6.7 multiply_convert_fusion.1
  1141.6 35.6 %fusion.51 = f32[128,2048]{1,0:T(8,128)S(1)} fusion(bf16[2048,22272]{1,0:T(8,128)(2,1)} %all-gather.6.cloned.1.call-done, bf16[128,8192]{1,0:T(8,128)(2,1)} %copy-done.9, bf16[128,8192]{1,0:T(8,128)(2,1)} %copy-done.7), kind=kOutput, calls=%fused_computation.62 | convolution fusion | flops 8598323200 | bytes 72351744 | tf_op jit(solution)/shard_map/dot_general | solution.py:57
  1180.8 6.4 fusion.66
  1190.6 88.3 %while.31 = (s32[]{:T(128)}, f32[8,128,4,64]{1,3,2,0:T(8,128)}, bf16[8,2048,64]{1,2,0:T(8,128)(2,1)}, bf16[8,2048,64]{1,2,0:T(8,128)(2,1)}, bf16[8,2048,64]{1,2,...) while((s32[]{:T(128)}, f32[8,128,4,64]{1,3,2,0:T(8,128)}, ...), condition=%wide.region_10.11_spmd.clone.clone, body=%wide.region_8.10_spmd.clone.sunk.clone | while | flops 681737728 | bytes 34236552 | solution.py:367
  1193.9 2.4 fusion.309
  1204.9 2.4 fusion.309
  1216.0 2.4 fusion.309
  1227.0 2.4 fusion.309
  1238.0 2.4 fusion.309
  1249.1 2.4 fusion.309
  1260.1 2.4 fusion.309
  1271.2 2.4 fusion.309
  1279.0 4.8 pad_maximum_fusion
  1283.8 20.5 %copy.99 = bf16[1,2048,1024]{2,0,1:T(2,128)(2,1)} copy(bf16[1,2048,1024]{1,2,0:T(8,128)(2,1)} %pad_maximum_fusion) | data formatting | bytes 8388608
  1304.4 7.1 copy.113
  1314.8 2.8 fusion.215
  1317.7 3.0 reshape_reshape.14
  1320.6 4.3 fusion.222
  1325.0 5.1 reshape_reshape.15
  1332.4 3.5 fusion.123
  1336.0 2.7 fusion.178
  1338.7 2.8 fusion.181
  1341.5 56.5 %reduce-scatter.4.cloned.1.call-done = bf16[128,1024]{1,0:T(8,128)(2,1)} async-done(((bf16[2048,1024]{1,0:T(8,128)(2,1)}), bf16[128,1024]{1,0:T(8,128)(2,1)}) %reduce-scatter.4.cloned.1.call-update) | async-done | bytes 262160
  1407.9 2.3 fusion.145
  1410.2 4.3 reshape_reshape.12
  1414.5 4.0 constant_dynamic-update-slice_fusion.14
  1425.3 6.3 fusion.65
  1435.2 21.5 %reshape.545 = f32[44032,128]{1,0:T(8,128)} reshape(f32[128,44032]{1,0:T(8,128)} %fusion.73) | data formatting | bytes 45088768 | tf_op jit(solution)/shard_map/reshape | solution.py:43
  1456.7 14.5 fusion.57
  1471.2 2.5 fusion.87
  1473.7 8.4 fusion.59
  1485.7 207.5 %all-reduce.6.cloned.1.call-done = f32[44032,128]{1,0:T(8,128)} async-done(((f32[44032,128]{1,0:T(8,128)}), f32[44032,128]{1,0:T(8,128)}) %all-reduce.6.cloned.1.call-update) | async-done | bytes 22544400
  (301 shorter events, 193.3 us)
Async XLA Ops:
  7.2 216.3 %all-gather.12.cloned.1.call-start = ((), (), s32[]{:S(2)}) async-start(), calls=%async_computation.4 | async-start | bytes 12152832 | tf_op jit(solution)/shard_map/all_gather | solution.py:29
  11.6 707.8 %all-gather.6.cloned.1.call-start = ((), (), s32[]{:S(2)}) async-start(), calls=%async_computation.1 | async-start | bytes 91938816 | tf_op jit(solution)/shard_map/all_gather | solution.py:29
  17.5 944.0 %all-gather.10.cloned.1.call-start = ((), (), s32[]{:S(2)}) async-start(), calls=%async_computation.3 | async-start | bytes 35930112 | tf_op jit(solution)/shard_map/all_gather | solution.py:29
  19.3 1015.9 %all-gather.8.cloned.1.call-start = ((), (), s32[]{:S(2)}) async-start(), calls=%async_computation.2 | async-start | bytes 4456448 | tf_op jit(solution)/shard_map/all_gather | solution.py:276
  90.0 631.4 %copy-start.39 = (f32[2048]{0:T(1024)}, f32[2048]{0:T(1024)S(1)}, u32[]{:S(2)}) copy-start(f32[2048]{0:T(1024)S(1)} %convert_element_type.176) | copy-start | bytes 24580
  91.0 141.4 %copy-start.21 = (bf16[128,3,128]{0,2,1:T(8,128)(2,1)}, bf16[128,3,128]{0,2,1:T(8,128)(2,1)S(1)}, u32[]{:S(2)}) copy-start(bf16[128,3,128]{0,2,1:T(8,128)(2,1)S(1)} %tile.8) | copy-start | bytes 294916
  92.9 628.5 %copy-start.41 = (f32[128]{0:T(128)}, f32[128]{0:T(128)S(1)}, u32[]{:S(2)}) copy-start(f32[128]{0:T(128)S(1)} %get-tuple-element.241) | copy-start | bytes 1540
  93.6 890.2 %copy-start.28 = (f32[128,32]{0,1:T(8,128)}, f32[128,32]{0,1:T(8,128)S(1)}, u32[]{:S(2)}) copy-start(f32[128,32]{0,1:T(8,128)S(1)} %get-tuple-element.239) | copy-start | bytes 49156
  93.6 625.8 %copy-start.2 = (bf16[1,128,2048]{2,1,0:T(8,128)(2,1)S(1)}, bf16[1,128,2048]{2,1,0:T(8,128)(2,1)}, u32[]{:S(2)}) copy-start(bf16[1,128,2048]{2,1,0:T(8,128)(2,1)} %param.22) | copy-start | bytes 1572868
  721.4 260.9 %copy-start.30 = (bf16[128,384]{1,0:T(8,128)(2,1)}, bf16[128,384]{1,0:T(8,128)(2,1)S(1)}, u32[]{:S(2)}) copy-start(bf16[128,384]{1,0:T(8,128)(2,1)S(1)} %fusion.111) | copy-start | bytes 294916
  721.4 11.0 copy-start.12
  731.6 666.4 %reduce-scatter.4.cloned.1.call-start = ((), (), s32[]{:S(2)}) async-start(), calls=%async_computation.5 | async-start | bytes 4456448
  733.7 244.0 %copy-start.32 = (bf16[128,128]{1,0:T(8,128)(2,1)}, bf16[128,128]{1,0:T(8,128)(2,1)S(1)}, u32[]{:S(2)}) copy-start(bf16[128,128]{1,0:T(8,128)(2,1)S(1)} %fusion.117) | copy-start | bytes 98308
  977.7 4.5 copy-start.17
  1092.1 4.9 copy-start.11
  1098.4 28.1 %copy-start.34 = (bf16[128,128]{1,0:T(8,128)(2,1)}, bf16[128,128]{1,0:T(8,128)(2,1)S(1)}, u32[]{:S(2)}) copy-start(bf16[128,128]{1,0:T(8,128)(2,1)S(1)} %fusion.122) | copy-start | bytes 98308
  1100.1 26.4 %copy-start.15 = (bf16[128,2048]{1,0:T(8,128)(2,1)}, bf16[128,2048]{1,0:T(8,128)(2,1)S(1)}, u32[]{:S(2)}) copy-start(bf16[128,2048]{1,0:T(8,128)(2,1)S(1)} %multiply_convert_fusion.4) | copy-start | bytes 1572868
  1128.0 4.0 copy-start.5
  1128.1 12.1 slice-start
  1132.1 8.1 slice-start.1
  1138.8 2.1 copy-start.7
  1177.2 1.9 copy-start.13
  1311.5 381.7 %all-reduce.6.cloned.1.call-start = ((), (), s32[]{:S(2)}) async-start(), calls=%async_computation.6 | async-start | bytes 45088768
  1313.7 7.0 copy-start.33
  1325.0 5.1 copy-start.18
  1325.0 5.1 copy-start.29
  1325.0 5.1 copy-start.31
  1330.0 5.9 copy-start.10
  1336.0 2.7 copy-start.8
  1338.7 69.2 %copy-start.3 = (bf16[1,128,2048]{2,1,0:T(8,128)(2,1)S(1)}, bf16[1,128,2048]{2,1,0:T(8,128)(2,1)}, u32[]{:S(2)}) copy-start(bf16[1,128,2048]{2,1,0:T(8,128)(2,1)} %param.22) | copy-start | bytes 1572868
  1338.7 69.2 %copy-start.40 = (f32[2048]{0:T(1024)S(1)}, f32[2048]{0:T(1024)}, u32[]{:S(2)}) copy-start(f32[2048]{0:T(1024)} %copy-done.39) | copy-start | bytes 24580
  1338.7 69.2 %copy-start.42 = (f32[128]{0:T(128)S(1)}, f32[128]{0:T(128)}, u32[]{:S(2)}) copy-start(f32[128]{0:T(128)} %copy-done.41) | copy-start | bytes 1540
  1403.1 3.9 copy-start.24
  1406.0 1.9 copy-start.26
  1414.5 6.2 copy-start.19
  1414.5 7.0 copy-start.6
  1414.5 8.1 copy-start.35
  1418.4 5.4 copy-start.4
  1421.5 3.8 copy-start.1
  1425.3 6.3 copy-start
  1431.6 2.3 copy-start.14
  1431.6 2.3 copy-start.36
  1456.7 17.0 copy-start.37
  1473.7 8.5 copy-start.22
  1473.7 8.5 copy-start.23
  1473.7 8.5 copy-start.25
  1473.7 8.5 copy-start.27
  1482.2 2.2 copy-start.43
  (4 other events, 4.0 us)
Sparse Core Ops, SparseCore 0:
  11.8 211.7 all-gather.11
  225.2 494.1 all-gather.5
  721.7 239.6 all-gather.9
  963.5 71.6 all-gather.7
  1311.6 86.3 reduce-scatter.3
  1456.8 236.3 all-reduce.5
where the time goes:
time: 1720 us; the launch traced here: 1710 us
  waiting for transfers between devices  1160 us (67%)
  matrix products  288 us (17%)
  local copies, waits for them, and re-layouts  123 us (7%)
  blocking collectives  68.9 us (4%)
  other arithmetic  53 us (3%)
    all_gather x3, waiting for transfers between devices, side_by_side(): result = lax.all_gather(both, axis, axis=dim, tiled=True)  845 us
    unnamed x8, waiting for transfers between devices  264 us
    dot_general x15, matrix products, product_with_transpose(): lax.dot_general(left, right, (((1,), (1,)), ((), ())), preferred_element_...  85.7 us
    dot_general x15, matrix products, matrix_product(): return jnp.dot(left, right, preferred_element_type=jnp.float32)  77.8 us
    unnamed x1, blocking collectives  68.9 us
    unnamed x114, local copies, waits for them, and re-layouts  61.9 us
    all_gather x1, waiting for transfers between devices, local(): group_kv = lax.all_gather(local_kv, ('grp', 'seq'), axis=1, tiled=True)  51.1 us
  transfers between devices with their start and end apart: 6, of which 6 were waited for; matrix products, arithmetic and copies ran while one was open for 7% of the time, Pallas kernels for 0%

commit v1 on v0

v1 whole, which is shorter than its diff:
```python
import functools

import jax
import jax.numpy as jnp
from jax import lax
from jax.experimental import pallas as pl
from jax.experimental.pallas import tpu as pltpu
from jax.sharding import Mesh
from jax.sharding import PartitionSpec as P

HEADS = 32
KVH = 8
HDIM = 64
D = HEADS * HDIM
UNITS = 8192
PROMPT = 1024
CLEN = 256
GTOK = 2048
TOK = 128
RANK = 16

EPS = 1e-5
SKIP = 0.22
ROPE_BASE = 10000000.0
NEG = -1e30

F32 = jnp.float32
BF16 = jnp.bfloat16

AXES = ("zl", "zh", "y", "x", "c")
BLOCKS = ("zl", "zh", "y")
NATURAL = ("zh", "zl", "y")
PLANE = ("x", "c")

def mm(a, b):
    return jnp.dot(a, b, preferred_element_type=F32)


def mm_nt(a, b):
    return lax.dot_general(a, b, (((1,), (1,)), ((), ())), preferred_element_type=F32)


def mm_tn(a, b):
    return lax.dot_general(a, b, (((0,), (0,)), ((), ())), preferred_element_type=F32)


def swap_mid(v, axis=-1):
    axis = axis % v.ndim
    n = v.shape[axis] // 4
    q = [lax.slice_in_dim(v, k * n, (k + 1) * n, axis=axis) for k in (0, 2, 1, 3)]
    return jnp.concatenate(q, axis=axis)


def a2a(v, axes):
    return lax.all_to_all(v, axes, 0, 0, tiled=True)


def other_core(v):
    return lax.ppermute(v, "c", [(0, 1), (1, 0)])


def along_x(v, k):
    return lax.ppermute(v, "x", [(i, (i + k) % 4) for i in range(4)])


MIB = 1024 * 1024


def nbytes(arrays):
    return sum(a.size * a.dtype.itemsize for a in arrays)


def job(g, j):
    return (j // 2) * 4 + g * 2 + j % 2


def far_of(one, three):
    half = one.shape[0] // 2
    return jnp.concatenate([along_x(one[:half], 1), along_x(three[half:], 3)])


def from_x(v):
    one, three = along_x(v, 1), along_x(v, 3)
    return one, three, far_of(one, three)


def call(kernel, outs, args, scratch=(), specs=None, flops=0, vmem=24):
    if specs is None:
        specs = [None] * len(args)
    ins = [pl.BlockSpec(memory_space=pltpu.VMEM) if s is None else s for s in specs]
    return pl.pallas_call(
        kernel,
        grid=(1,),
        out_shape=outs,
        in_specs=ins,
        out_specs=[pl.BlockSpec(memory_space=pltpu.VMEM)] * len(outs),
        scratch_shapes=list(scratch),
        compiler_params=pltpu.CompilerParams(vmem_limit_bytes=vmem * MIB),
        cost_estimate=pl.CostEstimate(
            flops=flops, bytes_accessed=nbytes(args) + nbytes(outs), transcendentals=0
        ),
    )(*args)


def tiled_call(kernel, outs, args, specs, out_specs, scratch=(), flops=0, steps=4, vmem=32):
    size = nbytes(outs) + 2 * flops // 1024
    return pl.pallas_call(
        kernel,
        grid=(steps,),
        out_shape=outs,
        in_specs=specs,
        out_specs=out_specs,
        scratch_shapes=list(scratch),
        compiler_params=pltpu.CompilerParams(vmem_limit_bytes=vmem * MIB),
        cost_estimate=pl.CostEstimate(flops=flops, bytes_accessed=size, transcendentals=0),
    )(*args)


def shape(*dims, dtype=F32):
    return jax.ShapeDtypeStruct(dims, dtype)


def block(rows, cols, index):
    return pl.BlockSpec((rows, cols), lambda i: (0, index), pipeline_mode=pl.Buffered(1))


def whole_spec(rows, cols):
    return pl.BlockSpec((rows, cols), lambda i: (0, 0))


def after(v, *others):
    return lax.optimization_barrier((v, others))[0]


def segment_of(block_index):
    return jnp.where(block_index < 8, 0, 1 + (block_index - 8) // 2)


SMEM = pl.BlockSpec(memory_space=pltpu.SMEM)


def rope(t, cos, sin):
    lane = lax.broadcasted_iota(jnp.int32, t.shape, 1) % HDIM
    partner = jnp.where(lane < HDIM // 2, pltpu.roll(t, 96, 1), pltpu.roll(t, 32, 1))
    return t * cos + partner * sin


def assemble(x, pieces, whole):
    for piece, ahead in zip(pieces, (0, 3, 1, 2)):
        at = lax.rem(x + ahead, 4) * 32

        def place(i, _, piece=piece, at=at):
            to = pl.multiple_of(i * 128 + at, 32)
            whole[pl.ds(to, 32), :] = piece[pl.ds(pl.multiple_of(i * 32, 32), 32), :]
            return 0

        lax.fori_loop(0, 16, place, 0)


def gain_row(g, first):
    lane = lax.broadcasted_iota(jnp.int32, (128, 128), 1)
    row = lax.broadcasted_iota(jnp.int32, (128, 128), 0)
    tiled = mm(g.astype(BF16), (row == first + lane % 16).astype(BF16))
    tiled = jnp.where(lane // 16 == row % 8, tiled, 0.0).astype(BF16)
    to_row = lax.broadcasted_iota(jnp.int32, (16, 128), 1) // 8
    to_row = (to_row == lax.broadcasted_iota(jnp.int32, (16, 128), 0)).astype(BF16)
    rows = mm(to_row, tiled)
    return jnp.concatenate([rows[k : k + 1] for k in range(16)], axis=1)


def only_keys(kv):
    lane = lax.broadcasted_iota(jnp.int32, kv.shape, 1) % 128
    return jnp.where(lane < HDIM, kv, 0.0).astype(BF16), jnp.where(lane < HDIM, 0.0, kv).astype(BF16)


def qkv_kernel(
    place, x, e, pick, cq, sq, ckv, skv, send, normed, small, gain, gain_mlp, n, s_all, wide
):
    core = place[1]
    wide[...] = e[:, 768:896].astype(F32)
    q_out = jnp.concatenate([wide[pl.ds(t, 128, stride=16), :] for t in range(2)], axis=1)
    q_out = q_out.astype(BF16)
    k_out, v_out = only_keys(wide[pl.ds(2, 128, stride=16), :])
    gain[...] = gain_row(wide[pl.ds(3, 128, stride=16), :], 0)
    gain_mlp[...] = gain_row(wide[pl.ds(3, 128, stride=16), :], 16)
    for k in range(4):
        rows = slice(2 * k * TOK, (2 * k + 2) * TOK)
        v = x[rows, :].astype(F32)
        r = lax.rsqrt(jnp.mean(v * v, axis=1, keepdims=True) + EPS)
        n[rows, :] = (v * r * gain[...]).astype(BF16)
        s = mm(n[rows, :], e[:, 384:768]).astype(BF16)
        s = jnp.concatenate(
            [s[:TOK] * pick[2 * k : 2 * k + 1, :], s[TOK:] * pick[2 * k + 1 : 2 * k + 2, :]], axis=0
        )
        s_all[rows, :] = s
        q = mm(n[rows, :], e[:, :256]) + 2.0 * mm(s[:, :128], q_out)
        kv = mm(n[rows, :], e[:, 256:384]) + 2.0 * (
            mm(s[:, 128:256], k_out) + mm(s[:, 256:], v_out)
        )
        for o in range(2):
            here = slice(o * TOK, (o + 1) * TOK)
            t = rope(kv[here], ckv[...], skv[...]).astype(BF16)
            at = k * 4 + 2 * lax.rem(core + o, 2)
            for j in range(2):
                p = rope(q[here, j * 128 : (j + 1) * 128], cq[...], sq[...]).astype(BF16)
                send[at + j, :, 0:128] = p
                send[at + j, :, 128:256] = t
    own = pl.multiple_of((2 * place[0] + core) * TOK, TOK)
    other = pl.multiple_of((2 * place[0] + 1 - core) * TOK, TOK)
    normed[...] = n[pl.ds(own, TOK), :]
    small[:TOK, :] = s_all[pl.ds(own, TOK), :]
    small[TOK:, :] = s_all[pl.ds(other, TOK), :]


def heads_of(ref, rows, scale=None):
    t = ref[rows, :128]
    both = jnp.concatenate([t[:, :HDIM], t[:, HDIM:]], axis=0)
    return both if scale is None else both * jnp.asarray(scale, BF16)


def allowed_in_block():
    key = lax.broadcasted_iota(jnp.int32, (CLEN, 2 * CLEN), 0)
    query = lax.broadcasted_iota(jnp.int32, (CLEN, 2 * CLEN), 1) % CLEN
    return key <= query


def attend_kernel(z, out, stat):
    allowed = allowed_in_block()
    for i in range(GTOK // CLEN):
        rows = slice(i * CLEN, (i + 1) * CLEN)
        full = min(i, PROMPT // CLEN) * CLEN
        q = heads_of(z, rows, 1.0 / 64.0)
        sd = jnp.where(allowed, mm_nt(z[rows, 128:192], q), NEG)
        top = jnp.max(sd, axis=0, keepdims=True)
        if full:
            sf = mm_nt(z[0:full, 128:192], q)
            top = jnp.maximum(top, jnp.max(sf, axis=0, keepdims=True))
        pd = jnp.exp(sd - top)
        total = jnp.sum(pd, axis=0, keepdims=True)
        o = mm_tn(z[rows, 192:256], pd.astype(BF16))
        if full:
            pf = jnp.exp(sf - top)
            total = total + jnp.sum(pf, axis=0, keepdims=True)
            o = o + mm_tn(z[0:full, 192:256], pf.astype(BF16))
        o = o / total
        stat[i : i + 1, :] = top + jnp.log(total)
        both = jnp.concatenate([o[:, :CLEN], o[:, CLEN:]], axis=0)
        out[rows, :] = both.T.astype(BF16)


def attend_back_kernel(z, d_out, stat, dz, dk, dv):
    allowed = allowed_in_block()
    dk[...] = jnp.zeros_like(dk)
    dv[...] = jnp.zeros_like(dv)
    for i in range(GTOK // CLEN):
        rows = slice(i * CLEN, (i + 1) * CLEN)
        full = min(i, PROMPT // CLEN) * CLEN
        q = heads_of(z, rows, 1.0 / 64.0)
        do = heads_of(d_out, rows)
        lse = stat[i : i + 1, :]
        kd = z[rows, 128:192]
        pd = jnp.exp(jnp.where(allowed, mm_nt(kd, q), NEG) - lse)
        dpd = mm_nt(z[rows, 192:256], do)
        inner = jnp.sum(pd * dpd, axis=0, keepdims=True)
        if full:
            kf = z[0:full, 128:192]
            pf = jnp.exp(mm_nt(kf, q) - lse)
            dpf = mm_nt(z[0:full, 192:256], do)
            inner = inner + jnp.sum(pf * dpf, axis=0, keepdims=True)
        dsd = (pd * (dpd - inner)).astype(BF16)
        dq = mm_tn(kd, dsd)
        dk[rows, :] += mm(dsd, q)
        dv[rows, :] += mm(pd.astype(BF16), do)
        if full:
            dsf = (pf * (dpf - inner)).astype(BF16)
            dq = dq + mm_tn(kf, dsf)
            dk[0:full, :] += mm(dsf, q)
            dv[0:full, :] += mm(pf.astype(BF16), do)
        dq = dq * (1.0 / 64.0)
        both = jnp.concatenate([dq[:, :CLEN], dq[:, CLEN:]], axis=0)
        dz[rows, 0:128] = both.T.astype(BF16)
    dz[:, 128:256] = jnp.concatenate([dk[...], dv[...]], axis=1).astype(BF16)


def project_kernel(
    place, mine, theirs, e0, e1, e2, e3, pick, part, small, attended, whole, a_out, att, wide
):
    assemble(place[0], (e0, e1, e2, e3), whole)
    wide[...] = whole[:, 1152:1280].astype(F32)
    for t in range(16):
        a_out[:, t * 128 : (t + 1) * 128] = wide[pl.ds(t, 128, stride=16), :].astype(BF16)
    c = place[1]
    here = pl.multiple_of(c * 1024, 1024)
    there = pl.multiple_of((1 - c) * 1024, 1024)
    for g in range(2):
        rows = slice(g * TOK, (g + 1) * TOK)
        for j in range(8):
            cols = slice(j * 128, (j + 1) * 128)
            att[0, rows, cols] = mine[job(g, j)]
            att[1, rows, cols] = theirs[job(1 - g, j)]
    m, t = att[0], att[1]
    attended[:, pl.ds(here, 1024)] = m[:TOK]
    attended[:, pl.ds(there, 1024)] = t[:TOK]
    s = mm(m, whole[pl.ds(here, 1024), 1024:1152]) + mm(t, whole[pl.ds(there, 1024), 1024:1152])
    s = s.astype(BF16)
    s = jnp.concatenate([s[:TOK] * pick[0:1, :128], s[TOK:] * pick[1:2, :128]], axis=0)
    small[...] = s
    part[...] = (
        mm(m, whole[pl.ds(here, 1024), :1024])
        + mm(t, whole[pl.ds(there, 1024), :1024])
        + 2.0 * mm(s, a_out[:, pl.ds(here, 1024)])
    )


def hidden_kernel(place, x, mine, theirs, gain, hidden, normed):
    c = place[1]
    here = pl.multiple_of(c * 1024, 1024)
    there = pl.multiple_of((1 - c) * 1024, 1024)
    hidden[:, pl.ds(here, 1024)] = SKIP * mine[...]
    hidden[:, pl.ds(there, 1024)] = SKIP * theirs[...]
    h = x[...].astype(F32) + hidden[...]
    hidden[...] = h
    r = lax.rsqrt(jnp.mean(h * h, axis=1, keepdims=True) + EPS)
    normed[...] = (h * r * gain[...]).astype(BF16)


def unpack_kernel(outs, gu_out, down_out, wide):
    for k in range(3):
        wide[...] = outs[:, k * 128 : (k + 1) * 128].astype(F32)
        for t in range(16):
            at = (3 * t + k) * 128
            part = wide[pl.ds(t, 128, stride=16), :].astype(BF16)
            if at < 4096:
                gu_out[:, at : at + 128] = part
            else:
                down_out[:, at - 4096 : at - 3968] = part


def turn_kernel(cot, dm, turned):
    d = (SKIP * cot[...].astype(F32)).astype(BF16)
    dm[...] = d
    turned[...] = d.T


def d_act_kernel(dm, turned, a_out, a_in, pick, w, d_act, small):
    @pl.when(pl.program_id(0) == 0)
    def _():
        s = 2.0 * mm_nt(dm[...], a_out[...]) * pick[...].astype(F32)
        small[...] = s.astype(BF16)

    d_act[...] = mm(w[...], turned[...]).T + mm_nt(small[...], a_in[...])


def feed_kernel(
    n, d_act, pick, w_gate, w_up, o_gate, o_up, a_in, a_down, g_gate0, g_up0,
    act, back, g_gate, g_up, total, small,
):
    step = pl.program_id(0)

    @pl.when(step == 0)
    def _():
        s = mm(n[...], a_in[...]).astype(BF16)
        p = pick[...]
        small[...] = s * jnp.concatenate([p, p], axis=1)
        total[...] = jnp.zeros_like(total)

    x = n[...]
    gate = mm(x, w_gate[...]) + 2.0 * mm(small[:, :128], o_gate[...])
    up = mm(x, w_up[...]) + 2.0 * mm(small[:, 128:], o_up[...])
    sg = 1.0 / (1.0 + jnp.exp(-gate))
    gs = gate * sg
    act[...] = (gs * up).astype(BF16)
    da = d_act[...]
    dg = (da * up * (sg + gs * (1.0 - sg))).astype(BF16)
    du = (da * gs).astype(BF16)
    total[:D, :] += mm_nt(w_gate[...], dg) + mm_nt(w_up[...], du)
    total[D : D + 128, :] += mm_nt(o_gate[...], dg)
    total[D + 128 : D + 256, :] += mm_nt(o_up[...], du)
    total[D + 256 :, :] += mm_nt(a_down[...].T, act[...])
    for t in range(4):
        cols = slice(t * 128, (t + 1) * 128)
        g = mm_tn(small[:, :128], dg[:, cols]).reshape(16, 8, 128)
        g_gate[:, t] = g_gate0[:, t] + g
        g = mm_tn(small[:, 128:], du[:, cols]).reshape(16, 8, 128)
        g_up[:, t] = g_up0[:, t] + g

    @pl.when(step == pl.num_programs(0) - 1)
    def _():
        back[...] = total[...].T.astype(BF16)


def down_kernel(act_a, act_b, d_small, w, out, g_in, total):
    step = pl.program_id(0)

    @pl.when(step == 0)
    def _():
        total[...] = jnp.zeros_like(total)

    for k, act in enumerate((act_a, act_b)):
        rows = slice(k * 256, (k + 1) * 256)
        total[rows, :] += mm(act[...], w[...])
    g = mm_tn(act_a[...], d_small[:256]) + mm_tn(act_b[...], d_small[256:])
    g_in[...] = g.astype(BF16)

    @pl.when(step == pl.num_programs(0) - 1)
    def _():
        out[...] = total[...].astype(BF16)


def output_kernel(hidden, p0, p1, p2, p3, a_out, small, out):
    total = p0[...].astype(F32) + p1[...].astype(F32) + p2[...].astype(F32) + p3[...].astype(F32)
    out[...] = (hidden[...] + SKIP * (total + 2.0 * mm(small[...], a_out[...]))).astype(BF16)


def rms_back(v, gain, e):
    r = lax.rsqrt(jnp.mean(v * v, axis=1, keepdims=True) + EPS)
    we = gain * e
    return r * we - v * (r * r * r) * jnp.mean(v * we, axis=1, keepdims=True)


def d_hidden_kernel(
    hidden, cot, gain, p0, p1, p2, p3, a_in, pick, d_hidden, d_attn, small, small_down
):
    total = p0[...].astype(F32) + p1[...].astype(F32) + p2[...].astype(F32) + p3[...].astype(F32)
    s = (2.0 * total[:, D : D + 256] * pick[0:1, :256]).astype(BF16)
    small[...] = s
    small_down[...] = (total[:, D + 256 :] * pick[0:1, :128]).astype(BF16)
    e = total[:, :D] + mm_nt(s, a_in[...])
    d = cot[...].astype(F32) + rms_back(hidden[...], gain[...], e)
    d_hidden[...] = d
    d_attn[...] = (SKIP * d).astype(BF16)


def project_back_kernel(place, own, other, w, a_in, a_out, pick, mine, theirs, small, halves):
    c = place[1]
    here = pl.multiple_of(c * 1024, 1024)
    there = pl.multiple_of((1 - c) * 1024, 1024)
    full = jnp.concatenate([own[...], other[...]], axis=0)
    s = 2.0 * mm_nt(full, a_out[...])
    s = jnp.concatenate([s[:TOK] * pick[0:1, :128], s[TOK:] * pick[1:2, :128]], axis=0)
    s = s.astype(BF16)
    small[...] = s
    half = jnp.concatenate([own[:, pl.ds(here, 1024)], other[:, pl.ds(here, 1024)]], axis=0)
    halves[...] = half
    theirs[...] = mm_nt(half, w[pl.ds(there, 1024), :]).astype(BF16)
    mine[...] = mm_nt(half, w[pl.ds(here, 1024), :]) + mm_nt(s, a_in[pl.ds(here, 1024), :])


def pack_kernel(mine, theirs, send):
    for g in range(2):
        rows = slice(g * TOK, (g + 1) * TOK)
        swapped = slice((1 - g) * TOK, (2 - g) * TOK)
        for j in range(8):
            cols = slice(j * 128, (j + 1) * 128)
            send[job(g, j)] = (mine[rows, cols] + theirs[swapped, cols].astype(F32)).astype(BF16)


def early_grads_kernel(
    gu, g_down_in, d_small_gu, normed, small_down, cot, d_small_o, attended, small_o, halves, fold,
    out, lines,
):
    f = mm(d_small_gu[...], fold[:256, :]).astype(BF16)[:, :HDIM]
    g = mm_tn(f, normed[...])
    f = mm(d_small_o[:TOK], fold[256:384, :]).astype(BF16)[:, :HDIM]
    g = g + mm_tn(f, attended[...])
    dm = (SKIP * cot[...].astype(F32)).astype(BF16)
    g_down = 2.0 * mm_tn(small_down[...], dm)
    g_o = 2.0 * mm_tn(small_o[...], halves[...])
    for k in range(16):
        lines[k, 128:192, :] = g[:, k * 128 : (k + 1) * 128]
        rows = slice(k * 8, (k + 1) * 8)
        for t in range(16):
            lines[k, 192 + t * 8 : 200 + t * 8, :] = g_down[rows, t * 128 : (t + 1) * 128]
        for t in range(8):
            lines[k, 320 + t * 8 : 328 + t * 8, :] = g_o[rows, t * 128 : (t + 1) * 128]
        out[k, :128, :] = g_down_in[k * 128 : (k + 1) * 128, :]
        out[k, 128:384, :] = lines[k, 128:, :].astype(BF16)
        out[k, 384:, :] = gu[k]


def sums_kernel(slot, early, plane, g_down_in, first, total):
    first[...] = jnp.zeros_like(first)
    total[...] = early[0, 384:, :].astype(F32)
    for k in range(1, 16):
        total[...] += early[k, 384:, :].astype(F32)
    for r in range(8):
        plane[r, 0:32, :] = total[pl.ds(r, 32, stride=8), :]
    d = early[0, :128, :].astype(F32)
    o = early[0, 192:384, :].astype(F32)
    for k in range(16):
        at = pl.multiple_of(slot[k] * HDIM, HDIM)
        first[pl.ds(at, HDIM), :] += early[k, 128:192, :].astype(F32)
        if k:
            d = d + early[k, :128, :].astype(F32)
            o = o + early[k, 192:384, :].astype(F32)
    g_down_in[...] = d
    total[:192, :] = o
    turned = first[...].T
    for r in range(8):
        for k in range(4):
            part = turned[r * 16 : (r + 1) * 16, k * 128 : (k + 1) * 128]
            plane[r, 32 + k * 16 : 48 + k * 16, :] = part
        plane[r, 96:120, :] = total[pl.ds(r, 24, stride=8), :]


def unpack_qkv_kernel(outs, q_out, k_out, v_out, wide):
    wide[...] = outs[...].astype(F32)
    q = [wide[pl.ds(t, 128, stride=16), :] for t in range(8)]
    q_out[...] = jnp.concatenate(q, axis=1).astype(BF16)
    kv = [wide[pl.ds(8 + t, 128, stride=16), :] for t in range(4)]
    k_out[...], v_out[...] = only_keys(jnp.concatenate(kv, axis=1))


def qkv_back_kernel(
    parts, q_out, k_out, v_out, cq, sq, ckv, skv, d_joint, mine_small, their_small
):
    for g in range(2):
        rows = slice(g * TOK, (g + 1) * TOK)
        for j in range(8):
            t = parts[job(g, j), :, 0:128].astype(F32)
            d_joint[rows, j * 128 : (j + 1) * 128] = rope(t, cq[...], -sq[...]).astype(BF16)
        for j in range(4):
            t = parts[job(g, 2 * j), :, 128:256].astype(F32)
            t = t + parts[job(g, 2 * j + 1), :, 128:256].astype(F32)
            d_joint[rows, 1024 + j * 128 : 1024 + (j + 1) * 128] = rope(
                t, ckv[...], -skv[...]
            ).astype(BF16)
    dq, dkv = d_joint[:, :1024], d_joint[:, 1024:]
    small = 2.0 * jnp.concatenate(
        [mm_nt(dq, q_out[...]), mm_nt(dkv, k_out[...]), mm_nt(dkv, v_out[...])], axis=1
    )
    mine_small[...] = small[:TOK]
    their_small[...] = small[TOK:].astype(BF16)


def late_grads_kernel(
    mine_small, their_small, pick, normed, small_qkv, d_joint, fold, small, out, g
):
    s = ((mine_small[...] + their_small[...].astype(F32)) * pick[0:1, :]).astype(BF16)
    small[...] = s
    f = mm(s, fold[...]).astype(BF16)
    out[:, :128] = mm_tn(normed[...], f).astype(BF16)
    gq = 2.0 * mm_tn(small_qkv[:, :128], d_joint[:, :1024])
    gk = mm_tn(small_qkv[:, 128:256], d_joint[:, 1024:])
    gv = mm_tn(small_qkv[:, 256:], d_joint[:, 1024:])
    lane = lax.broadcasted_iota(jnp.int32, gk.shape, 1) % 128
    gkv = 2.0 * jnp.where(lane < HDIM, gk, gv)
    for t in range(8):
        g[pl.ds(t, 128, stride=16), :] = gq[:, t * 128 : (t + 1) * 128]
    for t in range(4):
        g[pl.ds(8 + t, 128, stride=16), :] = gkv[:, t * 128 : (t + 1) * 128]
        g[pl.ds(12 + t, 128, stride=16), :] = jnp.zeros((128, 128), F32)
    out[:, 128:] = g[...].astype(BF16)


def late_sums_kernel(slot, late, first, second):
    first[...] = jnp.zeros_like(first)
    second[...] = jnp.zeros_like(second)

    def add(k, _):
        for core in range(2):
            v = late[2 * k + core].astype(F32)
            at = slot[2 * k + core]
            first[at] += v[:, :128]
            second[core] += v[:, 128:]
        return 0

    lax.fori_loop(0, 64, add, 0)


def d_normed_kernel(d_joint, w, mine, theirs):
    dn = mm_nt(d_joint[...], w[...])
    mine[...] = dn[:TOK]
    theirs[...] = dn[TOK:].astype(BF16)


def last_kernel(x, d_hidden, gain, mine, theirs, small, a, grad):
    dn = mine[...] + theirs[...].astype(F32) + mm_nt(small[...], a[...])
    v = x[...].astype(F32)
    grad[...] = (d_hidden[...] + rms_back(v, gain[...], dn)).astype(BF16)


def local(
    tokens,
    adapter_ids,
    norm_gain_attn,
    norm_gain_mlp,
    qkv_weight,
    output_projection_weight,
    gate_up_weight,
    down_projection_weight,
    qkv_adapter_in,
    q_adapter_out,
    kv_adapter_out,
    out_adapter_in,
    out_adapter_out,
    gate_up_adapter_in,
    gate_up_adapter_out,
    down_adapter_in,
    down_adapter_out,
    cotangent,
):
    c = lax.axis_index("c")
    x = lax.axis_index("x")
    b = lax.axis_index(BLOCKS)
    place = jnp.stack([x, c]).astype(jnp.int32)

    x_own = swap_mid(tokens[0])
    cot_own = swap_mid(cotangent[0])
    x_plane = lax.all_gather(x_own, PLANE, axis=0, tiled=True)

    q_w = swap_mid(qkv_weight[:, :D])
    k_w = swap_mid(qkv_weight[:, D : D + 512]).reshape(16, 8, 1, HDIM)
    v_w = swap_mid(qkv_weight[:, D + 512 :]).reshape(16, 8, 1, HDIM)
    kv_w = jnp.concatenate([k_w, v_w], axis=2).reshape(16, 1024)
    a_in = swap_mid(qkv_adapter_in.reshape(16, 3, 128)).reshape(16, 384)
    qo = swap_mid(q_adapter_out)
    ko = swap_mid(kv_adapter_out[:, :512]).reshape(8, 1, HDIM)
    vo = swap_mid(kv_adapter_out[:, 512:]).reshape(8, 1, HDIM)
    kvo = jnp.concatenate([ko, vo], axis=1).reshape(1, 1024)
    ids = adapter_ids[0]
    extra = jnp.concatenate([norm_gain_attn, norm_gain_mlp, ids.astype(BF16), jnp.zeros(91, BF16)])
    outs = jnp.concatenate(
        [
            qo.reshape(8, 2, 128),
            kvo.reshape(8, 1, 128),
            jnp.broadcast_to(extra, (8, 1, 128)),
            jnp.zeros((8, 12, 128), BF16),
        ],
        axis=1,
    )
    payload = jnp.concatenate(
        [
            q_w.reshape(16, 8, 256).transpose(1, 0, 2),
            kv_w.reshape(16, 8, 128).transpose(1, 0, 2),
            jnp.broadcast_to(a_in, (8, 16, 384)),
            outs,
        ],
        axis=2,
    )
    heads = payload.reshape(2, 4, 16, 896).transpose(1, 0, 2, 3).reshape(8, 16, 896)
    heads = a2a(heads, PLANE)
    ids_all = heads[:, 3, 800:805].astype(F32)
    heads = jnp.broadcast_to(heads.reshape(1, 128, 896), (16, 128, 896))
    heads = a2a(heads, NATURAL).reshape(D, 896)

    o_w = swap_mid(output_projection_weight).reshape(16, 2, 1024)
    o_out = swap_mid(out_adapter_out).reshape(16, 128)
    payload = jnp.concatenate(
        [
            o_w.transpose(1, 0, 2),
            jnp.broadcast_to(swap_mid(out_adapter_in), (2, 16, 128)),
            jnp.broadcast_to(o_out, (2, 16, 128)),
        ],
        axis=2,
    )

    def chip_rows(v):
        keep = lax.dynamic_index_in_dim(v, c, 0, keepdims=False)
        take = other_core(lax.dynamic_index_in_dim(v, 1 - c, 0, keepdims=False))
        return jnp.where(c == 0, jnp.concatenate([keep, take]), jnp.concatenate([take, keep]))

    chip = chip_rows(payload)
    o_mine = lax.all_gather(after(chip, x_plane), NATURAL, axis=0, tiled=True)
    o_set = [o_mine, *from_x(o_mine)]

    gu = gate_up_weight.reshape(16, 2, 2, 2, 4, 4, 128).transpose(5, 0, 1, 3, 2, 4, 6)
    gu = gu.reshape(4, 16, 4096)
    guo = gate_up_adapter_out.reshape(2, 2, 2, 4, 4, 128).transpose(4, 0, 2, 1, 3, 5)
    guo = guo.reshape(4, 4096)
    outs = jnp.concatenate([guo, jnp.broadcast_to(swap_mid(down_adapter_out), (4, D))], axis=1)
    gu_in = swap_mid(gate_up_adapter_in.reshape(16, 2, 128)).reshape(16, 256)
    to_x = jnp.concatenate(
        [
            gu,
            jnp.broadcast_to(gu_in, (4, 16, 256)),
            outs.reshape(4, 16, 384),
        ],
        axis=2,
    )

    def for_chip(k):
        return lax.dynamic_index_in_dim(to_x, (x + k) % 4, 0, keepdims=False)

    by_chip = [for_chip(0)] + [along_x(for_chip(k), k) for k in (1, 2, 3)]
    by_chip = jnp.stack(by_chip)

    def of_pair(core):
        two = [
            lax.dynamic_index_in_dim(by_chip, (x - 2 * core - j) % 4, 0, keepdims=False)
            for j in range(2)
        ]
        return jnp.stack(two)

    keep = of_pair(c)
    take = other_core(of_pair(1 - c))
    rows = jnp.where(c == 0, jnp.stack([keep, take], 1), jnp.stack([take, keep], 1))
    plane = rows.reshape(64, 4736)
    down_w = swap_mid(down_projection_weight)
    down_in = swap_mid(down_adapter_in)
    plane = jnp.concatenate(
        [plane[:, :4096], down_w, plane[:, 4096:4352], down_in, plane[:, 4352:]], axis=1
    )

    mlp_set = lax.all_gather(after(plane, heads), NATURAL + ("c",), axis=0, tiled=True)

    segment = segment_of(b)
    start = jnp.where(b < 8, b * TOK, PROMPT + ((b - 8) % 2) * TOK)
    positions = start + jnp.arange(TOK, dtype=jnp.int32)
    frequency = ROPE_BASE ** (-(jnp.arange(HDIM // 2, dtype=F32) * 2.0) / HDIM)
    angles = positions.astype(F32)[:, None] * frequency[None, :]
    cos, sin = jnp.cos(angles), jnp.sin(angles)
    one, zero = jnp.ones((TOK, HDIM), F32), jnp.zeros((TOK, HDIM), F32)
    cq = jnp.concatenate([cos] * 4, axis=1)
    sq = jnp.concatenate([-sin, sin, -sin, sin], axis=1)
    ckv = jnp.concatenate([cos, cos, one], axis=1)
    skv = jnp.concatenate([-sin, sin, zero], axis=1)

    col = jnp.arange(128)
    col_adapter = ((col >> 5) & 1) * 4 + ((col >> 6) & 1) * 2 + ((col >> 4) & 1)
    here = (jnp.arange(5) == segment).astype(F32)

    def picks(adapters):
        a = jnp.sum(adapters.astype(F32) * here)
        return (col_adapter.astype(F32) == a).astype(BF16)

    def picks_at(ahead, core):
        row = 2 * ((x + ahead) % 4) + core
        return picks(lax.dynamic_index_in_dim(ids_all, row, 0, keepdims=False))

    pick = jnp.stack([jnp.tile(picks(ids_all[k]), 3) for k in range(8)])
    pick_all = jnp.concatenate([pick, jnp.zeros((8, 384), BF16)], axis=0)
    pick = [lax.dynamic_slice_in_dim(pick, 2 * x + core, 1) for core in (c, 1 - c)]
    pick = jnp.concatenate([*pick, jnp.zeros((14, 384), BF16)], axis=0)
    pick_f = pick.astype(F32)

    send, normed_attn, small_qkv, gain_attn, gain_mlp = call(
        qkv_kernel,
        [
            shape(16, TOK, 256, dtype=BF16),
            shape(TOK, D, dtype=BF16),
            shape(256, 384, dtype=BF16),
            shape(1, D),
            shape(1, D),
        ],
        [place, after(x_plane, plane), heads, pick_all, cq, sq, ckv, skv],
        scratch=[
            pltpu.VMEM((1024, D), BF16),
            pltpu.VMEM((1024, 384), BF16),
            pltpu.VMEM((D, 128), F32),
        ],
        specs=[SMEM] + [None] * 7,
        flops=2 * 1024 * D * 768,
        vmem=40,
    )
    z = a2a(a2a(send, "x"), BLOCKS).reshape(GTOK, 256)
    cot = [cot_own, *from_x(after(cot_own, o_set))]
    cot = jnp.concatenate([cot[1], cot[2], cot[0], cot[3]])

    t2 = jnp.concatenate(
        [
            q_w.reshape(16, 2, 1024).transpose(1, 0, 2),
            kv_w.reshape(16, 2, 512).transpose(1, 0, 2),
            jnp.concatenate(
                [qo.reshape(2, 8, 128), kvo.reshape(2, 4, 128), jnp.zeros((2, 4, 128), BF16)], axis=1
            ),
        ],
        axis=2,
    )
    t2 = chip_rows(t2)
    rel = jnp.stack([t2] + [along_x(t2, k) for k in (1, 2, 3)])
    rel = [lax.dynamic_index_in_dim(rel, (x - k) % 4, 0, keepdims=False) for k in range(4)]
    t2 = jnp.concatenate(rel)

    attended, stat = call(
        attend_kernel,
        [shape(GTOK, 128, dtype=BF16), shape(8, 512)],
        [after(z, o_set[:3])],
        flops=2 * 2 * 2 * 30 * CLEN * CLEN * HDIM * 4,
        vmem=20,
    )
    mine = a2a(after(attended, t2, o_set).reshape(16, TOK, 128), BLOCKS)
    theirs = other_core(mine)
    part, small_o, attended, o_whole, out_out = call(
        project_kernel,
        [
            shape(256, 1024),
            shape(256, 128, dtype=BF16),
            shape(TOK, D, dtype=BF16),
            shape(D, 1280, dtype=BF16),
            shape(128, D, dtype=BF16),
        ],
        [place, mine, after(theirs, cot), *o_set, pick],
        scratch=[pltpu.VMEM((2, 256, 1024), BF16), pltpu.VMEM((D, 128), F32)],
        specs=[SMEM] + [None] * 7,
        flops=2 * 256 * D * 1024,
        vmem=24,
    )
    w_spec = block(D, 1536, 0)
    o_spec = block(D, 1024, 0)
    oa_spec = block(D, 128, 8)

    device = jnp.arange(128)
    device_segment = segment_of(((device >> 5) & 1) * 8 + (device >> 6) * 4 + ((device >> 3) & 3))
    device_segment = (device_segment[:, None] == jnp.arange(5)).astype(F32)
    device_ids = jnp.broadcast_to(ids_all[None], (16, 8, 5)).reshape(128, 5)
    device_adapter = jnp.sum(device_ids * device_segment, axis=1)
    natural = device_adapter.astype(jnp.int32)
    device_slot = (natural >> 1 & 1) * 4 + (natural >> 2) * 2 + (natural & 1)
    source_slot = lax.dynamic_slice_in_dim(
        device_slot.reshape(16, 8).T.reshape(128), (2 * x + c) * 16, 16
    )
    lane = jnp.arange(384)
    fold_to = jnp.where(lane < 256, lane // 128, 2) * RANK + lane % RANK
    fold = (fold_to[:, None] == jnp.arange(128)[None, :]).astype(BF16)

    gu_out, down_out = call(
        unpack_kernel,
        [shape(128, 4096, dtype=BF16), shape(128, D, dtype=BF16)],
        [mlp_set[:, 6528:]],
        scratch=[pltpu.VMEM((D, 128), F32)],
        vmem=12,
    )

    hidden, normed_mlp = call(
        hidden_kernel,
        [shape(TOK, D), shape(TOK, D, dtype=BF16)],
        [place, x_own, part[:TOK], other_core(part[TOK:]), gain_mlp],
        specs=[SMEM] + [None] * 4,
        vmem=10,
    )

    pick4 = jnp.concatenate(
        [jnp.broadcast_to(picks_at(ahead, c), (TOK, 128)) for ahead in (3, 1, 0, 2)]
    )
    dm, turned = call(
        turn_kernel, [shape(512, D, dtype=BF16), shape(D, 512, dtype=BF16)], [cot]
    )
    n1, n3, n2 = from_x(normed_mlp)
    t2 = lax.all_gather(after(t2, mlp_set, n2), NATURAL, axis=0, tiled=True)
    dm = after(dm, n1, n2, n3)
    d_act, d_small_down = tiled_call(
        d_act_kernel,
        [shape(512, 2048), shape(512, 128, dtype=BF16)],
        [dm, turned, down_out, mlp_set, pick4, mlp_set],
        [
            whole_spec(512, D),
            whole_spec(D, 512),
            whole_spec(128, D),
            pl.BlockSpec((512, 128), lambda i: (i, 50)),
            whole_spec(512, 128),
            pl.BlockSpec((512, 2048), lambda i: (i, 2)),
        ],
        [pl.BlockSpec((512, 512), lambda i: (0, i)), whole_spec(512, 128)],
        flops=2 * 512 * 2048 * D,
        vmem=52,
    )

    def feed(part, n, g_gate, g_up):
        lines = pl.BlockSpec((16, 4, 8, 128), lambda i: (0, i, 0, 0))
        return tiled_call(
            feed_kernel,
            [
                shape(256, 2048, dtype=BF16),
                shape(256, D + 384, dtype=BF16),
                shape(16, 16, 8, 128),
                shape(16, 16, 8, 128),
            ],
            [n, d_act, pick4, mlp_set, mlp_set, gu_out, gu_out, mlp_set, mlp_set, g_gate, g_up],
            [
                whole_spec(256, D),
                pl.BlockSpec((256, 512), lambda i: (part, i)),
                pl.BlockSpec((256, 128), lambda i: (part, 0)),
                pl.BlockSpec((D, 512), lambda i: (0, i)),
                pl.BlockSpec((D, 512), lambda i: (0, i + 4)),
                pl.BlockSpec((128, 512), lambda i: (0, i)),
                pl.BlockSpec((128, 512), lambda i: (0, i + 4)),
                block(D, 256, 24),
                pl.BlockSpec((512, 128), lambda i: (i, 50)),
                lines,
                lines,
            ],
            [pl.BlockSpec((256, 512), lambda i: (0, i)), whole_spec(256, D + 384), lines, lines],
            [pltpu.VMEM((D + 384, 256), F32), pltpu.VMEM((256, 256), BF16)],
            flops=2 * 256 * 4096 * D * 2,
            vmem=52,
        )

    none = jnp.zeros((16, 16, 8, 128), F32)
    act_a, back_a, g_gate, g_up = feed(0, jnp.concatenate([n1, n3]), none, none)
    back = [along_x(back_a[:TOK], 3), along_x(back_a[TOK:], 1)]
    act_b, back_b, g_gate, g_up = feed(1, jnp.concatenate([normed_mlp, n2]), g_gate, g_up)
    back = [*back, back_b[:TOK], along_x(after(back_b[TOK:], back), 2)]

    gu_lines = 2.0 * jnp.concatenate([g_gate, g_up], axis=1).reshape(16, 256, 128)
    gu_lines = gu_lines.astype(BF16)
    d_hidden, d_attn, d_small_gu, small_down = call(
        d_hidden_kernel,
        [
            shape(TOK, D),
            shape(TOK, D, dtype=BF16),
            shape(TOK, 256, dtype=BF16),
            shape(TOK, 128, dtype=BF16),
        ],
        [hidden, cot_own, gain_mlp, *back, mlp_set, pick_f],
        specs=[None] * 7 + [block(D, 256, 24), None],
        vmem=52,
    )

    mine, theirs, d_small_o, halves = call(
        project_back_kernel,
        [
            shape(256, 1024),
            shape(256, 1024, dtype=BF16),
            shape(256, 128, dtype=BF16),
            shape(256, 1024, dtype=BF16),
        ],
        [place, d_attn, other_core(d_attn), o_whole, o_whole, out_out, pick_f],
        specs=[SMEM, None, None, o_spec, oa_spec, None, None],
        flops=2 * 256 * D * 1024,
        vmem=20,
    )
    (send,) = call(
        pack_kernel, [shape(16, TOK, 128, dtype=BF16)], [mine, other_core(theirs)], vmem=6
    )

    down, g_down_in = tiled_call(
        down_kernel,
        [shape(512, D, dtype=BF16), shape(2048, 128, dtype=BF16)],
        [after(act_a, send), act_b, d_small_down, mlp_set],
        [
            pl.BlockSpec((256, 512), lambda i: (0, i)),
            pl.BlockSpec((256, 512), lambda i: (0, i)),
            whole_spec(512, 128),
            pl.BlockSpec((512, 2048), lambda i: (i, 2)),
        ],
        [whole_spec(512, D), pl.BlockSpec((512, 128), lambda i: (i, 0))],
        [pltpu.VMEM((512, D), F32)],
        flops=2 * 512 * 2048 * D,
        vmem=52,
    )
    down = after(down, d_attn)
    down = [
        along_x(down[:TOK], 3),
        along_x(down[TOK : 2 * TOK], 1),
        down[2 * TOK : 3 * TOK],
        along_x(down[3 * TOK :], 2),
    ]
    d_out = a2a(send, BLOCKS).reshape(GTOK, 128)
    (early,) = call(
        early_grads_kernel,
        [shape(16, 640, 128, dtype=BF16)],
        [
            gu_lines,
            g_down_in,
            after(d_small_gu, send),
            normed_mlp,
            small_down,
            cot_own,
            d_small_o,
            attended,
            small_o,
            halves,
            fold,
        ],
        scratch=[pltpu.VMEM((16, 384, 128), F32)],
        vmem=28,
    )
    early = a2a(after(early, d_out), NATURAL)
    q_out, k_out, v_out = call(
        unpack_qkv_kernel,
        [shape(128, 1024, dtype=BF16), shape(128, 512, dtype=BF16), shape(128, 512, dtype=BF16)],
        [t2[:, 1536:]],
        scratch=[pltpu.VMEM((D, 128), F32)],
        vmem=8,
    )
    (dz,) = call(
        attend_back_kernel,
        [shape(GTOK, 256, dtype=BF16)],
        [after(z, q_out), d_out, stat],
        scratch=[pltpu.VMEM((GTOK, HDIM), F32), pltpu.VMEM((GTOK, HDIM), F32)],
        flops=5 * 2 * 2 * 30 * CLEN * CLEN * HDIM * 4,
        vmem=24,
    )
    parts = a2a(after(dz, down, early).reshape(16, TOK, 256), BLOCKS)
    (output,) = call(
        output_kernel,
        [shape(TOK, D, dtype=BF16)],
        [after(hidden, dz), *down, down_out, small_down],
        vmem=12,
    )
    output = swap_mid(output)
    plane, g_down_in = call(
        sums_kernel,
        [shape(8, 120, 128), shape(128, 128)],
        [after(source_slot, dz), early],
        scratch=[pltpu.VMEM((512, 128), F32), pltpu.VMEM((256, 128), F32)],
        specs=[SMEM, None],
        vmem=12,
    )
    plane = plane.reshape(4, 2, 120, 128)

    def to_chip(k):
        return lax.dynamic_index_in_dim(plane, (x + k) % 4, 0, keepdims=False)

    by_chip = jnp.stack([to_chip(0)] + [along_x(to_chip(k), k) for k in (1, 2, 3)])
    keep = lax.dynamic_index_in_dim(by_chip, c, 1, keepdims=False)
    take = other_core(lax.dynamic_index_in_dim(by_chip, 1 - c, 1, keepdims=False))

    parts = after(parts, keep, take)
    d_joint, mine_small, their_small = call(
        qkv_back_kernel,
        [shape(256, 1536, dtype=BF16), shape(TOK, 384), shape(TOK, 384, dtype=BF16)],
        [parts, q_out, k_out, v_out, cq, sq, ckv, skv],
        vmem=12,
    )
    d_small_qkv, late = call(
        late_grads_kernel,
        [shape(TOK, 384, dtype=BF16), shape(D, 256, dtype=BF16)],
        [mine_small, other_core(their_small), pick_f, normed_attn, small_qkv, d_joint, fold],
        scratch=[pltpu.VMEM((D, 128), F32)],
        vmem=14,
    )
    mine, theirs = call(
        d_normed_kernel,
        [shape(TOK, D), shape(TOK, D, dtype=BF16)],
        [after(d_joint, late), t2],
        specs=[None, w_spec],
        flops=2 * 256 * D * 1536,
        vmem=20,
    )
    late = a2a(late.reshape(128, 16, 256), NATURAL + PLANE)
    (input_grad,) = call(
        last_kernel,
        [shape(TOK, D, dtype=BF16)],
        [x_own, d_hidden, gain_attn, mine, other_core(theirs), d_small_qkv, heads],
        specs=[None] * 6 + [block(D, 384, 1)],
        vmem=14,
    )
    input_grad = swap_mid(input_grad)

    late_first, late_second = call(
        late_sums_kernel,
        [shape(8, 16, 128), shape(2, 16, 128)],
        [device_slot, late],
        specs=[SMEM, None],
        vmem=8,
    )
    both = keep + take
    gu = [
        lax.dynamic_index_in_dim(both[:, :32], (x - k) % 4, 0, keepdims=False) for k in range(4)
    ]
    gu = jnp.stack(gu).reshape(4, 2, 2, 2, 4, 128).transpose(1, 3, 2, 4, 0, 5)
    grad_gu_out = gu.reshape(1, 2 * UNITS)
    half = g_down_in.reshape(2, 64, 128)
    to_other = lax.dynamic_index_in_dim(half, 1 - c, 0, keepdims=False)
    grad_down_in = lax.dynamic_index_in_dim(half, c, 0, keepdims=False)
    grad_down_in = swap_mid(grad_down_in + other_core(to_other))
    total = jnp.sum(both[:, 32:112], axis=0)
    first = total[:64].reshape(4, 16, 2, 4, RANK).transpose(1, 3, 0, 2, 4).reshape(16, 4, 128)
    grad_gu_in = swap_mid(first[:, :2]).reshape(16, 256)
    grad_out_in = swap_mid(first[:, 2])
    grad_down_out = swap_mid(total[64:80].reshape(1, D))
    keep, take = jnp.sum(keep[:, 112:], axis=0), jnp.sum(take[:, 112:], axis=0)
    halves = jnp.where(c == 0, jnp.stack([keep, take]), jnp.stack([take, keep]))
    grad_out_out = swap_mid(halves.reshape(1, D))
    first = late_first[:, :, :48].reshape(8, 16, 3, RANK).transpose(1, 2, 0, 3)
    grad_qkv_in = swap_mid(first.reshape(16, 3, 128)).reshape(16, 384)
    grad_q_out = swap_mid(late_second[:, :8].reshape(1, D))
    kv = late_second[:, 8:12].reshape(2, 4, 2, HDIM).transpose(2, 0, 1, 3).reshape(2, 512)
    grad_kv_out = swap_mid(kv).reshape(1, 1024)

    return (
        output[None],
        input_grad[None],
        grad_qkv_in,
        grad_q_out,
        grad_kv_out,
        grad_out_in,
        grad_out_out,
        grad_gu_in,
        grad_gu_out,
        grad_down_in,
        grad_down_out,
    )


def solution(mesh):
    fine = Mesh(mesh.devices.reshape(2, 2, 4, 4, 2), AXES)
    tok = P(PLANE, BLOCKS, None)
    flat = P(AXES)
    rows = P(AXES, None)
    return jax.shard_map(
        local,
        mesh=fine,
        in_specs=(tok, P(PLANE, None), flat, flat) + (rows,) * 13 + (tok,),
        out_specs=(tok, tok) + (rows,) * 9,
        check_vma=False,
    )
```

time: 1720 us -> 499 us (0.29)
  waiting for transfers between devices: 1160 us -> 170 us
  matrix products: 288 us -> 0 us
  Pallas kernels: 0 us -> 116 us
  starting transfers between devices: 0.77 us -> 100 us
  blocking collectives: 68.9 us -> 0 us
  local copies, waits for them, and re-layouts: 123 us -> 57.3 us
  other arithmetic: 53 us -> 31.3 us
    all_gather x4, waiting for transfers between devices: 896 us -> 16.1 us  [the longest x1 16 us: local(): x_plane = lax.all_gather(x_own, PLANE, axis=0, tiled=True)]
    dot_general x97 -> x0, matrix products: 288 us -> none  [the longest x15 85.7 us: product_with_transpose(): lax.dot_general(left, right, (((1,), (1,)), ((), ())), preferred_element_...]
    unnamed x8 -> x4, waiting for transfers between devices: 264 us -> 0.07 us
    pallas_call x0 -> x23, Pallas kernels: none -> 116 us  [the longest x19 60.3 us: call(): pl.pallas_call(kernel, grid=(1,), out_shape=outs, in_specs=ins, out_specs...]
    all_to_all x0 -> x9, waiting for transfers between devices: none -> 81.2 us  [a2a(): return lax.all_to_all(v, axes, 0, 0, tiled=True)]
    ppermute x0 -> x38, waiting for transfers between devices: none -> 72.5 us  [the longest x27 65.6 us: along_x(): return lax.ppermute(v, 'x', [(i, (i + k) % 4) for i in range(4)])]
    unnamed x1 -> x0, blocking collectives: 68.9 us -> none
    ppermute x0 -> x38, starting transfers between devices: none -> 51.9 us  [the longest x27 33.8 us: along_x(): return lax.ppermute(v, 'x', [(i, (i + k) % 4) for i in range(4)])]
  transfers between devices with their start and end apart: 6 -> 51, of which waited for: 6 -> 22; matrix products, arithmetic and copies ran while one was open for 7% -> 12% of each run, Pallas kernels for 0% -> 23%
where the time goes in v1:
time: 499 us; the launch traced here: 492 us
  waiting for transfers between devices  170 us (34%)
  Pallas kernels  116 us (23%)
  starting transfers between devices  100 us (20%)
  local copies, waits for them, and re-layouts  57.3 us (11%)
  other arithmetic  31.3 us (6%)
  between operations  16.5 us (3%)
    all_to_all x9, waiting for transfers between devices, a2a(): return lax.all_to_all(v, axes, 0, 0, tiled=True)  81.2 us
    ppermute x27, waiting for transfers between devices, along_x(): return lax.ppermute(v, 'x', [(i, (i + k) % 4) for i in range(4)])  65.6 us
    pallas_call x19, Pallas kernels, call(): pl.pallas_call(kernel, grid=(1,), out_shape=outs, in_specs=ins, out_specs...  60.3 us
    pallas_call x4, Pallas kernels, tiled_call(): pl.pallas_call(kernel, grid=(steps,), out_shape=outs, in_specs=specs, out...  55.9 us
    all_to_all x9, starting transfers between devices, a2a(): return lax.all_to_all(v, axes, 0, 0, tiled=True)  48.4 us
    ppermute x27, starting transfers between devices, along_x(): return lax.ppermute(v, 'x', [(i, (i + k) % 4) for i in range(4)])  33.8 us
    unnamed x211, local copies, waits for them, and re-layouts  28.4 us
    ppermute x11, starting transfers between devices, other_core(): return lax.ppermute(v, 'c', [(0, 1), (1, 0)])  18.1 us
  transfers between devices with their start and end apart: 51, of which 22 were waited for; matrix products, arithmetic and copies ran while one was open for 12% of the time, Pallas kernels for 23%

profile of v1, /device:TPU:1, one launch (start us, length us, event | category | flops | bytes accessed | tf_op | source)
XLA Modules:
  0.0 491.6 jit_solution(11414003960620469889)
XLA Ops:
  11.6 5.8 %all-to-all-start = ((bf16[8,16,896]{2,1,0:T(8,128)(2,1)}), bf16[8,16,896]{2,1,0:T(8,128)(2,1)S(1)}, u32[]{:S(2)}, u32[]{:S(2)}) async-start(bf16[8,16,896]{2,1,0:T(8,128)(2,1)} %bitcast.19), calls=%async_computation | async-start | bytes 458752 | tf_op jit(solution)/shard_map/all_to_all | solution.py:55
  19.6 2.9 collective-permute-start.2
  24.4 2.4 broadcast_in_dim.99
  26.7 7.9 %all-to-all-start.1 = ((bf16[16,128,896]{2,1,0:T(8,128)(2,1)}), bf16[16,128,896]{2,1,0:T(8,128)(2,1)}, u32[]{:S(2)}, u32[]{:S(2)}) async-start(bf16[16,128,896]{2,1,0:T(8,128)(2,1)} %broadcast_in_dim.99), calls=%async_computation.1 | async-start | bytes 7340032 | tf_op jit(solution)/shard_map/all_to_all | solution.py:55
  35.6 16.0 %all-gather.5.cloned.1.call-done.x = bf16[1024,2048]{1,0:T(8,128)(2,1)} async-done(((bf16[128,2048]{1,0:T(8,128)(2,1)}), bf16[1024,2048]{1,0:T(8,128)(2,1)}) %all-gather.5.cloned.1.call-update) | async-done | bytes 4194320 | tf_op jit(solution)/shard_map/all_gather | solution.py:610
  55.1 33.6 %all-to-all-done.1 = bf16[16,128,896]{2,1,0:T(8,128)(2,1)} async-done(((bf16[16,128,896]{2,1,0:T(8,128)(2,1)}), bf16[16,128,896]{2,1,0:T(8,128)(2,1)}, u32[]{:S(2)}, u32[]{:S(2)}) %all-to-all-start.1) | async-done | bytes 3670048 | tf_op jit(solution)/shard_map/all_to_all | solution.py:55
  96.0 2.3 copy-done.52
  98.3 10.5 %shard_map.257 = (bf16[16,128,256]{2,1,0:T(8,128)(2,1)}, bf16[128,2048]{1,0:T(8,128)(2,1)S(1)}, bf16[256,384]{1,0:T(8,128)(2,1)S(1)}, f32[1,2048]{1,0:T(1,128)S(1)}, f32[1,2048]{1,0:T(1,128)S(1)}) custom-call(s32[2]{0:T(128)S(1)} %pad_add_fusion.place, bf16[1024,2048]{1,0:T(8,128)(2,1)S(1)} %copy-done.52, bf16[2048,896]{1,0:T(8,128)(2,1)} %bitcast.21.e.a, ...), custom_call_target="tpu_custom_call" | custom-call | flops 3221225472 | bytes 9924616 | tf_op jit(solution)/shard_map/pallas_call | solution.py:91
  110.4 4.4 all-to-all-start.2
  117.6 2.8 collective-permute-start.7
  120.6 7.1 %all-to-all-done.2 = bf16[16,128,256]{2,1,0:T(8,128)(2,1)} async-done(((bf16[16,128,256]{2,1,0:T(8,128)(2,1)}), bf16[16,128,256]{2,1,0:T(8,128)(2,1)}, u32[]{:S(2)}, u32[]{:S(2)}) %all-to-all-start.2) | async-done | bytes 1048608 | tf_op jit(solution)/shard_map/all_to_all | solution.py:55
  127.8 4.8 all-to-all-start.3
  135.4 20.0 %collective-permute-done.5.e1 = bf16[512,1280]{1,0:T(8,128)(2,1)S(1)} collective-permute-done((bf16[512,1280]{1,0:T(8,128)(2,1)}, bf16[512,1280]{1,0:T(8,128)(2,1)S(1)}, u32[]{:S(2)}, u32[]{:S(2)}) %collective-permute-start.5) | collective-permute-done | bytes 1310752 | tf_op jit(solution)/shard_map/ppermute | solution.py:63
  157.7 2.3 collective-permute-done.9
  162.9 10.0 %collective-permute-done.11 = bf16[256,1280]{1,0:T(8,128)(2,1)} collective-permute-done((bf16[256,1280]{1,0:T(8,128)(2,1)}, bf16[256,1280]{1,0:T(8,128)(2,1)}, u32[]{:S(2)}, u32[]{:S(2)}) %collective-permute-start.11) | collective-permute-done | bytes 655392 | tf_op jit(solution)/shard_map/ppermute | solution.py:63
  176.3 2.7 collective-permute-start.15
  179.0 7.3 %shard_map.258 = (bf16[2048,128]{1,0:T(8,128)(2,1)}, f32[8,512]{1,0:T(8,128)S(1)}) custom-call(bf16[2048,256]{1,0:T(8,128)(2,1)S(1)} %bitcast.281), custom_call_target="tpu_custom_call" | custom-call | flops 4026531840 | bytes 1589248 | tf_op jit(solution)/shard_map/pallas_call | solution.py:91
  186.3 7.4 %all-to-all-start.4 = ((bf16[16,128,128]{2,1,0:T(8,128)(2,1)}), bf16[16,128,128]{2,1,0:T(8,128)(2,1)S(1)}, u32[]{:S(2)}, u32[]{:S(2)}) async-start(bf16[16,128,128]{2,1,0:T(8,128)(2,1)} %bitcast.46), calls=%async_computation.4 | async-start | bytes 1048576 | tf_op jit(solution)/shard_map/all_to_all | solution.py:55
  193.9 15.5 %all-to-all-done.4.mine = bf16[16,128,128]{2,1,0:T(8,128)(2,1)S(1)} async-done(((bf16[16,128,128]{2,1,0:T(8,128)(2,1)}), bf16[16,128,128]{2,1,0:T(8,128)(2,1)S(1)}, u32[]{:S(2)}, u32[]{:S(2)}) %all-to-all-start.4) | async-done | bytes 524320 | tf_op jit(solution)/shard_map/all_to_all | solution.py:55
  209.4 5.4 %collective-permute-start.13 = (bf16[16,128,128]{2,1,0:T(8,128)(2,1)S(1)}, bf16[16,128,128]{2,1,0:T(8,128)(2,1)S(1)}, u32[]{:S(2)}, u32[]{:S(2)}) collective-permute-start(bf16[16,128,128]{2,1,0:T(8,128)(2,1)S(1)} %all-to-all-done.4.mine), channel_id=1, source_target_pairs={{0,1},{1,0},{2,3},{3,2},{4,5},{5,4},{6,7},{7,6},{8,9},{9,8},{10,11... | collective-permute-start | bytes 1572872 | tf_op jit(solution)/shard_map/ppermute | solution.py:59
  216.0 2.6 collective-permute-start.17
  224.3 4.1 shard_map.259
  236.0 3.4 collective-permute-start.21
  239.4 11.6 %collective-permute-done.19 = bf16[128,2048]{1,0:T(8,128)(2,1)S(1)} collective-permute-done((bf16[128,2048]{1,0:T(8,128)(2,1)S(1)}, bf16[128,2048]{1,0:T(8,128)(2,1)S(1)}, u32[]{:S(2)}, u32[]{:S(2)}) %collective-permute-start.19) | collective-permute-done | bytes 524320 | tf_op jit(solution)/shard_map/ppermute | solution.py:63
  254.6 4.7 collective-permute-done.20
  270.9 11.4 %shard_map.264 = (f32[512,2048]{1,0:T(8,128)}, bf16[512,128]{1,0:T(8,128)(2,1)S(1)}) custom-call(bf16[512,2048]{1,0:T(8,128)(2,1)} %copy-done.16, bf16[2048,512]{1,0:T(8,128)(2,1)} %copy-done.17, bf16[128,2048]{1,0:T(8,128)(2,1)S(1)} %get-tuple-element.102.a_out, bf16[2048,6912]{1,0:T(8,128)(2,1)} %all-gather.9.cloned.1.call-done.a_in.w.w_gate.w_up.a_down, ...), custom_call_target="tpu_custom_call" | custom-call | flops 4294967296 | bytes 12713984 | tf_op jit(solution)/shard_map/pallas_call | solution.py:107
  283.4 17.6 %shard_map.265 = (bf16[256,2048]{1,0:T(8,128)(2,1)S(1)}, bf16[256,2432]{1,0:T(8,128)(2,1)}, f32[16,16,8,128]{3,2,1,0:T(8,128)}, f32[16,16,8,128]{3,2,1,0:T(8,128)}) custom-call(bf16[256,2048]{1,0:T(8,128)(2,1)} %pad_maximum_fusion.n, f32[512,2048]{1,0:T(8,128)} %get-tuple-element.103.d_act, bf16[512,128]{1,0:T(8,128)(2,1)S(1)} %pad_maximum_fusion.10.pick, ...), custom_call_target="tpu_custom_call" | custom-call | flops 8589934592 | bytes 21168128 | tf_op jit(solution)/shard_map/pallas_call | solution.py:107
  302.4 2.6 collective-permute-start.23
  305.2 17.4 %shard_map.266 = (bf16[256,2048]{1,0:T(8,128)(2,1)S(1)}, bf16[256,2432]{1,0:T(8,128)(2,1)}, f32[16,16,8,128]{3,2,1,0:T(8,128)}, f32[16,16,8,128]{3,2,1,0:T(8,128)}) custom-call(bf16[256,2048]{1,0:T(8,128)(2,1)} %pad_maximum_fusion.1.n, f32[512,2048]{1,0:T(8,128)} %get-tuple-element.103.d_act, bf16[512,128]{1,0:T(8,128)(2,1)S(1)} %pad_maximum_fusion.10.pick, ...), custom_call_target="tpu_custom_call" | custom-call | flops 8589934592 | bytes 21168128 | tf_op jit(solution)/shard_map/pallas_call | solution.py:107
  322.5 2.6 fusion.61
  326.5 13.6 %collective-permute-done.25.p3 = bf16[128,2432]{1,0:T(8,128)(2,1)S(1)} collective-permute-done((bf16[128,2432]{1,0:T(8,128)(2,1)S(1)}, bf16[128,2432]{1,0:T(8,128)(2,1)S(1)}, u32[]{:S(2)}, u32[]{:S(2)}) %collective-permute-start.25) | collective-permute-done | bytes 622624 | tf_op jit(solution)/shard_map/ppermute | solution.py:63
  340.9 4.6 shard_map.267
  345.5 3.1 collective-permute-start.26
  355.3 4.2 all-to-all-start.5
  361.4 9.6 %shard_map.271 = (bf16[512,2048]{1,0:T(8,128)(2,1)}, bf16[2048,128]{1,0:T(8,128)(2,1)S(1)}) custom-call(bf16[256,2048]{1,0:T(8,128)(2,1)S(1)} %get-tuple-element.118.act_a, bf16[256,2048]{1,0:T(8,128)(2,1)} %copy-done.23, bf16[512,128]{1,0:T(8,128)(2,1)S(1)} %get-tuple-element.120.d_small, ...), custom_call_target="tpu_custom_call" | custom-call | flops 4294967296 | bytes 11010048 | tf_op jit(solution)/shard_map/pallas_call | solution.py:107
  373.2 6.5 %all-to-all-start.6 = ((bf16[16,640,128]{2,1,0:T(8,128)(2,1)}), bf16[16,640,128]{2,1,0:T(8,128)(2,1)S(1)}, u32[]{:S(2)}, u32[]{:S(2)}) async-start(bf16[16,640,128]{2,1,0:T(8,128)(2,1)} %shard_map.273), calls=%async_computation.6 | async-start | bytes 5242880 | tf_op jit(solution)/shard_map/all_to_all | solution.py:55
  380.2 2.9 fusion.60
  383.1 2.6 collective-permute-start.28
  391.8 14.3 %shard_map.270 = bf16[2048,256]{1,0:T(8,128)(2,1)S(1)} custom-call(bf16[2048,256]{1,0:T(8,128)(2,1)S(1)} %bitcast.282, bf16[2048,128]{1,0:T(8,128)(2,1)} %bitcast.52.d_out, f32[8,512]{1,0:T(8,128)S(1)} %copy-done.54), custom_call_target="tpu_custom_call" | custom-call | flops 10066329600 | bytes 2637824 | tf_op jit(solution)/shard_map/pallas_call | solution.py:91
  407.1 11.6 %all-to-all-done.6.early = bf16[16,640,128]{2,1,0:T(8,128)(2,1)S(1)} async-done(((bf16[16,640,128]{2,1,0:T(8,128)(2,1)}), bf16[16,640,128]{2,1,0:T(8,128)(2,1)S(1)}, u32[]{:S(2)}, u32[]{:S(2)}) %all-to-all-start.6) | async-done | bytes 2621472 | tf_op jit(solution)/shard_map/all_to_all | solution.py:55
  420.8 3.6 collective-permute-start.32
  425.0 2.4 collective-permute-start.37
  427.4 3.7 all-to-all-start.7
  445.5 4.7 all-to-all-done.7.parts
  457.6 3.8 all-to-all-start.8
  461.4 2.9 copy-done.3
  469.0 2.3 shard_map.278
  472.2 8.7 %all-to-all-done.8.late = bf16[128,16,256]{2,1,0:T(8,128)(2,1)S(1)} async-done(((bf16[128,16,256]{2,1,0:T(8,128)(2,1)}), bf16[128,16,256]{2,1,0:T(8,128)(2,1)S(1)}, u32[]{:S(2)}, u32[]{:S(2)}) %all-to-all-start.8) | async-done | bytes 1048608 | tf_op jit(solution)/shard_map/all_to_all | solution.py:55
  (492 shorter events, 121.0 us)
Async XLA Ops:
  7.2 44.5 %all-gather.5.cloned.1.call-start = ((), (), s32[]{:S(2)}) async-start(), calls=%async_computation.9 | async-start | bytes 4718592 | tf_op jit(solution)/shard_map/all_gather | solution.py:610
  11.6 12.8 %all-to-all-start = ((bf16[8,16,896]{2,1,0:T(8,128)(2,1)}), bf16[8,16,896]{2,1,0:T(8,128)(2,1)S(1)}, u32[]{:S(2)}, u32[]{:S(2)}) async-start(bf16[8,16,896]{2,1,0:T(8,128)(2,1)} %bitcast.19), calls=%async_computation | async-start | bytes 458752 | tf_op jit(solution)/shard_map/all_to_all | solution.py:55
  17.7 17.2 %collective-permute-start.4 = (bf16[16,1280]{1,0:T(8,128)(2,1)S(1)}, bf16[16,1280]{1,0:T(8,128)(2,1)S(1)}, u32[]{:S(2)}, u32[]{:S(2)}) collective-permute-start(bf16[16,1280]{1,0:T(8,128)(2,1)S(1)} %get-tuple-element.232), channel_id=1, source_target_pairs={{0,1},{1,0},{2,3},{3,2},{4,5},{5,4},{6,7},{7,6},{8,9},{9,8},{10,11... | collective-permute-start | bytes 122888 | tf_op jit(solution)/shard_map/ppermute | solution.py:59
  19.6 32.1 %collective-permute-start.2 = (bf16[16,4736]{1,0:T(8,128)(2,1)S(1)}, bf16[16,4736]{1,0:T(8,128)(2,1)S(1)}, u32[]{:S(2)}, u32[]{:S(2)}) collective-permute-start(bf16[16,4736]{1,0:T(8,128)(2,1)S(1)} %get-tuple-element.184), channel_id=1, source_target_pairs={{0,6},{2,0},{4,2},{6,4},{1,7},{3,1},{5,3},{7,5},{8,14},{10,8},{12,... | collective-permute-start | bytes 454664 | tf_op jit(solution)/shard_map/ppermute | solution.py:63
  22.6 29.2 %collective-permute-start = (bf16[16,4736]{1,0:T(8,128)(2,1)S(1)}, bf16[16,4736]{1,0:T(8,128)(2,1)S(1)}, u32[]{:S(2)}, u32[]{:S(2)}) collective-permute-start(bf16[16,4736]{1,0:T(8,128)(2,1)S(1)} %get-tuple-element.186), channel_id=1, source_target_pairs={{0,2},{2,4},{4,6},{6,0},{1,3},{3,5},{5,7},{7,1},{8,10},{10,12},{12... | collective-permute-start | bytes 454664 | tf_op jit(solution)/shard_map/ppermute | solution.py:63
  22.6 29.2 %collective-permute-start.1 = (bf16[16,4736]{1,0:T(8,128)(2,1)S(1)}, bf16[16,4736]{1,0:T(8,128)(2,1)S(1)}, u32[]{:S(2)}, u32[]{:S(2)}) collective-permute-start(bf16[16,4736]{1,0:T(8,128)(2,1)S(1)} %get-tuple-element.185), channel_id=1, source_target_pairs={{0,4},{2,6},{4,0},{6,2},{1,5},{3,7},{5,1},{7,3},{8,12},{10,14},{12... | collective-permute-start | bytes 454664 | tf_op jit(solution)/shard_map/ppermute | solution.py:63
  26.7 62.0 %all-to-all-start.1 = ((bf16[16,128,896]{2,1,0:T(8,128)(2,1)}), bf16[16,128,896]{2,1,0:T(8,128)(2,1)}, u32[]{:S(2)}, u32[]{:S(2)}) async-start(bf16[16,128,896]{2,1,0:T(8,128)(2,1)} %broadcast_in_dim.99), calls=%async_computation.1 | async-start | bytes 7340032 | tf_op jit(solution)/shard_map/all_to_all | solution.py:55
  34.7 80.1 %all-gather.7.cloned.1.call-start = ((), (), s32[]{:S(2)}) async-start(), calls=%async_computation.10 | async-start | bytes 1392640 | tf_op jit(solution)/shard_map/all_gather | solution.py:664
  51.7 208.3 %all-gather.9.cloned.1.call-start = ((), (), s32[]{:S(2)}) async-start(), calls=%async_computation.11 | async-start | bytes 29196288 | tf_op jit(solution)/shard_map/all_gather | solution.py:705
  110.4 17.4 %all-to-all-start.2 = ((bf16[16,128,256]{2,1,0:T(8,128)(2,1)}), bf16[16,128,256]{2,1,0:T(8,128)(2,1)}, u32[]{:S(2)}, u32[]{:S(2)}) async-start(bf16[16,128,256]{2,1,0:T(8,128)(2,1)} %get-tuple-element.84), calls=%async_computation.2 | async-start | bytes 2097152 | tf_op jit(solution)/shard_map/all_to_all | solution.py:55
  114.8 40.7 %collective-permute-start.5 = (bf16[512,1280]{1,0:T(8,128)(2,1)}, bf16[512,1280]{1,0:T(8,128)(2,1)S(1)}, u32[]{:S(2)}, u32[]{:S(2)}) collective-permute-start(bf16[512,1280]{1,0:T(8,128)(2,1)} %all-gather.7.cloned.1.call-done.e0), channel_id=1, source_target_pairs={{0,2},{2,4},{4,6},{6,0},{1,3},{3,5},{5,7},{7,1},{8,10},{10,12},{12... | collective-permute-start | bytes 3932168 | tf_op jit(solution)/shard_map/ppermute | solution.py:63
  116.4 43.7 %collective-permute-start.6 = (bf16[512,1280]{1,0:T(8,128)(2,1)}, bf16[512,1280]{1,0:T(8,128)(2,1)}, u32[]{:S(2)}, u32[]{:S(2)}) collective-permute-start(bf16[512,1280]{1,0:T(8,128)(2,1)} %all-gather.7.cloned.1.call-done.e0), channel_id=1, source_target_pairs={{0,6},{2,0},{4,2},{6,4},{1,7},{3,1},{5,3},{7,5},{8,14},{10,8},{12,... | collective-permute-start | bytes 3932168 | tf_op jit(solution)/shard_map/ppermute | solution.py:63
  117.6 14.9 %collective-permute-start.7 = (bf16[16,1664]{1,0:T(8,128)(2,1)S(1)}, bf16[16,1664]{1,0:T(8,128)(2,1)S(1)}, u32[]{:S(2)}, u32[]{:S(2)}) collective-permute-start(bf16[16,1664]{1,0:T(8,128)(2,1)S(1)} %get-tuple-element.218), channel_id=1, source_target_pairs={{0,1},{1,0},{2,3},{3,2},{4,5},{5,4},{6,7},{7,6},{8,9},{9,8},{10,11... | collective-permute-start | bytes 159752 | tf_op jit(solution)/shard_map/ppermute | solution.py:59
  127.8 35.2 %all-to-all-start.3 = ((bf16[16,128,256]{2,1,0:T(8,128)(2,1)}), bf16[16,128,256]{2,1,0:T(8,128)(2,1)S(1)}, u32[]{:S(2)}, u32[]{:S(2)}) async-start(bf16[16,128,256]{2,1,0:T(8,128)(2,1)} %all-to-all-done.2), calls=%async_computation.3 | async-start | bytes 2097152 | tf_op jit(solution)/shard_map/all_to_all | solution.py:55
  132.6 25.2 %collective-permute-start.8 = (bf16[32,1664]{1,0:T(8,128)(2,1)S(1)}, bf16[32,1664]{1,0:T(8,128)(2,1)S(1)}, u32[]{:S(2)}, u32[]{:S(2)}) collective-permute-start(bf16[32,1664]{1,0:T(8,128)(2,1)S(1)} %maximum_select_fusion.2), channel_id=1, source_target_pairs={{0,2},{2,4},{4,6},{6,0},{1,3},{3,5},{5,7},{7,1},{8,10},{10,12},{12... | collective-permute-start | bytes 319496 | tf_op jit(solution)/shard_map/ppermute | solution.py:63
  132.9 27.1 %collective-permute-start.9 = (bf16[32,1664]{1,0:T(8,128)(2,1)S(1)}, bf16[32,1664]{1,0:T(8,128)(2,1)S(1)}, u32[]{:S(2)}, u32[]{:S(2)}) collective-permute-start(bf16[32,1664]{1,0:T(8,128)(2,1)S(1)} %maximum_select_fusion.2), channel_id=1, source_target_pairs={{0,4},{2,6},{4,0},{6,2},{1,5},{3,7},{5,1},{7,3},{8,12},{10,14},{12... | collective-permute-start | bytes 319496 | tf_op jit(solution)/shard_map/ppermute | solution.py:63
  134.8 25.2 %collective-permute-start.10 = (bf16[32,1664]{1,0:T(8,128)(2,1)S(1)}, bf16[32,1664]{1,0:T(8,128)(2,1)S(1)}, u32[]{:S(2)}, u32[]{:S(2)}) collective-permute-start(bf16[32,1664]{1,0:T(8,128)(2,1)S(1)} %maximum_select_fusion.2), channel_id=1, source_target_pairs={{0,6},{2,0},{4,2},{6,4},{1,7},{3,1},{5,3},{7,5},{8,14},{10,8},{12,... | collective-permute-start | bytes 319496 | tf_op jit(solution)/shard_map/ppermute | solution.py:63
  156.4 16.6 %collective-permute-start.11 = (bf16[256,1280]{1,0:T(8,128)(2,1)}, bf16[256,1280]{1,0:T(8,128)(2,1)}, u32[]{:S(2)}, u32[]{:S(2)}) collective-permute-start(bf16[256,1280]{1,0:T(8,128)(2,1)} %slice.641), channel_id=1, source_target_pairs={{0,2},{2,4},{4,6},{6,0},{1,3},{3,5},{5,7},{7,1},{8,10},{10,12},{12... | collective-permute-start | bytes 1966088 | tf_op jit(solution)/shard_map/ppermute | solution.py:63
  162.1 12.0 %collective-permute-start.12 = (bf16[256,1280]{1,0:T(8,128)(2,1)}, bf16[256,1280]{1,0:T(8,128)(2,1)}, u32[]{:S(2)}, u32[]{:S(2)}) collective-permute-start(bf16[256,1280]{1,0:T(8,128)(2,1)} %slice.642), channel_id=1, source_target_pairs={{0,6},{2,0},{4,2},{6,4},{1,7},{3,1},{5,3},{7,5},{8,14},{10,8},{12,... | collective-permute-start | bytes 1966088 | tf_op jit(solution)/shard_map/ppermute | solution.py:63
  176.3 38.5 %collective-permute-start.14 = (bf16[128,2048]{1,0:T(8,128)(2,1)S(1)}, bf16[128,2048]{1,0:T(8,128)(2,1)S(1)}, u32[]{:S(2)}, u32[]{:S(2)}) collective-permute-start(bf16[128,2048]{1,0:T(8,128)(2,1)S(1)} %pad_maximum_fusion.5.cot), channel_id=1, source_target_pairs={{0,2},{2,4},{4,6},{6,0},{1,3},{3,5},{5,7},{7,1},{8,10},{10,12},{12... | collective-permute-start | bytes 1572872 | tf_op jit(solution)/shard_map/ppermute | solution.py:63
  176.3 38.6 %collective-permute-start.15 = (bf16[128,2048]{1,0:T(8,128)(2,1)S(1)}, bf16[128,2048]{1,0:T(8,128)(2,1)}, u32[]{:S(2)}, u32[]{:S(2)}) collective-permute-start(bf16[128,2048]{1,0:T(8,128)(2,1)S(1)} %pad_maximum_fusion.5.cot), channel_id=1, source_target_pairs={{0,6},{2,0},{4,2},{6,4},{1,7},{3,1},{5,3},{7,5},{8,14},{10,8},{12,... | collective-permute-start | bytes 1572872 | tf_op jit(solution)/shard_map/ppermute | solution.py:63
  186.3 23.2 %all-to-all-start.4 = ((bf16[16,128,128]{2,1,0:T(8,128)(2,1)}), bf16[16,128,128]{2,1,0:T(8,128)(2,1)S(1)}, u32[]{:S(2)}, u32[]{:S(2)}) async-start(bf16[16,128,128]{2,1,0:T(8,128)(2,1)} %bitcast.46), calls=%async_computation.4 | async-start | bytes 1048576 | tf_op jit(solution)/shard_map/all_to_all | solution.py:55
  193.6 193.5 %all-gather.11.cloned.1.call-start = ((), (), s32[]{:S(2)}) async-start(), calls=%async_computation.12 | async-start | bytes 7241728 | tf_op jit(solution)/shard_map/all_gather | solution.py:840
  209.4 14.8 %collective-permute-start.13 = (bf16[16,128,128]{2,1,0:T(8,128)(2,1)S(1)}, bf16[16,128,128]{2,1,0:T(8,128)(2,1)S(1)}, u32[]{:S(2)}, u32[]{:S(2)}) collective-permute-start(bf16[16,128,128]{2,1,0:T(8,128)(2,1)S(1)} %all-to-all-done.4.mine), channel_id=1, source_target_pairs={{0,1},{1,0},{2,3},{3,2},{4,5},{5,4},{6,7},{7,6},{8,9},{9,8},{10,11... | collective-permute-start | bytes 1572872 | tf_op jit(solution)/shard_map/ppermute | solution.py:59
  214.8 9.3 %collective-permute-start.16 = (bf16[64,2048]{1,0:T(8,128)(2,1)S(1)}, bf16[64,2048]{1,0:T(8,128)(2,1)S(1)}, u32[]{:S(2)}, u32[]{:S(2)}) collective-permute-start(bf16[64,2048]{1,0:T(8,128)(2,1)S(1)} %slice.647), channel_id=1, source_target_pairs={{0,2},{2,4},{4,6},{6,0},{1,3},{3,5},{5,7},{7,1},{8,10},{10,12},{12... | collective-permute-start | bytes 786440 | tf_op jit(solution)/shard_map/ppermute | solution.py:63
  216.0 8.2 %collective-permute-start.17 = (bf16[64,2048]{1,0:T(8,128)(2,1)S(1)}, bf16[64,2048]{1,0:T(8,128)(2,1)S(1)}, u32[]{:S(2)}, u32[]{:S(2)}) collective-permute-start(bf16[64,2048]{1,0:T(8,128)(2,1)S(1)} %slice.648), channel_id=1, source_target_pairs={{0,6},{2,0},{4,2},{6,4},{1,7},{3,1},{5,3},{7,5},{8,14},{10,8},{12,... | collective-permute-start | bytes 786440 | tf_op jit(solution)/shard_map/ppermute | solution.py:63
  230.7 2.6 collective-permute-start.18
  235.2 15.8 %collective-permute-start.19 = (bf16[128,2048]{1,0:T(8,128)(2,1)S(1)}, bf16[128,2048]{1,0:T(8,128)(2,1)S(1)}, u32[]{:S(2)}, u32[]{:S(2)}) collective-permute-start(bf16[128,2048]{1,0:T(8,128)(2,1)S(1)} %get-tuple-element.95.normed), channel_id=1, source_target_pairs={{0,2},{2,4},{4,6},{6,0},{1,3},{3,5},{5,7},{7,1},{8,10},{10,12},{12... | collective-permute-start | bytes 1572872 | tf_op jit(solution)/shard_map/ppermute | solution.py:63
  236.0 15.1 %collective-permute-start.21 = (bf16[128,2048]{1,0:T(8,128)(2,1)S(1)}, bf16[128,2048]{1,0:T(8,128)(2,1)S(1)}, u32[]{:S(2)}, u32[]{:S(2)}) collective-permute-start(bf16[128,2048]{1,0:T(8,128)(2,1)S(1)} %get-tuple-element.95.normed), channel_id=1, source_target_pairs={{0,6},{2,0},{4,2},{6,4},{1,7},{3,1},{5,3},{7,5},{8,14},{10,8},{12,... | collective-permute-start | bytes 1572872 | tf_op jit(solution)/shard_map/ppermute | solution.py:63
  251.1 8.2 %collective-permute-start.20 = (bf16[64,2048]{1,0:T(8,128)(2,1)S(1)}, bf16[64,2048]{1,0:T(8,128)(2,1)S(1)}, u32[]{:S(2)}, u32[]{:S(2)}) collective-permute-start(bf16[64,2048]{1,0:T(8,128)(2,1)S(1)} %slice.649), channel_id=1, source_target_pairs={{0,2},{2,4},{4,6},{6,0},{1,3},{3,5},{5,7},{7,1},{8,10},{10,12},{12... | collective-permute-start | bytes 786440 | tf_op jit(solution)/shard_map/ppermute | solution.py:63
  252.6 7.4 %collective-permute-start.22 = (bf16[64,2048]{1,0:T(8,128)(2,1)S(1)}, bf16[64,2048]{1,0:T(8,128)(2,1)}, u32[]{:S(2)}, u32[]{:S(2)}) collective-permute-start(bf16[64,2048]{1,0:T(8,128)(2,1)S(1)} %slice.650), channel_id=1, source_target_pairs={{0,6},{2,0},{4,2},{6,4},{1,7},{3,1},{5,3},{7,5},{8,14},{10,8},{12,... | collective-permute-start | bytes 786440 | tf_op jit(solution)/shard_map/ppermute | solution.py:63
  302.4 22.8 %collective-permute-start.23 = (bf16[128,2432]{1,0:T(8,128)(2,1)S(1)}, bf16[128,2432]{1,0:T(8,128)(2,1)S(1)}, u32[]{:S(2)}, u32[]{:S(2)}) collective-permute-start(bf16[128,2432]{1,0:T(8,128)(2,1)S(1)} %get-tuple-element.176), channel_id=1, source_target_pairs={{0,6},{2,0},{4,2},{6,4},{1,7},{3,1},{5,3},{7,5},{8,14},{10,8},{12,... | collective-permute-start | bytes 1867784 | tf_op jit(solution)/shard_map/ppermute | solution.py:63
  305.0 20.1 %collective-permute-start.24 = (bf16[128,2432]{1,0:T(8,128)(2,1)S(1)}, bf16[128,2432]{1,0:T(8,128)(2,1)S(1)}, u32[]{:S(2)}, u32[]{:S(2)}) collective-permute-start(bf16[128,2432]{1,0:T(8,128)(2,1)S(1)} %get-tuple-element.175), channel_id=1, source_target_pairs={{0,2},{2,4},{4,6},{6,0},{1,3},{3,5},{5,7},{7,1},{8,10},{10,12},{12... | collective-permute-start | bytes 1867784 | tf_op jit(solution)/shard_map/ppermute | solution.py:63
  325.1 15.0 %collective-permute-start.25 = (bf16[128,2432]{1,0:T(8,128)(2,1)S(1)}, bf16[128,2432]{1,0:T(8,128)(2,1)S(1)}, u32[]{:S(2)}, u32[]{:S(2)}) collective-permute-start(bf16[128,2432]{1,0:T(8,128)(2,1)S(1)} %get-tuple-element.109), channel_id=1, source_target_pairs={{0,4},{2,6},{4,0},{6,2},{1,5},{3,7},{5,1},{7,3},{8,12},{10,14},{12... | collective-permute-start | bytes 1867784 | tf_op jit(solution)/shard_map/ppermute | solution.py:63
  345.5 4.6 collective-permute-start.26
  352.4 2.0 collective-permute-start.27
  355.3 17.9 %all-to-all-start.5 = ((bf16[16,128,128]{2,1,0:T(8,128)(2,1)}), bf16[16,128,128]{2,1,0:T(8,128)(2,1)}, u32[]{:S(2)}, u32[]{:S(2)}) async-start(bf16[16,128,128]{2,1,0:T(8,128)(2,1)} %shard_map.269), calls=%async_computation.5 | async-start | bytes 1048576 | tf_op jit(solution)/shard_map/all_to_all | solution.py:55
  373.2 45.5 %all-to-all-start.6 = ((bf16[16,640,128]{2,1,0:T(8,128)(2,1)}), bf16[16,640,128]{2,1,0:T(8,128)(2,1)S(1)}, u32[]{:S(2)}, u32[]{:S(2)}) async-start(bf16[16,640,128]{2,1,0:T(8,128)(2,1)} %shard_map.273), calls=%async_computation.6 | async-start | bytes 5242880 | tf_op jit(solution)/shard_map/all_to_all | solution.py:55
  383.1 41.9 %collective-permute-start.28 = (bf16[128,2048]{1,0:T(8,128)(2,1)}, bf16[128,2048]{1,0:T(8,128)(2,1)}, u32[]{:S(2)}, u32[]{:S(2)}) collective-permute-start(bf16[128,2048]{1,0:T(8,128)(2,1)} %get-tuple-element.172), channel_id=1, source_target_pairs={{0,6},{2,0},{4,2},{6,4},{1,7},{3,1},{5,3},{7,5},{8,14},{10,8},{12,... | collective-permute-start | bytes 1572872 | tf_op jit(solution)/shard_map/ppermute | solution.py:63
  385.7 39.2 %collective-permute-start.29 = (bf16[128,2048]{1,0:T(8,128)(2,1)}, bf16[128,2048]{1,0:T(8,128)(2,1)}, u32[]{:S(2)}, u32[]{:S(2)}) collective-permute-start(bf16[128,2048]{1,0:T(8,128)(2,1)} %get-tuple-element.171), channel_id=1, source_target_pairs={{0,2},{2,4},{4,6},{6,0},{1,3},{3,5},{5,7},{7,1},{8,10},{10,12},{12... | collective-permute-start | bytes 1572872 | tf_op jit(solution)/shard_map/ppermute | solution.py:63
  385.7 41.7 %collective-permute-start.30 = (bf16[128,2048]{1,0:T(8,128)(2,1)}, bf16[128,2048]{1,0:T(8,128)(2,1)}, u32[]{:S(2)}, u32[]{:S(2)}) collective-permute-start(bf16[128,2048]{1,0:T(8,128)(2,1)} %get-tuple-element.169), channel_id=1, source_target_pairs={{0,4},{2,6},{4,0},{6,2},{1,5},{3,7},{5,1},{7,3},{8,12},{10,14},{12... | collective-permute-start | bytes 1572872 | tf_op jit(solution)/shard_map/ppermute | solution.py:63
  420.5 15.9 %collective-permute-start.31 = (f32[2,120,128]{2,1,0:T(8,128)}, f32[2,120,128]{2,1,0:T(8,128)}, u32[]{:S(2)}, u32[]{:S(2)}) collective-permute-start(f32[2,120,128]{2,1,0:T(8,128)} %get-tuple-element.206), channel_id=1, source_target_pairs={{0,2},{2,4},{4,6},{6,0},{1,3},{3,5},{5,7},{7,1},{8,10},{10,12},{12... | collective-permute-start | bytes 368648 | tf_op jit(solution)/shard_map/ppermute | solution.py:63
  420.8 15.7 %collective-permute-start.32 = (f32[2,120,128]{2,1,0:T(8,128)}, f32[2,120,128]{2,1,0:T(8,128)}, u32[]{:S(2)}, u32[]{:S(2)}) collective-permute-start(f32[2,120,128]{2,1,0:T(8,128)} %get-tuple-element.205), channel_id=1, source_target_pairs={{0,4},{2,6},{4,0},{6,2},{1,5},{3,7},{5,1},{7,3},{8,12},{10,14},{12... | collective-permute-start | bytes 368648 | tf_op jit(solution)/shard_map/ppermute | solution.py:63
  425.0 11.5 %collective-permute-start.33 = (f32[2,120,128]{2,1,0:T(8,128)}, f32[2,120,128]{2,1,0:T(8,128)}, u32[]{:S(2)}, u32[]{:S(2)}) collective-permute-start(f32[2,120,128]{2,1,0:T(8,128)} %get-tuple-element.204), channel_id=1, source_target_pairs={{0,6},{2,0},{4,2},{6,4},{1,7},{3,1},{5,3},{7,5},{8,14},{10,8},{12,... | collective-permute-start | bytes 368648 | tf_op jit(solution)/shard_map/ppermute | solution.py:63
  425.0 10.7 %collective-permute-start.37 = (f32[64,128]{1,0:T(8,128)}, f32[64,128]{1,0:T(8,128)}, u32[]{:S(2)}, u32[]{:S(2)}) collective-permute-start(f32[64,128]{1,0:T(8,128)} %dynamic-slice_bitcast_fusion.15), channel_id=1, source_target_pairs={{0,1},{1,0},{2,3},{3,2},{4,5},{5,4},{6,7},{7,6},{8,9},{9,8},{10,11... | collective-permute-start | bytes 98312 | tf_op jit(solution)/shard_map/ppermute | solution.py:59
  427.4 22.8 %all-to-all-start.7 = ((bf16[16,128,256]{2,1,0:T(8,128)(2,1)}), bf16[16,128,256]{2,1,0:T(8,128)(2,1)S(1)}, u32[]{:S(2)}, u32[]{:S(2)}) async-start(bf16[16,128,256]{2,1,0:T(8,128)(2,1)} %bitcast.283), calls=%async_computation.7 | async-start | bytes 2097152 | tf_op jit(solution)/shard_map/all_to_all | solution.py:55
  457.6 23.3 %all-to-all-start.8 = ((bf16[128,16,256]{2,1,0:T(8,128)(2,1)}), bf16[128,16,256]{2,1,0:T(8,128)(2,1)S(1)}, u32[]{:S(2)}, u32[]{:S(2)}) async-start(bf16[128,16,256]{2,1,0:T(8,128)(2,1)} %bitcast.68), calls=%async_computation.8 | async-start | bytes 2097152 | tf_op jit(solution)/shard_map/all_to_all | solution.py:55
  466.2 2.8 collective-permute-start.36
  (96 other events, 683.5 us)
Sparse Core Ops, SparseCore 0:
  10.3 41.2 all-gather.4
  54.4 55.6 all-gather.6
  112.3 117.7 all-gather.8
  260.1 62.2 all-gather.10

commit v2 on v1

--- a/solution.py
+++ b/solution.py
@@ -84,12 +84,14 @@
     return one, three, far_of(one, three)
 
 
-def call(kernel, outs, args, scratch=(), specs=None, flops=0, vmem=24):
+def call(kernel, outs, args, scratch=(), specs=None, flops=0, vmem=24, deps=()):
     if specs is None:
         specs = [None] * len(args)
     ins = [pl.BlockSpec(memory_space=pltpu.VMEM) if s is None else s for s in specs]
+    ins = ins + [pl.BlockSpec(memory_space=pl.ANY)] * len(deps)
     return pl.pallas_call(
-        kernel,
+        ignoring(kernel, len(args), len(deps)),
+        name=kernel.__name__,
         grid=(1,),
         out_shape=outs,
         in_specs=ins,
@@ -99,21 +101,24 @@
         cost_estimate=pl.CostEstimate(
             flops=flops, bytes_accessed=nbytes(args) + nbytes(outs), transcendentals=0
         ),
-    )(*args)
-
-
-def tiled_call(kernel, outs, args, specs, out_specs, scratch=(), flops=0, steps=4, vmem=32):
+    )(*args, *deps)
+
+
+def tiled_call(
+    kernel, outs, args, specs, out_specs, scratch=(), flops=0, steps=4, vmem=32, deps=()
+):
     size = nbytes(outs) + 2 * flops // 1024
     return pl.pallas_call(
-        kernel,
+        ignoring(kernel, len(args), len(deps)),
+        name=kernel.__name__,
         grid=(steps,),
         out_shape=outs,
-        in_specs=specs,
+        in_specs=specs + [pl.BlockSpec(memory_space=pl.ANY)] * len(deps),
         out_specs=out_specs,
         scratch_shapes=list(scratch),
         compiler_params=pltpu.CompilerParams(vmem_limit_bytes=vmem * MIB),
         cost_estimate=pl.CostEstimate(flops=flops, bytes_accessed=size, transcendentals=0),
-    )(*args)
+    )(*args, *deps)
 
 
 def shape(*dims, dtype=F32):
@@ -124,12 +129,26 @@
     return pl.BlockSpec((rows, cols), lambda i: (0, index), pipeline_mode=pl.Buffered(1))
 
 
+def once(rows, cols):
+    return pl.BlockSpec((rows, cols), lambda i: (0, 0), pipeline_mode=pl.Buffered(1))
+
+
 def whole_spec(rows, cols):
     return pl.BlockSpec((rows, cols), lambda i: (0, 0))
 
 
-def after(v, *others):
-    return lax.optimization_barrier((v, others))[0]
+def ignoring(kernel, first, count):
+    def body(*refs):
+        kernel(*refs[:first], *refs[first + count :])
+
+    return body
+
+
+def gate(v, *deps):
+    def copy(ref, out):
+        out[...] = ref[...]
+
+    return call(copy, [jax.ShapeDtypeStruct(v.shape, v.dtype)], [v], deps=deps, vmem=8)[0]
 
 
 def segment_of(block_index):
@@ -283,7 +302,8 @@
 
 
 def project_kernel(
-    place, mine, theirs, e0, e1, e2, e3, pick, part, small, attended, whole, a_out, att, wide
+    place, mine, theirs, e0, e1, e2, e3, pick,
+    part, their_part, small, attended, whole, a_out, att, wide,
 ):
     assemble(place[0], (e0, e1, e2, e3), whole)
     wide[...] = whole[:, 1152:1280].astype(F32)
@@ -305,11 +325,13 @@
     s = s.astype(BF16)
     s = jnp.concatenate([s[:TOK] * pick[0:1, :128], s[TOK:] * pick[1:2, :128]], axis=0)
     small[...] = s
-    part[...] = (
+    both = (
         mm(m, whole[pl.ds(here, 1024), :1024])
         + mm(t, whole[pl.ds(there, 1024), :1024])
         + 2.0 * mm(s, a_out[:, pl.ds(here, 1024)])
     )
+    part[...] = both[:TOK]
+    their_part[...] = both[TOK:]
 
 
 def hidden_kernel(place, x, mine, theirs, gain, hidden, normed):
@@ -324,6 +346,11 @@
     normed[...] = (h * r * gain[...]).astype(BF16)
 
 
+def halves_kernel(one, three, half_one, half_three):
+    half_one[...] = one[: TOK // 2, :]
+    half_three[...] = three[TOK // 2 :, :]
+
+
 def unpack_kernel(outs, gu_out, down_out, wide):
     for k in range(3):
         wide[...] = outs[:, k * 128 : (k + 1) * 128].astype(F32)
@@ -352,13 +379,15 @@
 
 
 def feed_kernel(
-    n, d_act, pick, w_gate, w_up, o_gate, o_up, a_in, a_down, g_gate0, g_up0,
-    act, back, g_gate, g_up, total, small,
+    n_one, n_two, d_act, pick, w_gate, w_up, o_gate, o_up, a_in, a_down, g_gate0, g_up0,
+    act, back, back1, g_gate, g_up, total, small, n,
 ):
     step = pl.program_id(0)
 
     @pl.when(step == 0)
     def _():
+        n[:TOK, :] = n_one[...]
+        n[TOK:, :] = n_two[...]
         s = mm(n[...], a_in[...]).astype(BF16)
         p = pick[...]
         small[...] = s * jnp.concatenate([p, p], axis=1)
@@ -386,10 +415,11 @@
 
     @pl.when(step == pl.num_programs(0) - 1)
     def _():
-        back[...] = total[...].T.astype(BF16)
-
-
-def down_kernel(act_a, act_b, d_small, w, out, g_in, total):
+        back[...] = total[:, :TOK].T.astype(BF16)
+        back1[...] = total[:, TOK:].T.astype(BF16)
+
+
+def down_kernel(act_a, act_b, d_small, w, out, out1, out2, out3, g_in, total):
     step = pl.program_id(0)
 
     @pl.when(step == 0)
@@ -404,7 +434,8 @@
 
     @pl.when(step == pl.num_programs(0) - 1)
     def _():
-        out[...] = total[...].astype(BF16)
+        for k, ref in enumerate((out, out1, out2, out3)):
+            ref[...] = total[k * TOK : (k + 1) * TOK, :].astype(BF16)
 
 
 def output_kernel(hidden, p0, p1, p2, p3, a_out, small, out):
@@ -456,7 +487,7 @@
 
 
 def early_grads_kernel(
-    gu, g_down_in, d_small_gu, normed, small_down, cot, d_small_o, attended, small_o, halves, fold,
+    g_down_in, d_small_gu, normed, small_down, cot, d_small_o, attended, small_o, halves, fold,
     out, lines,
 ):
     f = mm(d_small_gu[...], fold[:256, :]).astype(BF16)[:, :HDIM]
@@ -474,15 +505,14 @@
         for t in range(8):
             lines[k, 320 + t * 8 : 328 + t * 8, :] = g_o[rows, t * 128 : (t + 1) * 128]
         out[k, :128, :] = g_down_in[k * 128 : (k + 1) * 128, :]
-        out[k, 128:384, :] = lines[k, 128:, :].astype(BF16)
-        out[k, 384:, :] = gu[k]
-
-
-def sums_kernel(slot, early, plane, g_down_in, first, total):
+        out[k, 128:, :] = lines[k, 128:, :].astype(BF16)
+
+
+def sums_kernel(slot, gu, early, plane, g_down_in, first, total):
     first[...] = jnp.zeros_like(first)
-    total[...] = early[0, 384:, :].astype(F32)
+    total[...] = gu[0].astype(F32)
     for k in range(1, 16):
-        total[...] += early[k, 384:, :].astype(F32)
+        total[...] += gu[k].astype(F32)
     for r in range(8):
         plane[r, 0:32, :] = total[pl.ds(r, 32, stride=8), :]
     d = early[0, :128, :].astype(F32)
@@ -639,9 +669,9 @@
         axis=2,
     )
     heads = payload.reshape(2, 4, 16, 896).transpose(1, 0, 2, 3).reshape(8, 16, 896)
-    heads = a2a(heads, PLANE)
-    ids_all = heads[:, 3, 800:805].astype(F32)
-    heads = jnp.broadcast_to(heads.reshape(1, 128, 896), (16, 128, 896))
+    in_plane = a2a(heads, PLANE)
+    ids_all = in_plane[:, 3, 800:805].astype(F32)
+    heads = jnp.broadcast_to(in_plane.reshape(1, 128, 896), (16, 128, 896))
     heads = a2a(heads, NATURAL).reshape(D, 896)
 
     o_w = swap_mid(output_projection_weight).reshape(16, 2, 1024)
@@ -661,7 +691,7 @@
         return jnp.where(c == 0, jnp.concatenate([keep, take]), jnp.concatenate([take, keep]))
 
     chip = chip_rows(payload)
-    o_mine = lax.all_gather(after(chip, x_plane), NATURAL, axis=0, tiled=True)
+    o_mine = lax.all_gather(gate(chip, x_plane, in_plane), NATURAL, axis=0, tiled=True)
     o_set = [o_mine, *from_x(o_mine)]
 
     gu = gate_up_weight.reshape(16, 2, 2, 2, 4, 4, 128).transpose(5, 0, 1, 3, 2, 4, 6)
@@ -679,6 +709,8 @@
         axis=2,
     )
 
+    to_x = gate(to_x, x_plane)
+
     def for_chip(k):
         return lax.dynamic_index_in_dim(to_x, (x + k) % 4, 0, keepdims=False)
 
@@ -702,7 +734,6 @@
         [plane[:, :4096], down_w, plane[:, 4096:4352], down_in, plane[:, 4352:]], axis=1
     )
 
-    mlp_set = lax.all_gather(after(plane, heads), NATURAL + ("c",), axis=0, tiled=True)
 
     segment = segment_of(b)
     start = jnp.where(b < 8, b * TOK, PROMPT + ((b - 8) % 2) * TOK)
@@ -743,7 +774,8 @@
             shape(1, D),
             shape(1, D),
         ],
-        [place, after(x_plane, plane), heads, pick_all, cq, sq, ckv, skv],
+        [place, x_plane, heads, pick_all, cq, sq, ckv, skv],
+        deps=[plane],
         scratch=[
             pltpu.VMEM((1024, D), BF16),
             pltpu.VMEM((1024, 384), BF16),
@@ -753,8 +785,9 @@
         flops=2 * 1024 * D * 768,
         vmem=40,
     )
+    mlp_set = lax.all_gather(gate(plane, o_mine, send), NATURAL + ("c",), axis=0, tiled=True)
     z = a2a(a2a(send, "x"), BLOCKS).reshape(GTOK, 256)
-    cot = [cot_own, *from_x(after(cot_own, o_set))]
+    cot = [cot_own, *from_x(gate(cot_own, o_set[1]))]
     cot = jnp.concatenate([cot[1], cot[2], cot[0], cot[3]])
 
     t2 = jnp.concatenate(
@@ -775,22 +808,24 @@
     attended, stat = call(
         attend_kernel,
         [shape(GTOK, 128, dtype=BF16), shape(8, 512)],
-        [after(z, o_set[:3])],
+        [z],
+        deps=o_set[1:3],
         flops=2 * 2 * 2 * 30 * CLEN * CLEN * HDIM * 4,
         vmem=20,
     )
-    mine = a2a(after(attended, t2, o_set).reshape(16, TOK, 128), BLOCKS)
+    mine = a2a(attended.reshape(16, TOK, 128), BLOCKS)
     theirs = other_core(mine)
-    part, small_o, attended, o_whole, out_out = call(
+    part, their_part, small_o, attended, o_whole, out_out = call(
         project_kernel,
         [
-            shape(256, 1024),
+            shape(TOK, 1024),
+            shape(TOK, 1024),
             shape(256, 128, dtype=BF16),
             shape(TOK, D, dtype=BF16),
             shape(D, 1280, dtype=BF16),
             shape(128, D, dtype=BF16),
         ],
-        [place, mine, after(theirs, cot), *o_set, pick],
+        [place, mine, theirs, *o_set, pick],
         scratch=[pltpu.VMEM((2, 256, 1024), BF16), pltpu.VMEM((D, 128), F32)],
         specs=[SMEM] + [None] * 7,
         flops=2 * 256 * D * 1024,
@@ -825,7 +860,8 @@
     hidden, normed_mlp = call(
         hidden_kernel,
         [shape(TOK, D), shape(TOK, D, dtype=BF16)],
-        [place, x_own, part[:TOK], other_core(part[TOK:]), gain_mlp],
+        [place, x_own, part, other_core(their_part), gain_mlp],
+        deps=[cot],
         specs=[SMEM] + [None] * 4,
         vmem=10,
     )
@@ -836,9 +872,7 @@
     dm, turned = call(
         turn_kernel, [shape(512, D, dtype=BF16), shape(D, 512, dtype=BF16)], [cot]
     )
-    n1, n3, n2 = from_x(normed_mlp)
-    t2 = lax.all_gather(after(t2, mlp_set, n2), NATURAL, axis=0, tiled=True)
-    dm = after(dm, n1, n2, n3)
+    n1, n3 = along_x(normed_mlp, 1), along_x(normed_mlp, 3)
     d_act, d_small_down = tiled_call(
         d_act_kernel,
         [shape(512, 2048), shape(512, 128, dtype=BF16)],
@@ -856,19 +890,31 @@
         vmem=52,
     )
 
-    def feed(part, n, g_gate, g_up):
+    half_one, half_three = call(
+        halves_kernel,
+        [shape(TOK // 2, D, dtype=BF16)] * 2,
+        [n1, n3],
+        deps=[d_act],
+        vmem=6,
+    )
+    n2 = jnp.concatenate([along_x(half_one, 1), along_x(half_three, 3)])
+    t2 = lax.all_gather(gate(t2, normed_mlp), NATURAL, axis=0, tiled=True)
+
+    def feed(part, one, two, g_gate, g_up):
         lines = pl.BlockSpec((16, 4, 8, 128), lambda i: (0, i, 0, 0))
         return tiled_call(
             feed_kernel,
             [
                 shape(256, 2048, dtype=BF16),
-                shape(256, D + 384, dtype=BF16),
+                shape(TOK, D + 384, dtype=BF16),
+                shape(TOK, D + 384, dtype=BF16),
                 shape(16, 16, 8, 128),
                 shape(16, 16, 8, 128),
             ],
-            [n, d_act, pick4, mlp_set, mlp_set, gu_out, gu_out, mlp_set, mlp_set, g_gate, g_up],
+            [one, two, d_act, pick4, mlp_set, mlp_set, gu_out, gu_out, mlp_set, mlp_set, g_gate, g_up],
             [
-                whole_spec(256, D),
+                once(TOK, D),
+                once(TOK, D),
                 pl.BlockSpec((256, 512), lambda i: (part, i)),
                 pl.BlockSpec((256, 128), lambda i: (part, 0)),
                 pl.BlockSpec((D, 512), lambda i: (0, i)),
@@ -880,20 +926,37 @@
                 lines,
                 lines,
             ],
-            [pl.BlockSpec((256, 512), lambda i: (0, i)), whole_spec(256, D + 384), lines, lines],
-            [pltpu.VMEM((D + 384, 256), F32), pltpu.VMEM((256, 256), BF16)],
+            [pl.BlockSpec((256, 512), lambda i: (0, i))]
+            + [whole_spec(TOK, D + 384)] * 2
+            + [lines] * 2,
+            [pltpu.VMEM((D + 384, 256), F32), pltpu.VMEM((256, 256), BF16), pltpu.VMEM((256, D), BF16)],
             flops=2 * 256 * 4096 * D * 2,
             vmem=52,
         )
 
     none = jnp.zeros((16, 16, 8, 128), F32)
-    act_a, back_a, g_gate, g_up = feed(0, jnp.concatenate([n1, n3]), none, none)
-    back = [along_x(back_a[:TOK], 3), along_x(back_a[TOK:], 1)]
-    act_b, back_b, g_gate, g_up = feed(1, jnp.concatenate([normed_mlp, n2]), g_gate, g_up)
-    back = [*back, back_b[:TOK], along_x(after(back_b[TOK:], back), 2)]
+    act_a, back_1, back_3, g_gate, g_up = feed(0, n1, n3, none, none)
+    act_b, back_b, back_2, g_gate, g_up = feed(1, normed_mlp, n2, g_gate, g_up)
+    back = [along_x(back_1, 3), along_x(back_3, 1), back_b, along_x(back_2, 2)]
 
     gu_lines = 2.0 * jnp.concatenate([g_gate, g_up], axis=1).reshape(16, 256, 128)
-    gu_lines = gu_lines.astype(BF16)
+    gu_lines = a2a(gu_lines.astype(BF16), NATURAL)
+    *down, g_down_in = tiled_call(
+        down_kernel,
+        [shape(TOK, D, dtype=BF16)] * 4 + [shape(2048, 128, dtype=BF16)],
+        [act_a, act_b, d_small_down, mlp_set],
+        [
+            pl.BlockSpec((256, 512), lambda i: (0, i)),
+            pl.BlockSpec((256, 512), lambda i: (0, i)),
+            once(512, 128),
+            pl.BlockSpec((512, D), lambda i: (i, 2)),
+        ],
+        [whole_spec(TOK, D)] * 4 + [pl.BlockSpec((512, 128), lambda i: (i, 0))],
+        [pltpu.VMEM((512, D), F32)],
+        flops=2 * 512 * 2048 * D,
+        deps=[back_b, back[0], back[1]],
+        vmem=52,
+    )
     d_hidden, d_attn, d_small_gu, small_down = call(
         d_hidden_kernel,
         [
@@ -903,6 +966,7 @@
             shape(TOK, 128, dtype=BF16),
         ],
         [hidden, cot_own, gain_mlp, *back, mlp_set, pick_f],
+        deps=[down[0], gu_lines],
         specs=[None] * 7 + [block(D, 256, 24), None],
         vmem=52,
     )
@@ -924,36 +988,19 @@
         pack_kernel, [shape(16, TOK, 128, dtype=BF16)], [mine, other_core(theirs)], vmem=6
     )
 
-    down, g_down_in = tiled_call(
-        down_kernel,
-        [shape(512, D, dtype=BF16), shape(2048, 128, dtype=BF16)],
-        [after(act_a, send), act_b, d_small_down, mlp_set],
-        [
-            pl.BlockSpec((256, 512), lambda i: (0, i)),
-            pl.BlockSpec((256, 512), lambda i: (0, i)),
-            whole_spec(512, 128),
-            pl.BlockSpec((512, 2048), lambda i: (i, 2)),
-        ],
-        [whole_spec(512, D), pl.BlockSpec((512, 128), lambda i: (i, 0))],
-        [pltpu.VMEM((512, D), F32)],
-        flops=2 * 512 * 2048 * D,
-        vmem=52,
-    )
-    down = after(down, d_attn)
     down = [
-        along_x(down[:TOK], 3),
-        along_x(down[TOK : 2 * TOK], 1),
-        down[2 * TOK : 3 * TOK],
-        along_x(down[3 * TOK :], 2),
+        along_x(down[0], 3),
+        along_x(down[1], 1),
+        down[2],
+        along_x(down[3], 2),
     ]
     d_out = a2a(send, BLOCKS).reshape(GTOK, 128)
     (early,) = call(
         early_grads_kernel,
-        [shape(16, 640, 128, dtype=BF16)],
+        [shape(16, 384, 128, dtype=BF16)],
         [
-            gu_lines,
             g_down_in,
-            after(d_small_gu, send),
+            d_small_gu,
             normed_mlp,
             small_down,
             cot_own,
@@ -964,9 +1011,10 @@
             fold,
         ],
         scratch=[pltpu.VMEM((16, 384, 128), F32)],
+        deps=[d_out],
         vmem=28,
     )
-    early = a2a(after(early, d_out), NATURAL)
+    early = a2a(early, NATURAL)
     q_out, k_out, v_out = call(
         unpack_qkv_kernel,
         [shape(128, 1024, dtype=BF16), shape(128, 512, dtype=BF16), shape(128, 512, dtype=BF16)],
@@ -977,41 +1025,46 @@
     (dz,) = call(
         attend_back_kernel,
         [shape(GTOK, 256, dtype=BF16)],
-        [after(z, q_out), d_out, stat],
+        [z, d_out, stat],
+        deps=[q_out],
         scratch=[pltpu.VMEM((GTOK, HDIM), F32), pltpu.VMEM((GTOK, HDIM), F32)],
         flops=5 * 2 * 2 * 30 * CLEN * CLEN * HDIM * 4,
         vmem=24,
     )
-    parts = a2a(after(dz, down, early).reshape(16, TOK, 256), BLOCKS)
+    parts = a2a(dz.reshape(16, TOK, 256), BLOCKS)
+    plane, g_down_in = call(
+        sums_kernel,
+        [shape(8, 120, 128), shape(128, 128)],
+        [source_slot, gu_lines, early],
+        deps=[dz],
+        scratch=[pltpu.VMEM((512, 128), F32), pltpu.VMEM((256, 128), F32)],
+        specs=[SMEM, None, None],
+        vmem=14,
+    )
+    def in_chip(v):
+        v = v.reshape(4, 2, *v.shape[1:])
+
+        def to_chip(k):
+            return lax.dynamic_index_in_dim(v, (x + k) % 4, 0, keepdims=False)
+
+        by_chip = jnp.stack([to_chip(0)] + [along_x(to_chip(k), k) for k in (1, 2, 3)])
+        keep = lax.dynamic_index_in_dim(by_chip, c, 1, keepdims=False)
+        return keep, other_core(lax.dynamic_index_in_dim(by_chip, 1 - c, 1, keepdims=False))
+
+    keep, take = in_chip(plane)
     (output,) = call(
         output_kernel,
         [shape(TOK, D, dtype=BF16)],
-        [after(hidden, dz), *down, down_out, small_down],
+        [hidden, *down, down_out, small_down],
+        deps=[take],
         vmem=12,
     )
     output = swap_mid(output)
-    plane, g_down_in = call(
-        sums_kernel,
-        [shape(8, 120, 128), shape(128, 128)],
-        [after(source_slot, dz), early],
-        scratch=[pltpu.VMEM((512, 128), F32), pltpu.VMEM((256, 128), F32)],
-        specs=[SMEM, None],
-        vmem=12,
-    )
-    plane = plane.reshape(4, 2, 120, 128)
-
-    def to_chip(k):
-        return lax.dynamic_index_in_dim(plane, (x + k) % 4, 0, keepdims=False)
-
-    by_chip = jnp.stack([to_chip(0)] + [along_x(to_chip(k), k) for k in (1, 2, 3)])
-    keep = lax.dynamic_index_in_dim(by_chip, c, 1, keepdims=False)
-    take = other_core(lax.dynamic_index_in_dim(by_chip, 1 - c, 1, keepdims=False))
-
-    parts = after(parts, keep, take)
     d_joint, mine_small, their_small = call(
         qkv_back_kernel,
         [shape(256, 1536, dtype=BF16), shape(TOK, 384), shape(TOK, 384, dtype=BF16)],
         [parts, q_out, k_out, v_out, cq, sq, ckv, skv],
+        deps=[take],
         vmem=12,
     )
     d_small_qkv, late = call(
@@ -1024,7 +1077,8 @@
     mine, theirs = call(
         d_normed_kernel,
         [shape(TOK, D), shape(TOK, D, dtype=BF16)],
-        [after(d_joint, late), t2],
+        [d_joint, t2],
+        deps=[late],
         specs=[None, w_spec],
         flops=2 * 256 * D * 1536,
         vmem=20,
@@ -1047,9 +1101,8 @@
         vmem=8,
     )
     both = keep + take
-    gu = [
-        lax.dynamic_index_in_dim(both[:, :32], (x - k) % 4, 0, keepdims=False) for k in range(4)
-    ]
+    gu = both[:, :32]
+    gu = [lax.dynamic_index_in_dim(gu, (x - k) % 4, 0, keepdims=False) for k in range(4)]
     gu = jnp.stack(gu).reshape(4, 2, 2, 2, 4, 128).transpose(1, 3, 2, 4, 0, 5)
     grad_gu_out = gu.reshape(1, 2 * UNITS)
     half = g_down_in.reshape(2, 64, 128)

time: 499 us -> 467 us (0.936)
  waiting for transfers between devices: 170 us -> 126 us
  local copies, waits for them, and re-layouts: 57.3 us -> 67.9 us
    ppermute x27, waiting for transfers between devices: 65.6 us -> 39.8 us  [along_x(): return lax.ppermute(v, 'x', [(i, (i + k) % 4) for i in range(4)])]
    unnamed x211 -> x241, local copies, waits for them, and re-layouts: 28.4 us -> 44.8 us
    all_to_all x9 -> x10, waiting for transfers between devices: 81.2 us -> 65 us  [a2a(): return lax.all_to_all(v, axes, 0, 0, tiled=True)]
    all_gather x1, waiting for transfers between devices: 16 us -> 5.86 us  [local(): x_plane = lax.all_gather(x_own, PLANE, axis=0, tiled=True)]
    all_gather x3, waiting for transfers between devices: 0.02 us -> 8.93 us  [the longest x1 7.92 us: local(): lax.all_gather(gate(chip, x_plane, in_plane), NATURAL, axis=0, tiled=True)]
    all_to_all x9 -> x10, starting transfers between devices: 48.4 us -> 55.8 us  [a2a(): return lax.all_to_all(v, axes, 0, 0, tiled=True)]
    slice x5 -> x1, local copies, waits for them, and re-layouts: 6.91 us -> 0.01 us  [local(): gu = both[:, :32]]
    pallas_call x23 -> x29, Pallas kernels: 116 us -> 120 us  [the longest x25 64.8 us: call(): pl.pallas_call(ignoring(kernel, len(args), len(deps)), name=kernel.__name...]
  transfers between devices with their start and end apart: 51 -> 52, of which waited for: 22 -> 24; matrix products, arithmetic and copies ran while one was open for 12% -> 11% of each run, Pallas kernels for 23% -> 26%
where the time goes in v2:
time: 467 us; the launch traced here: 459 us
  waiting for transfers between devices  126 us (27%)
  Pallas kernels  120 us (26%)
  starting transfers between devices  102 us (22%)
  local copies, waits for them, and re-layouts  67.9 us (15%)
  other arithmetic  27.5 us (6%)
  between operations  16.6 us (4%)
    all_to_all x10, waiting for transfers between devices, a2a(): return lax.all_to_all(v, axes, 0, 0, tiled=True)  65 us
    pallas_call x25, Pallas kernels, call(): pl.pallas_call(ignoring(kernel, len(args), len(deps)), name=kernel.__name...  64.8 us
    all_to_all x10, starting transfers between devices, a2a(): return lax.all_to_all(v, axes, 0, 0, tiled=True)  55.8 us
    pallas_call x4, Pallas kernels, tiled_call(): pl.pallas_call(ignoring(kernel, len(args), len(deps)), name=kernel.__name...  55.5 us
    unnamed x241, local copies, waits for them, and re-layouts  44.8 us
    ppermute x27, waiting for transfers between devices, along_x(): return lax.ppermute(v, 'x', [(i, (i + k) % 4) for i in range(4)])  39.8 us
    ppermute x27, starting transfers between devices, along_x(): return lax.ppermute(v, 'x', [(i, (i + k) % 4) for i in range(4)])  30.9 us
    ppermute x11, starting transfers between devices, other_core(): return lax.ppermute(v, 'c', [(0, 1), (1, 0)])  14.7 us
  transfers between devices with their start and end apart: 52, of which 24 were waited for; matrix products, arithmetic and copies ran while one was open for 11% of the time, Pallas kernels for 26%

profile of v2, /device:TPU:1, one launch (start us, length us, event | category | flops | bytes accessed | tf_op | source)
XLA Modules:
  0.0 459.3 jit_solution(17850722585669939725)
XLA Ops:
  11.6 5.8 %all-to-all-start = ((bf16[8,16,896]{2,1,0:T(8,128)(2,1)}), bf16[8,16,896]{2,1,0:T(8,128)(2,1)S(1)}, u32[]{:S(2)}, u32[]{:S(2)}) async-start(bf16[8,16,896]{2,1,0:T(8,128)(2,1)} %bitcast.8), calls=%async_computation | async-start | bytes 458752 | tf_op jit(solution)/shard_map/all_to_all | solution.py:55
  20.6 3.0 all-to-all-done.refs_2_
  23.6 2.4 broadcast_in_dim.96
  26.0 7.8 %all-to-all-start.1 = ((bf16[16,128,896]{2,1,0:T(8,128)(2,1)}), bf16[16,128,896]{2,1,0:T(8,128)(2,1)}, u32[]{:S(2)}, u32[]{:S(2)}) async-start(bf16[16,128,896]{2,1,0:T(8,128)(2,1)} %broadcast_in_dim.96), calls=%async_computation.1 | async-start | bytes 7340032 | tf_op jit(solution)/shard_map/all_to_all | solution.py:55
  40.2 5.9 %all-gather.5.cloned.1.call-done.refs_1_ = bf16[1024,2048]{1,0:T(8,128)(2,1)} async-done(((bf16[128,2048]{1,0:T(8,128)(2,1)}), bf16[1024,2048]{1,0:T(8,128)(2,1)}) %all-gather.5.cloned.1.call-update) | async-done | bytes 4194320 | tf_op jit(solution)/shard_map/all_gather | solution.py:640
  55.6 4.1 collective-permute-done
  62.4 25.6 %all-to-all-done.1 = bf16[16,128,896]{2,1,0:T(8,128)(2,1)} async-done(((bf16[16,128,896]{2,1,0:T(8,128)(2,1)}), bf16[16,128,896]{2,1,0:T(8,128)(2,1)}, u32[]{:S(2)}, u32[]{:S(2)}) %all-to-all-start.1) | async-done | bytes 3670048 | tf_op jit(solution)/shard_map/all_to_all | solution.py:55
  90.2 10.5 %qkv_kernel.1 = (bf16[16,128,256]{2,1,0:T(8,128)(2,1)}, bf16[128,2048]{1,0:T(8,128)(2,1)S(1)}, bf16[256,384]{1,0:T(8,128)(2,1)S(1)}, f32[1,2048]{1,0:T(1,128)S(1)}, f32[1,2048]{1,0:T(1,128)S(1)}) custom-call(s32[2]{0:T(128)S(1)} %pad_add_fusion.refs_0_, bf16[1024,2048]{1,0:T(8,128)(2,1)S(1)} %copy-done.5, bf16[2048,896]{1,0:T(8,128)(2,1)} %bitcast.10.refs_2_.refs_6_, ...), custom_call_target="tpu_custom_call" | custom-call | flops 3221225472 | bytes 9924616 | tf_op jit(solution)/shard_map/qkv_kernel/pallas_call | solution.py:92
  102.2 7.9 %all-gather.7.cloned.1.call-done.refs_3_.refs_1_ = bf16[512,1280]{1,0:T(8,128)(2,1)} async-done(((bf16[32,1280]{1,0:T(8,128)(2,1)}), bf16[512,1280]{1,0:T(8,128)(2,1)}) %all-gather.7.cloned.1.call-update) | async-done | bytes 1310736 | tf_op jit(solution)/shard_map/all_gather | solution.py:694
  112.7 4.2 all-to-all-start.2
  122.2 8.4 %all-to-all-done.2 = bf16[16,128,256]{2,1,0:T(8,128)(2,1)} async-done(((bf16[16,128,256]{2,1,0:T(8,128)(2,1)}), bf16[16,128,256]{2,1,0:T(8,128)(2,1)}, u32[]{:S(2)}, u32[]{:S(2)}) %all-to-all-start.2) | async-done | bytes 1048608 | tf_op jit(solution)/shard_map/all_to_all | solution.py:55
  130.6 4.5 all-to-all-start.3
  139.9 19.6 %collective-permute-done.30 = bf16[32,1664]{1,0:T(8,128)(2,1)S(1)} collective-permute-done((bf16[32,1664]{1,0:T(8,128)(2,1)S(1)}, bf16[32,1664]{1,0:T(8,128)(2,1)S(1)}, u32[]{:S(2)}, u32[]{:S(2)}) %collective-permute-start.30) | collective-permute-done | bytes 106528 | tf_op jit(solution)/shard_map/ppermute | solution.py:63
  166.4 6.4 %attend_kernel.1 = (bf16[2048,128]{1,0:T(8,128)(2,1)S(1)}, f32[8,512]{1,0:T(8,128)S(1)}) custom-call(bf16[2048,256]{1,0:T(8,128)(2,1)S(1)} %bitcast.288, bf16[512,1280]{1,0:T(8,128)(2,1)S(1)} %collective-permute-done.5.refs_1_.refs_4_, bf16[512,1280]{1,0:T(8,128)(2,1)} %collective-permute-done.6.refs_2_.refs_5_), custom_call_target="tpu_custom_call" | custom-call | flops 4026531840 | bytes 1589248 | tf_op jit(solution)/shard_map/attend_kernel/pallas_call | solution.py:92
  174.2 4.6 %all-to-all-start.4 = ((bf16[16,128,128]{2,1,0:T(8,128)(2,1)}), bf16[16,128,128]{2,1,0:T(8,128)(2,1)S(1)}, u32[]{:S(2)}, u32[]{:S(2)}) async-start(bf16[16,128,128]{2,1,0:T(8,128)(2,1)} %bitcast.290), calls=%async_computation.4 | async-start | bytes 1048576 | tf_op jit(solution)/shard_map/all_to_all | solution.py:55
  186.0 8.7 %all-to-all-done.4.refs_1_ = bf16[16,128,128]{2,1,0:T(8,128)(2,1)S(1)} async-done(((bf16[16,128,128]{2,1,0:T(8,128)(2,1)}), bf16[16,128,128]{2,1,0:T(8,128)(2,1)S(1)}, u32[]{:S(2)}, u32[]{:S(2)}) %all-to-all-start.4) | async-done | bytes 524320 | tf_op jit(solution)/shard_map/all_to_all | solution.py:55
  194.8 5.5 %collective-permute-start.7 = (bf16[16,128,128]{2,1,0:T(8,128)(2,1)S(1)}, bf16[16,128,128]{2,1,0:T(8,128)(2,1)S(1)}, u32[]{:S(2)}, u32[]{:S(2)}) collective-permute-start(bf16[16,128,128]{2,1,0:T(8,128)(2,1)S(1)} %all-to-all-done.4.refs_1_), channel_id=1, source_target_pairs={{0,1},{1,0},{2,3},{3,2},{4,5},{5,4},{6,7},{7,6},{8,9},{9,8},{10,11... | collective-permute-start | bytes 1572872 | tf_op jit(solution)/shard_map/ppermute | solution.py:59
  202.4 2.7 collective-permute-start.14
  208.9 4.5 project_kernel.1
  222.6 3.0 collective-permute-start.16
  234.4 11.5 %d_act_kernel.1 = (f32[512,2048]{1,0:T(8,128)}, bf16[512,128]{1,0:T(8,128)(2,1)S(1)}) custom-call(bf16[512,2048]{1,0:T(8,128)(2,1)} %copy-done.23, bf16[2048,512]{1,0:T(8,128)(2,1)} %copy-done.24, bf16[128,2048]{1,0:T(8,128)(2,1)S(1)} %get-tuple-element.80.refs_2_.refs_5_, ...), custom_call_target="tpu_custom_call" | custom-call | flops 4294967296 | bytes 12713984 | tf_op jit(solution)/shard_map/d_act_kernel/pallas_call | solution.py:111
  246.0 2.2 copy-done
  249.5 2.4 collective-permute-start.18
  253.0 17.7 %feed_kernel.2 = (bf16[256,2048]{1,0:T(8,128)(2,1)}, bf16[128,2432]{1,0:T(8,128)(2,1)}, bf16[128,2432]{1,0:T(8,128)(2,1)}, f32[16,16,8,128]{3,2,1,0:T(8,128)}, f32[16,16,8,128]{3,2,1,0:T(8,128)}) custom-call(bf16[128,2048]{1,0:T(8,128)(2,1)} %collective-permute-done.15.refs_0_, bf16[128,2048]{1,0:T(8,128)(2,1)} %collective-permute-done.16.refs_1_, ...), custom_call_target="tpu_custom_call" | custom-call | flops 8589934592 | bytes 21168128 | tf_op jit(solution)/shard_map/feed_kernel/pallas_call | solution.py:111
  270.7 2.7 collective-permute-start.19
  273.7 16.9 %feed_kernel.3 = (bf16[256,2048]{1,0:T(8,128)(2,1)}, bf16[128,2432]{1,0:T(8,128)(2,1)S(1)}, bf16[128,2432]{1,0:T(8,128)(2,1)}, f32[16,16,8,128]{3,2,1,0:T(8,128)}, f32[16,16,8,128]{3,2,1,0:T(8,128)}) custom-call(bf16[128,2048]{1,0:T(8,128)(2,1)S(1)} %copy-done.15, bf16[128,2048]{1,0:T(8,128)(2,1)S(1)} %pad_maximum_fusion.5.refs_1_, ...), custom_call_target="tpu_custom_call" | custom-call | flops 8589934592 | bytes 21168128 | tf_op jit(solution)/shard_map/feed_kernel/pallas_call | solution.py:111
  291.4 2.7 fusion.1
  294.2 4.2 all-to-all-start.5
  299.7 9.4 %down_kernel.1 = (bf16[128,2048]{1,0:T(8,128)(2,1)}, bf16[128,2048]{1,0:T(8,128)(2,1)S(1)}, bf16[128,2048]{1,0:T(8,128)(2,1)S(1)}, bf16[128,2048]{1,0:T(8,128)(2,1)}, bf16[2048,128]{1,0:T(8,128)(2,1)}) custom-call(bf16[256,2048]{1,0:T(8,128)(2,1)} %get-tuple-element.83.refs_0_, bf16[256,2048]{1,0:T(8,128)(2,1)} %get-tuple-element.88.refs_1_, ...), custom_call_target="tpu_custom_call" | custom-call | flops 4294967296 | bytes 11010048 | tf_op jit(solution)/shard_map/down_kernel/pallas_call | solution.py:111
  310.7 3.7 collective-permute-done.24.refs_6_
  315.4 4.9 %d_hidden_kernel.1 = (f32[128,2048]{1,0:T(8,128)}, bf16[128,2048]{1,0:T(8,128)(2,1)S(1)}, bf16[128,256]{1,0:T(8,128)(2,1)S(1)}, bf16[128,128]{1,0:T(8,128)(2,1)S(1)}) custom-call(f32[128,2048]{1,0:T(8,128)} %copy-done.16, bf16[128,2048]{1,0:T(8,128)(2,1)S(1)} %pad_maximum_fusion.4.refs_0_.refs_1_.refs_4_, f32[1,2048]{1,0:T(1,128)S(1)} %get-tuple-element.75.refs_4_.refs_2_, ...), custom_call_target="tpu_custom_call" | custom-call | bytes 34078720 | tf_op jit(solution)/shard_map/d_hidden_kernel/pallas_call | solution.py:92
  320.9 2.4 collective-permute-start.25
  325.9 2.2 project_back_kernel.1
  331.7 6.4 %all-to-all-start.6 = ((bf16[16,128,128]{2,1,0:T(8,128)(2,1)}), bf16[16,128,128]{2,1,0:T(8,128)(2,1)S(1)}, u32[]{:S(2)}, u32[]{:S(2)}) async-start(bf16[16,128,128]{2,1,0:T(8,128)(2,1)} %pack_kernel.1), calls=%async_computation.6 | async-start | bytes 1048576 | tf_op jit(solution)/shard_map/all_to_all | solution.py:55
  338.3 10.9 %all-to-all-done.6 = bf16[16,128,128]{2,1,0:T(8,128)(2,1)S(1)} async-done(((bf16[16,128,128]{2,1,0:T(8,128)(2,1)}), bf16[16,128,128]{2,1,0:T(8,128)(2,1)S(1)}, u32[]{:S(2)}, u32[]{:S(2)}) %all-to-all-start.6) | async-done | bytes 524320 | tf_op jit(solution)/shard_map/all_to_all | solution.py:55
  354.3 3.8 all-to-all-start.7
  361.5 2.6 collective-permute-start.21
  365.6 13.3 %attend_back_kernel.1.refs_3_ = bf16[2048,256]{1,0:T(8,128)(2,1)S(1)} custom-call(bf16[2048,256]{1,0:T(8,128)(2,1)S(1)} %bitcast.289, bf16[2048,128]{1,0:T(8,128)(2,1)S(1)} %bitcast.286, f32[8,512]{1,0:T(8,128)S(1)} %copy-done.68, bf16[128,1024]{1,0:T(8,128)(2,1)S(1)} %get-tuple-element.113.refs_3_.refs_1_), custom_call_target="tpu_custom_call" | custom-call | flops 10066329600 | bytes 2637824 | tf_op jit(solution)/shard_map/attend_back_kernel/pallas_call | solution.py:92
  380.5 6.8 %all-to-all-start.8 = ((bf16[16,128,256]{2,1,0:T(8,128)(2,1)}), bf16[16,128,256]{2,1,0:T(8,128)(2,1)}, u32[]{:S(2)}, u32[]{:S(2)}) async-start(bf16[16,128,256]{2,1,0:T(8,128)(2,1)} %bitcast.284), calls=%async_computation.8 | async-start | bytes 2097152 | tf_op jit(solution)/shard_map/all_to_all | solution.py:55
  389.7 2.4 collective-permute-start.37
  392.1 3.0 collective-permute-start.33
  395.8 4.5 collective-permute-done.33
  401.4 2.7 collective-permute-done.31
  414.9 2.9 copy-done.11
  417.8 2.6 d_normed_kernel.1
  421.5 7.6 %all-to-all-start.9 = ((bf16[128,16,256]{2,1,0:T(8,128)(2,1)}), bf16[128,16,256]{2,1,0:T(8,128)(2,1)S(1)}, u32[]{:S(2)}, u32[]{:S(2)}) async-start(bf16[128,16,256]{2,1,0:T(8,128)(2,1)} %bitcast.67), calls=%async_computation.9 | async-start | bytes 2097152 | tf_op jit(solution)/shard_map/all_to_all | solution.py:55
  436.7 2.5 last_kernel.1
  440.1 8.4 %all-to-all-done.9.refs_1_ = bf16[128,16,256]{2,1,0:T(8,128)(2,1)S(1)} async-done(((bf16[128,16,256]{2,1,0:T(8,128)(2,1)}), bf16[128,16,256]{2,1,0:T(8,128)(2,1)S(1)}, u32[]{:S(2)}, u32[]{:S(2)}) %all-to-all-start.9) | async-done | bytes 1048608 | tf_op jit(solution)/shard_map/all_to_all | solution.py:55
  (524 shorter events, 133.8 us)
Async XLA Ops:
  7.2 38.9 %all-gather.5.cloned.1.call-start = ((), (), s32[]{:S(2)}) async-start(), calls=%async_computation.10 | async-start | bytes 4718592 | tf_op jit(solution)/shard_map/all_gather | solution.py:640
  11.6 12.0 %all-to-all-start = ((bf16[8,16,896]{2,1,0:T(8,128)(2,1)}), bf16[8,16,896]{2,1,0:T(8,128)(2,1)S(1)}, u32[]{:S(2)}, u32[]{:S(2)}) async-start(bf16[8,16,896]{2,1,0:T(8,128)(2,1)} %bitcast.8), calls=%async_computation | async-start | bytes 458752 | tf_op jit(solution)/shard_map/all_to_all | solution.py:55
  17.7 2.9 collective-permute-start.4
  26.0 62.0 %all-to-all-start.1 = ((bf16[16,128,896]{2,1,0:T(8,128)(2,1)}), bf16[16,128,896]{2,1,0:T(8,128)(2,1)}, u32[]{:S(2)}, u32[]{:S(2)}) async-start(bf16[16,128,896]{2,1,0:T(8,128)(2,1)} %broadcast_in_dim.96), calls=%async_computation.1 | async-start | bytes 7340032 | tf_op jit(solution)/shard_map/all_to_all | solution.py:55
  33.8 76.3 %all-gather.7.cloned.1.call-start = ((), (), s32[]{:S(2)}) async-start(), calls=%async_computation.11 | async-start | bytes 1392640 | tf_op jit(solution)/shard_map/all_gather | solution.py:694
  48.4 5.4 %collective-permute-start.2 = (bf16[16,4736]{1,0:T(8,128)(2,1)S(1)}, bf16[16,4736]{1,0:T(8,128)(2,1)S(1)}, u32[]{:S(2)}, u32[]{:S(2)}) collective-permute-start(bf16[16,4736]{1,0:T(8,128)(2,1)S(1)} %get-tuple-element.150), channel_id=1, source_target_pairs={{0,6},{2,0},{4,2},{6,4},{1,7},{3,1},{5,3},{7,5},{8,14},{10,8},{12,... | collective-permute-start | bytes 454664 | tf_op jit(solution)/shard_map/ppermute | solution.py:63
  49.1 6.6 %collective-permute-start.1 = (bf16[16,4736]{1,0:T(8,128)(2,1)S(1)}, bf16[16,4736]{1,0:T(8,128)(2,1)S(1)}, u32[]{:S(2)}, u32[]{:S(2)}) collective-permute-start(bf16[16,4736]{1,0:T(8,128)(2,1)S(1)} %get-tuple-element.151), channel_id=1, source_target_pairs={{0,4},{2,6},{4,0},{6,2},{1,5},{3,7},{5,1},{7,3},{8,12},{10,14},{12... | collective-permute-start | bytes 454664 | tf_op jit(solution)/shard_map/ppermute | solution.py:63
  50.4 9.3 %collective-permute-start = (bf16[16,4736]{1,0:T(8,128)(2,1)S(1)}, bf16[16,4736]{1,0:T(8,128)(2,1)S(1)}, u32[]{:S(2)}, u32[]{:S(2)}) collective-permute-start(bf16[16,4736]{1,0:T(8,128)(2,1)S(1)} %get-tuple-element.152), channel_id=1, source_target_pairs={{0,2},{2,4},{4,6},{6,0},{1,3},{3,5},{5,7},{7,1},{8,10},{10,12},{12... | collective-permute-start | bytes 454664 | tf_op jit(solution)/shard_map/ppermute | solution.py:63
  53.7 176.9 %all-gather.9.cloned.1.call-start = ((), (), s32[]{:S(2)}) async-start(), calls=%async_computation.12 | async-start | bytes 29196288 | tf_op jit(solution)/shard_map/all_gather | solution.py:788
  112.7 17.9 %all-to-all-start.2 = ((bf16[16,128,256]{2,1,0:T(8,128)(2,1)}), bf16[16,128,256]{2,1,0:T(8,128)(2,1)}, u32[]{:S(2)}, u32[]{:S(2)}) async-start(bf16[16,128,256]{2,1,0:T(8,128)(2,1)} %get-tuple-element.71.refs_2_), calls=%async_computation.2 | async-start | bytes 2097152 | tf_op jit(solution)/shard_map/all_to_all | solution.py:55
  117.7 18.3 %collective-permute-start.27 = (bf16[16,1664]{1,0:T(8,128)(2,1)}, bf16[16,1664]{1,0:T(8,128)(2,1)}, u32[]{:S(2)}, u32[]{:S(2)}) collective-permute-start(bf16[16,1664]{1,0:T(8,128)(2,1)} %get-tuple-element.184), channel_id=1, source_target_pairs={{0,1},{1,0},{2,3},{3,2},{4,5},{5,4},{6,7},{7,6},{8,9},{9,8},{10,11... | collective-permute-start | bytes 159752 | tf_op jit(solution)/shard_map/ppermute | solution.py:59
  119.2 43.4 %collective-permute-start.5 = (bf16[512,1280]{1,0:T(8,128)(2,1)}, bf16[512,1280]{1,0:T(8,128)(2,1)S(1)}, u32[]{:S(2)}, u32[]{:S(2)}) collective-permute-start(bf16[512,1280]{1,0:T(8,128)(2,1)} %all-gather.7.cloned.1.call-done.refs_3_.refs_1_), channel_id=1, source_target_pairs={{0,2},{2,4},{4,6},{6,0},{1,3},{3,5},{5,7},{7,1},{8,10},{10,12},{12... | collective-permute-start | bytes 3932168 | tf_op jit(solution)/shard_map/ppermute | solution.py:63
  120.9 45.4 %collective-permute-start.6 = (bf16[512,1280]{1,0:T(8,128)(2,1)}, bf16[512,1280]{1,0:T(8,128)(2,1)}, u32[]{:S(2)}, u32[]{:S(2)}) collective-permute-start(bf16[512,1280]{1,0:T(8,128)(2,1)} %all-gather.7.cloned.1.call-done.refs_3_.refs_1_), channel_id=1, source_target_pairs={{0,6},{2,0},{4,2},{6,4},{1,7},{3,1},{5,3},{7,5},{8,14},{10,8},{12,... | collective-permute-start | bytes 3932168 | tf_op jit(solution)/shard_map/ppermute | solution.py:63
  130.6 35.7 %all-to-all-start.3 = ((bf16[16,128,256]{2,1,0:T(8,128)(2,1)}), bf16[16,128,256]{2,1,0:T(8,128)(2,1)S(1)}, u32[]{:S(2)}, u32[]{:S(2)}) async-start(bf16[16,128,256]{2,1,0:T(8,128)(2,1)} %all-to-all-done.2), calls=%async_computation.3 | async-start | bytes 2097152 | tf_op jit(solution)/shard_map/all_to_all | solution.py:55
  136.8 22.6 %collective-permute-start.30 = (bf16[32,1664]{1,0:T(8,128)(2,1)S(1)}, bf16[32,1664]{1,0:T(8,128)(2,1)S(1)}, u32[]{:S(2)}, u32[]{:S(2)}) collective-permute-start(bf16[32,1664]{1,0:T(8,128)(2,1)S(1)} %maximum_select_fusion.2), channel_id=1, source_target_pairs={{0,6},{2,0},{4,2},{6,4},{1,7},{3,1},{5,3},{7,5},{8,14},{10,8},{12,... | collective-permute-start | bytes 319496 | tf_op jit(solution)/shard_map/ppermute | solution.py:63
  137.8 22.8 %collective-permute-start.29 = (bf16[32,1664]{1,0:T(8,128)(2,1)S(1)}, bf16[32,1664]{1,0:T(8,128)(2,1)S(1)}, u32[]{:S(2)}, u32[]{:S(2)}) collective-permute-start(bf16[32,1664]{1,0:T(8,128)(2,1)S(1)} %maximum_select_fusion.2), channel_id=1, source_target_pairs={{0,4},{2,6},{4,0},{6,2},{1,5},{3,7},{5,1},{7,3},{8,12},{10,14},{12... | collective-permute-start | bytes 319496 | tf_op jit(solution)/shard_map/ppermute | solution.py:63
  139.0 22.7 %collective-permute-start.28 = (bf16[32,1664]{1,0:T(8,128)(2,1)S(1)}, bf16[32,1664]{1,0:T(8,128)(2,1)S(1)}, u32[]{:S(2)}, u32[]{:S(2)}) collective-permute-start(bf16[32,1664]{1,0:T(8,128)(2,1)S(1)} %maximum_select_fusion.2), channel_id=1, source_target_pairs={{0,2},{2,4},{4,6},{6,0},{1,3},{3,5},{5,7},{7,1},{8,10},{10,12},{12... | collective-permute-start | bytes 319496 | tf_op jit(solution)/shard_map/ppermute | solution.py:63
  163.5 36.8 %collective-permute-start.11 = (bf16[128,2048]{1,0:T(8,128)(2,1)}, bf16[128,2048]{1,0:T(8,128)(2,1)}, u32[]{:S(2)}, u32[]{:S(2)}) collective-permute-start(bf16[128,2048]{1,0:T(8,128)(2,1)} %copy.171), channel_id=1, source_target_pairs={{0,2},{2,4},{4,6},{6,0},{1,3},{3,5},{5,7},{7,1},{8,10},{10,12},{12... | collective-permute-start | bytes 1572872 | tf_op jit(solution)/shard_map/ppermute | solution.py:63
  165.0 36.4 %collective-permute-start.12 = (bf16[128,2048]{1,0:T(8,128)(2,1)}, bf16[128,2048]{1,0:T(8,128)(2,1)}, u32[]{:S(2)}, u32[]{:S(2)}) collective-permute-start(bf16[128,2048]{1,0:T(8,128)(2,1)} %copy.171), channel_id=1, source_target_pairs={{0,6},{2,0},{4,2},{6,4},{1,7},{3,1},{5,3},{7,5},{8,14},{10,8},{12,... | collective-permute-start | bytes 1572872 | tf_op jit(solution)/shard_map/ppermute | solution.py:63
  174.2 20.6 %all-to-all-start.4 = ((bf16[16,128,128]{2,1,0:T(8,128)(2,1)}), bf16[16,128,128]{2,1,0:T(8,128)(2,1)S(1)}, u32[]{:S(2)}, u32[]{:S(2)}) async-start(bf16[16,128,128]{2,1,0:T(8,128)(2,1)} %bitcast.290), calls=%async_computation.4 | async-start | bytes 1048576 | tf_op jit(solution)/shard_map/all_to_all | solution.py:55
  178.8 179.9 %all-gather.11.cloned.1.call-start = ((), (), s32[]{:S(2)}) async-start(), calls=%async_computation.13 | async-start | bytes 7241728 | tf_op jit(solution)/shard_map/all_gather | solution.py:901
  183.6 23.9 %collective-permute-start.9 = (bf16[256,1280]{1,0:T(8,128)(2,1)}, bf16[256,1280]{1,0:T(8,128)(2,1)}, u32[]{:S(2)}, u32[]{:S(2)}) collective-permute-start(bf16[256,1280]{1,0:T(8,128)(2,1)} %slice.591), channel_id=1, source_target_pairs={{0,6},{2,0},{4,2},{6,4},{1,7},{3,1},{5,3},{7,5},{8,14},{10,8},{12,... | collective-permute-start | bytes 1966088 | tf_op jit(solution)/shard_map/ppermute | solution.py:63
  185.4 22.1 %collective-permute-start.8 = (bf16[256,1280]{1,0:T(8,128)(2,1)}, bf16[256,1280]{1,0:T(8,128)(2,1)}, u32[]{:S(2)}, u32[]{:S(2)}) collective-permute-start(bf16[256,1280]{1,0:T(8,128)(2,1)} %slice.590), channel_id=1, source_target_pairs={{0,2},{2,4},{4,6},{6,0},{1,3},{3,5},{5,7},{7,1},{8,10},{10,12},{12... | collective-permute-start | bytes 1966088 | tf_op jit(solution)/shard_map/ppermute | solution.py:63
  194.8 14.1 %collective-permute-start.7 = (bf16[16,128,128]{2,1,0:T(8,128)(2,1)S(1)}, bf16[16,128,128]{2,1,0:T(8,128)(2,1)S(1)}, u32[]{:S(2)}, u32[]{:S(2)}) collective-permute-start(bf16[16,128,128]{2,1,0:T(8,128)(2,1)S(1)} %all-to-all-done.4.refs_1_), channel_id=1, source_target_pairs={{0,1},{1,0},{2,3},{3,2},{4,5},{5,4},{6,7},{7,6},{8,9},{9,8},{10,11... | collective-permute-start | bytes 1572872 | tf_op jit(solution)/shard_map/ppermute | solution.py:59
  201.3 13.5 %collective-permute-start.13 = (bf16[64,2048]{1,0:T(8,128)(2,1)S(1)}, bf16[64,2048]{1,0:T(8,128)(2,1)S(1)}, u32[]{:S(2)}, u32[]{:S(2)}) collective-permute-start(bf16[64,2048]{1,0:T(8,128)(2,1)S(1)} %slice.596), channel_id=1, source_target_pairs={{0,2},{2,4},{4,6},{6,0},{1,3},{3,5},{5,7},{7,1},{8,10},{10,12},{12... | collective-permute-start | bytes 786440 | tf_op jit(solution)/shard_map/ppermute | solution.py:63
  202.4 12.5 %collective-permute-start.14 = (bf16[64,2048]{1,0:T(8,128)(2,1)S(1)}, bf16[64,2048]{1,0:T(8,128)(2,1)S(1)}, u32[]{:S(2)}, u32[]{:S(2)}) collective-permute-start(bf16[64,2048]{1,0:T(8,128)(2,1)S(1)} %slice.597), channel_id=1, source_target_pairs={{0,6},{2,0},{4,2},{6,4},{1,7},{3,1},{5,3},{7,5},{8,14},{10,8},{12,... | collective-permute-start | bytes 786440 | tf_op jit(solution)/shard_map/ppermute | solution.py:63
  222.5 23.5 %collective-permute-start.15 = (bf16[128,2048]{1,0:T(8,128)(2,1)}, bf16[128,2048]{1,0:T(8,128)(2,1)}, u32[]{:S(2)}, u32[]{:S(2)}) collective-permute-start(bf16[128,2048]{1,0:T(8,128)(2,1)} %copy-done.14), channel_id=1, source_target_pairs={{0,2},{2,4},{4,6},{6,0},{1,3},{3,5},{5,7},{7,1},{8,10},{10,12},{12... | collective-permute-start | bytes 1572872 | tf_op jit(solution)/shard_map/ppermute | solution.py:63
  222.6 23.4 %collective-permute-start.16 = (bf16[128,2048]{1,0:T(8,128)(2,1)}, bf16[128,2048]{1,0:T(8,128)(2,1)}, u32[]{:S(2)}, u32[]{:S(2)}) collective-permute-start(bf16[128,2048]{1,0:T(8,128)(2,1)} %copy-done.14), channel_id=1, source_target_pairs={{0,6},{2,0},{4,2},{6,4},{1,7},{3,1},{5,3},{7,5},{8,14},{10,8},{12,... | collective-permute-start | bytes 1572872 | tf_op jit(solution)/shard_map/ppermute | solution.py:63
  249.5 24.2 %collective-permute-start.18 = (bf16[64,2048]{1,0:T(8,128)(2,1)S(1)}, bf16[64,2048]{1,0:T(8,128)(2,1)S(1)}, u32[]{:S(2)}, u32[]{:S(2)}) collective-permute-start(bf16[64,2048]{1,0:T(8,128)(2,1)S(1)} %get-tuple-element.85), channel_id=1, source_target_pairs={{0,6},{2,0},{4,2},{6,4},{1,7},{3,1},{5,3},{7,5},{8,14},{10,8},{12,... | collective-permute-start | bytes 786440 | tf_op jit(solution)/shard_map/ppermute | solution.py:63
  251.9 21.7 %collective-permute-start.17 = (bf16[64,2048]{1,0:T(8,128)(2,1)S(1)}, bf16[64,2048]{1,0:T(8,128)(2,1)S(1)}, u32[]{:S(2)}, u32[]{:S(2)}) collective-permute-start(bf16[64,2048]{1,0:T(8,128)(2,1)S(1)} %get-tuple-element.84), channel_id=1, source_target_pairs={{0,2},{2,4},{4,6},{6,0},{1,3},{3,5},{5,7},{7,1},{8,10},{10,12},{12... | collective-permute-start | bytes 786440 | tf_op jit(solution)/shard_map/ppermute | solution.py:63
  270.7 29.0 %collective-permute-start.19 = (bf16[128,2432]{1,0:T(8,128)(2,1)}, bf16[128,2432]{1,0:T(8,128)(2,1)}, u32[]{:S(2)}, u32[]{:S(2)}) collective-permute-start(bf16[128,2432]{1,0:T(8,128)(2,1)} %get-tuple-element.91), channel_id=1, source_target_pairs={{0,6},{2,0},{4,2},{6,4},{1,7},{3,1},{5,3},{7,5},{8,14},{10,8},{12,... | collective-permute-start | bytes 1867784 | tf_op jit(solution)/shard_map/ppermute | solution.py:63
  273.5 26.2 %collective-permute-start.20 = (bf16[128,2432]{1,0:T(8,128)(2,1)}, bf16[128,2432]{1,0:T(8,128)(2,1)}, u32[]{:S(2)}, u32[]{:S(2)}) collective-permute-start(bf16[128,2432]{1,0:T(8,128)(2,1)} %get-tuple-element.92), channel_id=1, source_target_pairs={{0,2},{2,4},{4,6},{6,0},{1,3},{3,5},{5,7},{7,1},{8,10},{10,12},{12... | collective-permute-start | bytes 1867784 | tf_op jit(solution)/shard_map/ppermute | solution.py:63
  294.2 20.2 %all-to-all-start.5 = ((bf16[16,256,128]{2,1,0:T(8,128)(2,1)}), bf16[16,256,128]{2,1,0:T(8,128)(2,1)S(1)}, u32[]{:S(2)}, u32[]{:S(2)}) async-start(bf16[16,256,128]{2,1,0:T(8,128)(2,1)} %fusion.1), calls=%async_computation.5 | async-start | bytes 2097152 | tf_op jit(solution)/shard_map/all_to_all | solution.py:55
  298.3 16.1 %collective-permute-start.24 = (bf16[128,2432]{1,0:T(8,128)(2,1)}, bf16[128,2432]{1,0:T(8,128)(2,1)}, u32[]{:S(2)}, u32[]{:S(2)}) collective-permute-start(bf16[128,2432]{1,0:T(8,128)(2,1)} %get-tuple-element.97), channel_id=1, source_target_pairs={{0,4},{2,6},{4,0},{6,2},{1,5},{3,7},{5,1},{7,3},{8,12},{10,14},{12... | collective-permute-start | bytes 1867784 | tf_op jit(solution)/shard_map/ppermute | solution.py:63
  320.9 4.0 collective-permute-start.25
  331.7 17.4 %all-to-all-start.6 = ((bf16[16,128,128]{2,1,0:T(8,128)(2,1)}), bf16[16,128,128]{2,1,0:T(8,128)(2,1)S(1)}, u32[]{:S(2)}, u32[]{:S(2)}) async-start(bf16[16,128,128]{2,1,0:T(8,128)(2,1)} %pack_kernel.1), calls=%async_computation.6 | async-start | bytes 1048576 | tf_op jit(solution)/shard_map/all_to_all | solution.py:55
  354.3 26.2 %all-to-all-start.7 = ((bf16[16,384,128]{2,1,0:T(8,128)(2,1)}), bf16[16,384,128]{2,1,0:T(8,128)(2,1)S(1)}, u32[]{:S(2)}, u32[]{:S(2)}) async-start(bf16[16,384,128]{2,1,0:T(8,128)(2,1)} %early_grads_kernel.1), calls=%async_computation.7 | async-start | bytes 3145728 | tf_op jit(solution)/shard_map/all_to_all | solution.py:55
  361.5 70.6 %collective-permute-start.21 = (bf16[128,2048]{1,0:T(8,128)(2,1)}, bf16[128,2048]{1,0:T(8,128)(2,1)}, u32[]{:S(2)}, u32[]{:S(2)}) collective-permute-start(bf16[128,2048]{1,0:T(8,128)(2,1)} %get-tuple-element.93.refs_9_), channel_id=1, source_target_pairs={{0,6},{2,0},{4,2},{6,4},{1,7},{3,1},{5,3},{7,5},{8,14},{10,8},{12,... | collective-permute-start | bytes 1572872 | tf_op jit(solution)/shard_map/ppermute | solution.py:63
  364.1 67.9 %collective-permute-start.22 = (bf16[128,2048]{1,0:T(8,128)(2,1)}, bf16[128,2048]{1,0:T(8,128)(2,1)}, u32[]{:S(2)}, u32[]{:S(2)}) collective-permute-start(bf16[128,2048]{1,0:T(8,128)(2,1)} %copy-done.66), channel_id=1, source_target_pairs={{0,2},{2,4},{4,6},{6,0},{1,3},{3,5},{5,7},{7,1},{8,10},{10,12},{12... | collective-permute-start | bytes 1572872 | tf_op jit(solution)/shard_map/ppermute | solution.py:63
  380.5 26.6 %all-to-all-start.8 = ((bf16[16,128,256]{2,1,0:T(8,128)(2,1)}), bf16[16,128,256]{2,1,0:T(8,128)(2,1)}, u32[]{:S(2)}, u32[]{:S(2)}) async-start(bf16[16,128,256]{2,1,0:T(8,128)(2,1)} %bitcast.284), calls=%async_computation.8 | async-start | bytes 2097152 | tf_op jit(solution)/shard_map/all_to_all | solution.py:55
  389.7 5.4 %collective-permute-start.37 = (f32[64,128]{1,0:T(8,128)S(1)}, f32[64,128]{1,0:T(8,128)S(1)}, u32[]{:S(2)}, u32[]{:S(2)}) collective-permute-start(f32[64,128]{1,0:T(8,128)S(1)} %dynamic-slice_bitcast_fusion.16), channel_id=1, source_target_pairs={{0,1},{1,0},{2,3},{3,2},{4,5},{5,4},{6,7},{7,6},{8,9},{9,8},{10,11... | collective-permute-start | bytes 98312 | tf_op jit(solution)/shard_map/ppermute | solution.py:59
  392.1 8.2 %collective-permute-start.33 = (f32[2,120,128]{2,1,0:T(8,128)S(1)}, f32[2,120,128]{2,1,0:T(8,128)S(1)}, u32[]{:S(2)}, u32[]{:S(2)}) collective-permute-start(f32[2,120,128]{2,1,0:T(8,128)S(1)} %get-tuple-element.170), channel_id=1, source_target_pairs={{0,6},{2,0},{4,2},{6,4},{1,7},{3,1},{5,3},{7,5},{8,14},{10,8},{12,... | collective-permute-start | bytes 368648 | tf_op jit(solution)/shard_map/ppermute | solution.py:63
  395.1 6.3 %collective-permute-start.32 = (f32[2,120,128]{2,1,0:T(8,128)S(1)}, f32[2,120,128]{2,1,0:T(8,128)S(1)}, u32[]{:S(2)}, u32[]{:S(2)}) collective-permute-start(f32[2,120,128]{2,1,0:T(8,128)S(1)} %get-tuple-element.171), channel_id=1, source_target_pairs={{0,4},{2,6},{4,0},{6,2},{1,5},{3,7},{5,1},{7,3},{8,12},{10,14},{12... | collective-permute-start | bytes 368648 | tf_op jit(solution)/shard_map/ppermute | solution.py:63
  395.1 8.9 %collective-permute-start.31 = (f32[2,120,128]{2,1,0:T(8,128)S(1)}, f32[2,120,128]{2,1,0:T(8,128)S(1)}, u32[]{:S(2)}, u32[]{:S(2)}) collective-permute-start(f32[2,120,128]{2,1,0:T(8,128)S(1)} %get-tuple-element.172), channel_id=1, source_target_pairs={{0,2},{2,4},{4,6},{6,0},{1,3},{3,5},{5,7},{7,1},{8,10},{10,12},{12... | collective-permute-start | bytes 368648 | tf_op jit(solution)/shard_map/ppermute | solution.py:63
  400.3 31.7 %collective-permute-start.23 = (bf16[128,2048]{1,0:T(8,128)(2,1)}, bf16[128,2048]{1,0:T(8,128)(2,1)}, u32[]{:S(2)}, u32[]{:S(2)}) collective-permute-start(bf16[128,2048]{1,0:T(8,128)(2,1)} %get-tuple-element.96), channel_id=1, source_target_pairs={{0,4},{2,6},{4,0},{6,2},{1,5},{3,7},{5,1},{7,3},{8,12},{10,14},{12... | collective-permute-start | bytes 1572872 | tf_op jit(solution)/shard_map/ppermute | solution.py:63
  409.3 3.7 collective-permute-start.35
  421.4 14.5 %collective-permute-start.36 = (bf16[128,2048]{1,0:T(8,128)(2,1)}, bf16[128,2048]{1,0:T(8,128)(2,1)}, u32[]{:S(2)}, u32[]{:S(2)}) collective-permute-start(bf16[128,2048]{1,0:T(8,128)(2,1)} %get-tuple-element.126), channel_id=1, source_target_pairs={{0,1},{1,0},{2,3},{3,2},{4,5},{5,4},{6,7},{7,6},{8,9},{9,8},{10,11... | collective-permute-start | bytes 1572872 | tf_op jit(solution)/shard_map/ppermute | solution.py:59
  421.5 27.0 %all-to-all-start.9 = ((bf16[128,16,256]{2,1,0:T(8,128)(2,1)}), bf16[128,16,256]{2,1,0:T(8,128)(2,1)S(1)}, u32[]{:S(2)}, u32[]{:S(2)}) async-start(bf16[128,16,256]{2,1,0:T(8,128)(2,1)} %bitcast.67), calls=%async_computation.9 | async-start | bytes 2097152 | tf_op jit(solution)/shard_map/all_to_all | solution.py:55
  (113 other events, 899.1 us)
Sparse Core Ops, SparseCore 0:
  10.3 35.6 all-gather.4
  53.9 56.2 all-gather.6
  112.6 117.9 all-gather.8
  232.6 62.5 all-gather.10

commit v3 on v2

--- a/solution.py
+++ b/solution.py
@@ -380,7 +380,7 @@
 
 def feed_kernel(
     n_one, n_two, d_act, pick, w_gate, w_up, o_gate, o_up, a_in, a_down, g_gate0, g_up0,
-    act, back, back1, g_gate, g_up, total, small, n,
+    act, back, back1, g_gate, g_up, total, small, turned, n,
 ):
     step = pl.program_id(0)
 
@@ -390,7 +390,9 @@
         n[TOK:, :] = n_two[...]
         s = mm(n[...], a_in[...]).astype(BF16)
         p = pick[...]
-        small[...] = s * jnp.concatenate([p, p], axis=1)
+        s = s * jnp.concatenate([p, p], axis=1)
+        small[...] = s
+        turned[...] = s.T
         total[...] = jnp.zeros_like(total)
 
     x = n[...]
@@ -406,12 +408,10 @@
     total[D : D + 128, :] += mm_nt(o_gate[...], dg)
     total[D + 128 : D + 256, :] += mm_nt(o_up[...], du)
     total[D + 256 :, :] += mm_nt(a_down[...].T, act[...])
-    for t in range(4):
-        cols = slice(t * 128, (t + 1) * 128)
-        g = mm_tn(small[:, :128], dg[:, cols]).reshape(16, 8, 128)
-        g_gate[:, t] = g_gate0[:, t] + g
-        g = mm_tn(small[:, 128:], du[:, cols]).reshape(16, 8, 128)
-        g_up[:, t] = g_up0[:, t] + g
+    for g0, out, d, rows in ((g_gate0, g_gate, dg, 0), (g_up0, g_up, du, 128)):
+        g = mm(turned[rows : rows + 128, :], d)
+        for t in range(4):
+            out[:, t] = g0[:, t] + g[:, t * 128 : (t + 1) * 128].reshape(16, 8, 128)
 
     @pl.when(step == pl.num_programs(0) - 1)
     def _():
@@ -929,7 +929,7 @@
             [pl.BlockSpec((256, 512), lambda i: (0, i))]
             + [whole_spec(TOK, D + 384)] * 2
             + [lines] * 2,
-            [pltpu.VMEM((D + 384, 256), F32), pltpu.VMEM((256, 256), BF16), pltpu.VMEM((256, D), BF16)],
+            [pltpu.VMEM((D + 384, 256), F32), pltpu.VMEM((256, 256), BF16), pltpu.VMEM((256, 256), BF16), pltpu.VMEM((256, D), BF16)],
             flops=2 * 256 * 4096 * D * 2,
             vmem=52,
         )

time: 467 us -> 467 us (level)
  no operation moved by 1% of the time
where the time goes in v3:
time: 467 us; the launch traced here: 459 us
  waiting for transfers between devices  125 us (27%)
  Pallas kernels  120 us (26%)
  starting transfers between devices  101 us (22%)
  local copies, waits for them, and re-layouts  67.9 us (15%)
  other arithmetic  27.5 us (6%)
  between operations  16.6 us (4%)
    all_to_all x10, waiting for transfers between devices, a2a(): return lax.all_to_all(v, axes, 0, 0, tiled=True)  65 us
    pallas_call x25, Pallas kernels, call(): pl.pallas_call(ignoring(kernel, len(args), len(deps)), name=kernel.__name...  64.8 us
    all_to_all x10, starting transfers between devices, a2a(): return lax.all_to_all(v, axes, 0, 0, tiled=True)  55.7 us
    pallas_call x4, Pallas kernels, tiled_call(): pl.pallas_call(ignoring(kernel, len(args), len(deps)), name=kernel.__name...  55.3 us
    unnamed x241, local copies, waits for them, and re-layouts  44.8 us
    ppermute x27, waiting for transfers between devices, along_x(): return lax.ppermute(v, 'x', [(i, (i + k) % 4) for i in range(4)])  39.8 us
    ppermute x27, starting transfers between devices, along_x(): return lax.ppermute(v, 'x', [(i, (i + k) % 4) for i in range(4)])  30.9 us
    ppermute x11, starting transfers between devices, other_core(): return lax.ppermute(v, 'c', [(0, 1), (1, 0)])  14.7 us
  transfers between devices with their start and end apart: 52, of which 24 were waited for; matrix products, arithmetic and copies ran while one was open for 11% of the time, Pallas kernels for 26%

profile of v3, /device:TPU:1, one launch (start us, length us, event | category | flops | bytes accessed | tf_op | source)
XLA Modules:
  0.0 459.0 jit_solution(16361974531436624657)
XLA Ops:
  11.6 5.8 %all-to-all-start = ((bf16[8,16,896]{2,1,0:T(8,128)(2,1)}), bf16[8,16,896]{2,1,0:T(8,128)(2,1)S(1)}, u32[]{:S(2)}, u32[]{:S(2)}) async-start(bf16[8,16,896]{2,1,0:T(8,128)(2,1)} %bitcast.8), calls=%async_computation | async-start | bytes 458752 | tf_op jit(solution)/shard_map/all_to_all | solution.py:55
  20.6 3.0 all-to-all-done.refs_2_
  23.6 2.4 broadcast_in_dim.96
  26.0 7.8 %all-to-all-start.1 = ((bf16[16,128,896]{2,1,0:T(8,128)(2,1)}), bf16[16,128,896]{2,1,0:T(8,128)(2,1)}, u32[]{:S(2)}, u32[]{:S(2)}) async-start(bf16[16,128,896]{2,1,0:T(8,128)(2,1)} %broadcast_in_dim.96), calls=%async_computation.1 | async-start | bytes 7340032 | tf_op jit(solution)/shard_map/all_to_all | solution.py:55
  40.2 5.9 %all-gather.5.cloned.1.call-done.refs_1_ = bf16[1024,2048]{1,0:T(8,128)(2,1)} async-done(((bf16[128,2048]{1,0:T(8,128)(2,1)}), bf16[1024,2048]{1,0:T(8,128)(2,1)}) %all-gather.5.cloned.1.call-update) | async-done | bytes 4194320 | tf_op jit(solution)/shard_map/all_gather | solution.py:640
  55.6 4.1 collective-permute-done
  62.4 25.6 %all-to-all-done.1 = bf16[16,128,896]{2,1,0:T(8,128)(2,1)} async-done(((bf16[16,128,896]{2,1,0:T(8,128)(2,1)}), bf16[16,128,896]{2,1,0:T(8,128)(2,1)}, u32[]{:S(2)}, u32[]{:S(2)}) %all-to-all-start.1) | async-done | bytes 3670048 | tf_op jit(solution)/shard_map/all_to_all | solution.py:55
  90.2 10.5 %qkv_kernel.1 = (bf16[16,128,256]{2,1,0:T(8,128)(2,1)}, bf16[128,2048]{1,0:T(8,128)(2,1)S(1)}, bf16[256,384]{1,0:T(8,128)(2,1)S(1)}, f32[1,2048]{1,0:T(1,128)S(1)}, f32[1,2048]{1,0:T(1,128)S(1)}) custom-call(s32[2]{0:T(128)S(1)} %pad_add_fusion.refs_0_, bf16[1024,2048]{1,0:T(8,128)(2,1)S(1)} %copy-done.5, bf16[2048,896]{1,0:T(8,128)(2,1)} %bitcast.10.refs_2_.refs_6_, ...), custom_call_target="tpu_custom_call" | custom-call | flops 3221225472 | bytes 9924616 | tf_op jit(solution)/shard_map/qkv_kernel/pallas_call | solution.py:92
  102.2 7.9 %all-gather.7.cloned.1.call-done.refs_3_.refs_1_ = bf16[512,1280]{1,0:T(8,128)(2,1)} async-done(((bf16[32,1280]{1,0:T(8,128)(2,1)}), bf16[512,1280]{1,0:T(8,128)(2,1)}) %all-gather.7.cloned.1.call-update) | async-done | bytes 1310736 | tf_op jit(solution)/shard_map/all_gather | solution.py:694
  112.7 4.2 all-to-all-start.2
  122.2 8.4 %all-to-all-done.2 = bf16[16,128,256]{2,1,0:T(8,128)(2,1)} async-done(((bf16[16,128,256]{2,1,0:T(8,128)(2,1)}), bf16[16,128,256]{2,1,0:T(8,128)(2,1)}, u32[]{:S(2)}, u32[]{:S(2)}) %all-to-all-start.2) | async-done | bytes 1048608 | tf_op jit(solution)/shard_map/all_to_all | solution.py:55
  130.6 4.5 all-to-all-start.3
  139.9 19.6 %collective-permute-done.30 = bf16[32,1664]{1,0:T(8,128)(2,1)S(1)} collective-permute-done((bf16[32,1664]{1,0:T(8,128)(2,1)S(1)}, bf16[32,1664]{1,0:T(8,128)(2,1)S(1)}, u32[]{:S(2)}, u32[]{:S(2)}) %collective-permute-start.30) | collective-permute-done | bytes 106528 | tf_op jit(solution)/shard_map/ppermute | solution.py:63
  166.4 6.4 %attend_kernel.1 = (bf16[2048,128]{1,0:T(8,128)(2,1)S(1)}, f32[8,512]{1,0:T(8,128)S(1)}) custom-call(bf16[2048,256]{1,0:T(8,128)(2,1)S(1)} %bitcast.288, bf16[512,1280]{1,0:T(8,128)(2,1)S(1)} %collective-permute-done.5.refs_1_.refs_4_, bf16[512,1280]{1,0:T(8,128)(2,1)} %collective-permute-done.6.refs_2_.refs_5_), custom_call_target="tpu_custom_call" | custom-call | flops 4026531840 | bytes 1589248 | tf_op jit(solution)/shard_map/attend_kernel/pallas_call | solution.py:92
  174.2 4.6 %all-to-all-start.4 = ((bf16[16,128,128]{2,1,0:T(8,128)(2,1)}), bf16[16,128,128]{2,1,0:T(8,128)(2,1)S(1)}, u32[]{:S(2)}, u32[]{:S(2)}) async-start(bf16[16,128,128]{2,1,0:T(8,128)(2,1)} %bitcast.290), calls=%async_computation.4 | async-start | bytes 1048576 | tf_op jit(solution)/shard_map/all_to_all | solution.py:55
  186.0 8.7 %all-to-all-done.4.refs_1_ = bf16[16,128,128]{2,1,0:T(8,128)(2,1)S(1)} async-done(((bf16[16,128,128]{2,1,0:T(8,128)(2,1)}), bf16[16,128,128]{2,1,0:T(8,128)(2,1)S(1)}, u32[]{:S(2)}, u32[]{:S(2)}) %all-to-all-start.4) | async-done | bytes 524320 | tf_op jit(solution)/shard_map/all_to_all | solution.py:55
  194.8 5.5 %collective-permute-start.7 = (bf16[16,128,128]{2,1,0:T(8,128)(2,1)S(1)}, bf16[16,128,128]{2,1,0:T(8,128)(2,1)S(1)}, u32[]{:S(2)}, u32[]{:S(2)}) collective-permute-start(bf16[16,128,128]{2,1,0:T(8,128)(2,1)S(1)} %all-to-all-done.4.refs_1_), channel_id=1, source_target_pairs={{0,1},{1,0},{2,3},{3,2},{4,5},{5,4},{6,7},{7,6},{8,9},{9,8},{10,11... | collective-permute-start | bytes 1572872 | tf_op jit(solution)/shard_map/ppermute | solution.py:59
  202.4 2.7 collective-permute-start.14
  208.9 4.5 project_kernel.1
  222.6 3.0 collective-permute-start.16
  234.4 11.5 %d_act_kernel.1 = (f32[512,2048]{1,0:T(8,128)}, bf16[512,128]{1,0:T(8,128)(2,1)S(1)}) custom-call(bf16[512,2048]{1,0:T(8,128)(2,1)} %copy-done.23, bf16[2048,512]{1,0:T(8,128)(2,1)} %copy-done.24, bf16[128,2048]{1,0:T(8,128)(2,1)S(1)} %get-tuple-element.80.refs_2_.refs_5_, ...), custom_call_target="tpu_custom_call" | custom-call | flops 4294967296 | bytes 12713984 | tf_op jit(solution)/shard_map/d_act_kernel/pallas_call | solution.py:111
  246.0 2.2 copy-done
  249.5 2.4 collective-permute-start.18
  253.0 17.6 %feed_kernel.2 = (bf16[256,2048]{1,0:T(8,128)(2,1)}, bf16[128,2432]{1,0:T(8,128)(2,1)}, bf16[128,2432]{1,0:T(8,128)(2,1)}, f32[16,16,8,128]{3,2,1,0:T(8,128)}, f32[16,16,8,128]{3,2,1,0:T(8,128)}) custom-call(bf16[128,2048]{1,0:T(8,128)(2,1)} %collective-permute-done.15.refs_0_, bf16[128,2048]{1,0:T(8,128)(2,1)} %collective-permute-done.16.refs_1_, ...), custom_call_target="tpu_custom_call" | custom-call | flops 8589934592 | bytes 21168128 | tf_op jit(solution)/shard_map/feed_kernel/pallas_call | solution.py:111
  270.6 2.7 collective-permute-start.19
  273.6 16.8 %feed_kernel.3 = (bf16[256,2048]{1,0:T(8,128)(2,1)}, bf16[128,2432]{1,0:T(8,128)(2,1)S(1)}, bf16[128,2432]{1,0:T(8,128)(2,1)}, f32[16,16,8,128]{3,2,1,0:T(8,128)}, f32[16,16,8,128]{3,2,1,0:T(8,128)}) custom-call(bf16[128,2048]{1,0:T(8,128)(2,1)S(1)} %copy-done.15, bf16[128,2048]{1,0:T(8,128)(2,1)S(1)} %pad_maximum_fusion.5.refs_1_, ...), custom_call_target="tpu_custom_call" | custom-call | flops 8589934592 | bytes 21168128 | tf_op jit(solution)/shard_map/feed_kernel/pallas_call | solution.py:111
  291.3 2.7 fusion.1
  294.0 4.1 all-to-all-start.5
  299.5 9.4 %down_kernel.1 = (bf16[128,2048]{1,0:T(8,128)(2,1)}, bf16[128,2048]{1,0:T(8,128)(2,1)S(1)}, bf16[128,2048]{1,0:T(8,128)(2,1)S(1)}, bf16[128,2048]{1,0:T(8,128)(2,1)}, bf16[2048,128]{1,0:T(8,128)(2,1)}) custom-call(bf16[256,2048]{1,0:T(8,128)(2,1)} %get-tuple-element.83.refs_0_, bf16[256,2048]{1,0:T(8,128)(2,1)} %get-tuple-element.88.refs_1_, ...), custom_call_target="tpu_custom_call" | custom-call | flops 4294967296 | bytes 11010048 | tf_op jit(solution)/shard_map/down_kernel/pallas_call | solution.py:111
  310.4 3.7 collective-permute-done.24.refs_6_
  315.1 4.9 %d_hidden_kernel.1 = (f32[128,2048]{1,0:T(8,128)}, bf16[128,2048]{1,0:T(8,128)(2,1)S(1)}, bf16[128,256]{1,0:T(8,128)(2,1)S(1)}, bf16[128,128]{1,0:T(8,128)(2,1)S(1)}) custom-call(f32[128,2048]{1,0:T(8,128)} %copy-done.16, bf16[128,2048]{1,0:T(8,128)(2,1)S(1)} %pad_maximum_fusion.4.refs_0_.refs_1_.refs_4_, f32[1,2048]{1,0:T(1,128)S(1)} %get-tuple-element.75.refs_4_.refs_2_, ...), custom_call_target="tpu_custom_call" | custom-call | bytes 34078720 | tf_op jit(solution)/shard_map/d_hidden_kernel/pallas_call | solution.py:92
  320.6 2.4 collective-permute-start.25
  325.7 2.2 project_back_kernel.1
  331.5 6.4 %all-to-all-start.6 = ((bf16[16,128,128]{2,1,0:T(8,128)(2,1)}), bf16[16,128,128]{2,1,0:T(8,128)(2,1)S(1)}, u32[]{:S(2)}, u32[]{:S(2)}) async-start(bf16[16,128,128]{2,1,0:T(8,128)(2,1)} %pack_kernel.1), calls=%async_computation.6 | async-start | bytes 1048576 | tf_op jit(solution)/shard_map/all_to_all | solution.py:55
  338.1 10.9 %all-to-all-done.6 = bf16[16,128,128]{2,1,0:T(8,128)(2,1)S(1)} async-done(((bf16[16,128,128]{2,1,0:T(8,128)(2,1)}), bf16[16,128,128]{2,1,0:T(8,128)(2,1)S(1)}, u32[]{:S(2)}, u32[]{:S(2)}) %all-to-all-start.6) | async-done | bytes 524320 | tf_op jit(solution)/shard_map/all_to_all | solution.py:55
  354.1 3.8 all-to-all-start.7
  361.2 2.7 collective-permute-start.21
  365.3 13.3 %attend_back_kernel.1.refs_3_ = bf16[2048,256]{1,0:T(8,128)(2,1)S(1)} custom-call(bf16[2048,256]{1,0:T(8,128)(2,1)S(1)} %bitcast.289, bf16[2048,128]{1,0:T(8,128)(2,1)S(1)} %bitcast.286, f32[8,512]{1,0:T(8,128)S(1)} %copy-done.68, bf16[128,1024]{1,0:T(8,128)(2,1)S(1)} %get-tuple-element.113.refs_3_.refs_1_), custom_call_target="tpu_custom_call" | custom-call | flops 10066329600 | bytes 2637824 | tf_op jit(solution)/shard_map/attend_back_kernel/pallas_call | solution.py:92
  380.3 6.8 %all-to-all-start.8 = ((bf16[16,128,256]{2,1,0:T(8,128)(2,1)}), bf16[16,128,256]{2,1,0:T(8,128)(2,1)}, u32[]{:S(2)}, u32[]{:S(2)}) async-start(bf16[16,128,256]{2,1,0:T(8,128)(2,1)} %bitcast.284), calls=%async_computation.8 | async-start | bytes 2097152 | tf_op jit(solution)/shard_map/all_to_all | solution.py:55
  389.4 2.4 collective-permute-start.37
  391.9 3.0 collective-permute-start.33
  395.6 4.5 collective-permute-done.33
  401.1 2.7 collective-permute-done.31
  414.6 2.9 copy-done.11
  417.6 2.6 d_normed_kernel.1
  421.3 7.6 %all-to-all-start.9 = ((bf16[128,16,256]{2,1,0:T(8,128)(2,1)}), bf16[128,16,256]{2,1,0:T(8,128)(2,1)S(1)}, u32[]{:S(2)}, u32[]{:S(2)}) async-start(bf16[128,16,256]{2,1,0:T(8,128)(2,1)} %bitcast.67), calls=%async_computation.9 | async-start | bytes 2097152 | tf_op jit(solution)/shard_map/all_to_all | solution.py:55
  436.5 2.5 last_kernel.1
  439.9 8.4 %all-to-all-done.9.refs_1_ = bf16[128,16,256]{2,1,0:T(8,128)(2,1)S(1)} async-done(((bf16[128,16,256]{2,1,0:T(8,128)(2,1)}), bf16[128,16,256]{2,1,0:T(8,128)(2,1)S(1)}, u32[]{:S(2)}, u32[]{:S(2)}) %all-to-all-start.9) | async-done | bytes 1048608 | tf_op jit(solution)/shard_map/all_to_all | solution.py:55
  (524 shorter events, 133.8 us)
Async XLA Ops:
  7.2 38.9 %all-gather.5.cloned.1.call-start = ((), (), s32[]{:S(2)}) async-start(), calls=%async_computation.10 | async-start | bytes 4718592 | tf_op jit(solution)/shard_map/all_gather | solution.py:640
  11.6 12.0 %all-to-all-start = ((bf16[8,16,896]{2,1,0:T(8,128)(2,1)}), bf16[8,16,896]{2,1,0:T(8,128)(2,1)S(1)}, u32[]{:S(2)}, u32[]{:S(2)}) async-start(bf16[8,16,896]{2,1,0:T(8,128)(2,1)} %bitcast.8), calls=%async_computation | async-start | bytes 458752 | tf_op jit(solution)/shard_map/all_to_all | solution.py:55
  17.7 2.9 collective-permute-start.4
  26.0 62.0 %all-to-all-start.1 = ((bf16[16,128,896]{2,1,0:T(8,128)(2,1)}), bf16[16,128,896]{2,1,0:T(8,128)(2,1)}, u32[]{:S(2)}, u32[]{:S(2)}) async-start(bf16[16,128,896]{2,1,0:T(8,128)(2,1)} %broadcast_in_dim.96), calls=%async_computation.1 | async-start | bytes 7340032 | tf_op jit(solution)/shard_map/all_to_all | solution.py:55
  33.8 76.3 %all-gather.7.cloned.1.call-start = ((), (), s32[]{:S(2)}) async-start(), calls=%async_computation.11 | async-start | bytes 1392640 | tf_op jit(solution)/shard_map/all_gather | solution.py:694
  48.4 5.4 %collective-permute-start.2 = (bf16[16,4736]{1,0:T(8,128)(2,1)S(1)}, bf16[16,4736]{1,0:T(8,128)(2,1)S(1)}, u32[]{:S(2)}, u32[]{:S(2)}) collective-permute-start(bf16[16,4736]{1,0:T(8,128)(2,1)S(1)} %get-tuple-element.150), channel_id=1, source_target_pairs={{0,6},{2,0},{4,2},{6,4},{1,7},{3,1},{5,3},{7,5},{8,14},{10,8},{12,... | collective-permute-start | bytes 454664 | tf_op jit(solution)/shard_map/ppermute | solution.py:63
  49.1 6.6 %collective-permute-start.1 = (bf16[16,4736]{1,0:T(8,128)(2,1)S(1)}, bf16[16,4736]{1,0:T(8,128)(2,1)S(1)}, u32[]{:S(2)}, u32[]{:S(2)}) collective-permute-start(bf16[16,4736]{1,0:T(8,128)(2,1)S(1)} %get-tuple-element.151), channel_id=1, source_target_pairs={{0,4},{2,6},{4,0},{6,2},{1,5},{3,7},{5,1},{7,3},{8,12},{10,14},{12... | collective-permute-start | bytes 454664 | tf_op jit(solution)/shard_map/ppermute | solution.py:63
  50.4 9.3 %collective-permute-start = (bf16[16,4736]{1,0:T(8,128)(2,1)S(1)}, bf16[16,4736]{1,0:T(8,128)(2,1)S(1)}, u32[]{:S(2)}, u32[]{:S(2)}) collective-permute-start(bf16[16,4736]{1,0:T(8,128)(2,1)S(1)} %get-tuple-element.152), channel_id=1, source_target_pairs={{0,2},{2,4},{4,6},{6,0},{1,3},{3,5},{5,7},{7,1},{8,10},{10,12},{12... | collective-permute-start | bytes 454664 | tf_op jit(solution)/shard_map/ppermute | solution.py:63
  53.7 176.9 %all-gather.9.cloned.1.call-start = ((), (), s32[]{:S(2)}) async-start(), calls=%async_computation.12 | async-start | bytes 29196288 | tf_op jit(solution)/shard_map/all_gather | solution.py:788
  112.7 17.9 %all-to-all-start.2 = ((bf16[16,128,256]{2,1,0:T(8,128)(2,1)}), bf16[16,128,256]{2,1,0:T(8,128)(2,1)}, u32[]{:S(2)}, u32[]{:S(2)}) async-start(bf16[16,128,256]{2,1,0:T(8,128)(2,1)} %get-tuple-element.71.refs_2_), calls=%async_computation.2 | async-start | bytes 2097152 | tf_op jit(solution)/shard_map/all_to_all | solution.py:55
  117.7 18.3 %collective-permute-start.27 = (bf16[16,1664]{1,0:T(8,128)(2,1)}, bf16[16,1664]{1,0:T(8,128)(2,1)}, u32[]{:S(2)}, u32[]{:S(2)}) collective-permute-start(bf16[16,1664]{1,0:T(8,128)(2,1)} %get-tuple-element.184), channel_id=1, source_target_pairs={{0,1},{1,0},{2,3},{3,2},{4,5},{5,4},{6,7},{7,6},{8,9},{9,8},{10,11... | collective-permute-start | bytes 159752 | tf_op jit(solution)/shard_map/ppermute | solution.py:59
  119.2 43.4 %collective-permute-start.5 = (bf16[512,1280]{1,0:T(8,128)(2,1)}, bf16[512,1280]{1,0:T(8,128)(2,1)S(1)}, u32[]{:S(2)}, u32[]{:S(2)}) collective-permute-start(bf16[512,1280]{1,0:T(8,128)(2,1)} %all-gather.7.cloned.1.call-done.refs_3_.refs_1_), channel_id=1, source_target_pairs={{0,2},{2,4},{4,6},{6,0},{1,3},{3,5},{5,7},{7,1},{8,10},{10,12},{12... | collective-permute-start | bytes 3932168 | tf_op jit(solution)/shard_map/ppermute | solution.py:63
  120.9 45.4 %collective-permute-start.6 = (bf16[512,1280]{1,0:T(8,128)(2,1)}, bf16[512,1280]{1,0:T(8,128)(2,1)}, u32[]{:S(2)}, u32[]{:S(2)}) collective-permute-start(bf16[512,1280]{1,0:T(8,128)(2,1)} %all-gather.7.cloned.1.call-done.refs_3_.refs_1_), channel_id=1, source_target_pairs={{0,6},{2,0},{4,2},{6,4},{1,7},{3,1},{5,3},{7,5},{8,14},{10,8},{12,... | collective-permute-start | bytes 3932168 | tf_op jit(solution)/shard_map/ppermute | solution.py:63
  130.6 35.7 %all-to-all-start.3 = ((bf16[16,128,256]{2,1,0:T(8,128)(2,1)}), bf16[16,128,256]{2,1,0:T(8,128)(2,1)S(1)}, u32[]{:S(2)}, u32[]{:S(2)}) async-start(bf16[16,128,256]{2,1,0:T(8,128)(2,1)} %all-to-all-done.2), calls=%async_computation.3 | async-start | bytes 2097152 | tf_op jit(solution)/shard_map/all_to_all | solution.py:55
  136.8 22.6 %collective-permute-start.30 = (bf16[32,1664]{1,0:T(8,128)(2,1)S(1)}, bf16[32,1664]{1,0:T(8,128)(2,1)S(1)}, u32[]{:S(2)}, u32[]{:S(2)}) collective-permute-start(bf16[32,1664]{1,0:T(8,128)(2,1)S(1)} %maximum_select_fusion.2), channel_id=1, source_target_pairs={{0,6},{2,0},{4,2},{6,4},{1,7},{3,1},{5,3},{7,5},{8,14},{10,8},{12,... | collective-permute-start | bytes 319496 | tf_op jit(solution)/shard_map/ppermute | solution.py:63
  137.8 22.8 %collective-permute-start.29 = (bf16[32,1664]{1,0:T(8,128)(2,1)S(1)}, bf16[32,1664]{1,0:T(8,128)(2,1)S(1)}, u32[]{:S(2)}, u32[]{:S(2)}) collective-permute-start(bf16[32,1664]{1,0:T(8,128)(2,1)S(1)} %maximum_select_fusion.2), channel_id=1, source_target_pairs={{0,4},{2,6},{4,0},{6,2},{1,5},{3,7},{5,1},{7,3},{8,12},{10,14},{12... | collective-permute-start | bytes 319496 | tf_op jit(solution)/shard_map/ppermute | solution.py:63
  139.0 22.7 %collective-permute-start.28 = (bf16[32,1664]{1,0:T(8,128)(2,1)S(1)}, bf16[32,1664]{1,0:T(8,128)(2,1)S(1)}, u32[]{:S(2)}, u32[]{:S(2)}) collective-permute-start(bf16[32,1664]{1,0:T(8,128)(2,1)S(1)} %maximum_select_fusion.2), channel_id=1, source_target_pairs={{0,2},{2,4},{4,6},{6,0},{1,3},{3,5},{5,7},{7,1},{8,10},{10,12},{12... | collective-permute-start | bytes 319496 | tf_op jit(solution)/shard_map/ppermute | solution.py:63
  163.5 36.8 %collective-permute-start.11 = (bf16[128,2048]{1,0:T(8,128)(2,1)}, bf16[128,2048]{1,0:T(8,128)(2,1)}, u32[]{:S(2)}, u32[]{:S(2)}) collective-permute-start(bf16[128,2048]{1,0:T(8,128)(2,1)} %copy.171), channel_id=1, source_target_pairs={{0,2},{2,4},{4,6},{6,0},{1,3},{3,5},{5,7},{7,1},{8,10},{10,12},{12... | collective-permute-start | bytes 1572872 | tf_op jit(solution)/shard_map/ppermute | solution.py:63
  165.0 36.4 %collective-permute-start.12 = (bf16[128,2048]{1,0:T(8,128)(2,1)}, bf16[128,2048]{1,0:T(8,128)(2,1)}, u32[]{:S(2)}, u32[]{:S(2)}) collective-permute-start(bf16[128,2048]{1,0:T(8,128)(2,1)} %copy.171), channel_id=1, source_target_pairs={{0,6},{2,0},{4,2},{6,4},{1,7},{3,1},{5,3},{7,5},{8,14},{10,8},{12,... | collective-permute-start | bytes 1572872 | tf_op jit(solution)/shard_map/ppermute | solution.py:63
  174.2 20.6 %all-to-all-start.4 = ((bf16[16,128,128]{2,1,0:T(8,128)(2,1)}), bf16[16,128,128]{2,1,0:T(8,128)(2,1)S(1)}, u32[]{:S(2)}, u32[]{:S(2)}) async-start(bf16[16,128,128]{2,1,0:T(8,128)(2,1)} %bitcast.290), calls=%async_computation.4 | async-start | bytes 1048576 | tf_op jit(solution)/shard_map/all_to_all | solution.py:55
  178.8 179.6 %all-gather.11.cloned.1.call-start = ((), (), s32[]{:S(2)}) async-start(), calls=%async_computation.13 | async-start | bytes 7241728 | tf_op jit(solution)/shard_map/all_gather | solution.py:901
  183.6 23.9 %collective-permute-start.9 = (bf16[256,1280]{1,0:T(8,128)(2,1)}, bf16[256,1280]{1,0:T(8,128)(2,1)}, u32[]{:S(2)}, u32[]{:S(2)}) collective-permute-start(bf16[256,1280]{1,0:T(8,128)(2,1)} %slice.591), channel_id=1, source_target_pairs={{0,6},{2,0},{4,2},{6,4},{1,7},{3,1},{5,3},{7,5},{8,14},{10,8},{12,... | collective-permute-start | bytes 1966088 | tf_op jit(solution)/shard_map/ppermute | solution.py:63
  185.4 22.1 %collective-permute-start.8 = (bf16[256,1280]{1,0:T(8,128)(2,1)}, bf16[256,1280]{1,0:T(8,128)(2,1)}, u32[]{:S(2)}, u32[]{:S(2)}) collective-permute-start(bf16[256,1280]{1,0:T(8,128)(2,1)} %slice.590), channel_id=1, source_target_pairs={{0,2},{2,4},{4,6},{6,0},{1,3},{3,5},{5,7},{7,1},{8,10},{10,12},{12... | collective-permute-start | bytes 1966088 | tf_op jit(solution)/shard_map/ppermute | solution.py:63
  194.8 14.1 %collective-permute-start.7 = (bf16[16,128,128]{2,1,0:T(8,128)(2,1)S(1)}, bf16[16,128,128]{2,1,0:T(8,128)(2,1)S(1)}, u32[]{:S(2)}, u32[]{:S(2)}) collective-permute-start(bf16[16,128,128]{2,1,0:T(8,128)(2,1)S(1)} %all-to-all-done.4.refs_1_), channel_id=1, source_target_pairs={{0,1},{1,0},{2,3},{3,2},{4,5},{5,4},{6,7},{7,6},{8,9},{9,8},{10,11... | collective-permute-start | bytes 1572872 | tf_op jit(solution)/shard_map/ppermute | solution.py:59
  201.3 13.5 %collective-permute-start.13 = (bf16[64,2048]{1,0:T(8,128)(2,1)S(1)}, bf16[64,2048]{1,0:T(8,128)(2,1)S(1)}, u32[]{:S(2)}, u32[]{:S(2)}) collective-permute-start(bf16[64,2048]{1,0:T(8,128)(2,1)S(1)} %slice.596), channel_id=1, source_target_pairs={{0,2},{2,4},{4,6},{6,0},{1,3},{3,5},{5,7},{7,1},{8,10},{10,12},{12... | collective-permute-start | bytes 786440 | tf_op jit(solution)/shard_map/ppermute | solution.py:63
  202.4 12.5 %collective-permute-start.14 = (bf16[64,2048]{1,0:T(8,128)(2,1)S(1)}, bf16[64,2048]{1,0:T(8,128)(2,1)S(1)}, u32[]{:S(2)}, u32[]{:S(2)}) collective-permute-start(bf16[64,2048]{1,0:T(8,128)(2,1)S(1)} %slice.597), channel_id=1, source_target_pairs={{0,6},{2,0},{4,2},{6,4},{1,7},{3,1},{5,3},{7,5},{8,14},{10,8},{12,... | collective-permute-start | bytes 786440 | tf_op jit(solution)/shard_map/ppermute | solution.py:63
  222.5 23.5 %collective-permute-start.15 = (bf16[128,2048]{1,0:T(8,128)(2,1)}, bf16[128,2048]{1,0:T(8,128)(2,1)}, u32[]{:S(2)}, u32[]{:S(2)}) collective-permute-start(bf16[128,2048]{1,0:T(8,128)(2,1)} %copy-done.14), channel_id=1, source_target_pairs={{0,2},{2,4},{4,6},{6,0},{1,3},{3,5},{5,7},{7,1},{8,10},{10,12},{12... | collective-permute-start | bytes 1572872 | tf_op jit(solution)/shard_map/ppermute | solution.py:63
  222.6 23.4 %collective-permute-start.16 = (bf16[128,2048]{1,0:T(8,128)(2,1)}, bf16[128,2048]{1,0:T(8,128)(2,1)}, u32[]{:S(2)}, u32[]{:S(2)}) collective-permute-start(bf16[128,2048]{1,0:T(8,128)(2,1)} %copy-done.14), channel_id=1, source_target_pairs={{0,6},{2,0},{4,2},{6,4},{1,7},{3,1},{5,3},{7,5},{8,14},{10,8},{12,... | collective-permute-start | bytes 1572872 | tf_op jit(solution)/shard_map/ppermute | solution.py:63
  249.5 24.1 %collective-permute-start.18 = (bf16[64,2048]{1,0:T(8,128)(2,1)S(1)}, bf16[64,2048]{1,0:T(8,128)(2,1)S(1)}, u32[]{:S(2)}, u32[]{:S(2)}) collective-permute-start(bf16[64,2048]{1,0:T(8,128)(2,1)S(1)} %get-tuple-element.85), channel_id=1, source_target_pairs={{0,6},{2,0},{4,2},{6,4},{1,7},{3,1},{5,3},{7,5},{8,14},{10,8},{12,... | collective-permute-start | bytes 786440 | tf_op jit(solution)/shard_map/ppermute | solution.py:63
  251.9 21.6 %collective-permute-start.17 = (bf16[64,2048]{1,0:T(8,128)(2,1)S(1)}, bf16[64,2048]{1,0:T(8,128)(2,1)S(1)}, u32[]{:S(2)}, u32[]{:S(2)}) collective-permute-start(bf16[64,2048]{1,0:T(8,128)(2,1)S(1)} %get-tuple-element.84), channel_id=1, source_target_pairs={{0,2},{2,4},{4,6},{6,0},{1,3},{3,5},{5,7},{7,1},{8,10},{10,12},{12... | collective-permute-start | bytes 786440 | tf_op jit(solution)/shard_map/ppermute | solution.py:63
  270.6 28.8 %collective-permute-start.19 = (bf16[128,2432]{1,0:T(8,128)(2,1)}, bf16[128,2432]{1,0:T(8,128)(2,1)}, u32[]{:S(2)}, u32[]{:S(2)}) collective-permute-start(bf16[128,2432]{1,0:T(8,128)(2,1)} %get-tuple-element.91), channel_id=1, source_target_pairs={{0,6},{2,0},{4,2},{6,4},{1,7},{3,1},{5,3},{7,5},{8,14},{10,8},{12,... | collective-permute-start | bytes 1867784 | tf_op jit(solution)/shard_map/ppermute | solution.py:63
  273.4 26.1 %collective-permute-start.20 = (bf16[128,2432]{1,0:T(8,128)(2,1)}, bf16[128,2432]{1,0:T(8,128)(2,1)}, u32[]{:S(2)}, u32[]{:S(2)}) collective-permute-start(bf16[128,2432]{1,0:T(8,128)(2,1)} %get-tuple-element.92), channel_id=1, source_target_pairs={{0,2},{2,4},{4,6},{6,0},{1,3},{3,5},{5,7},{7,1},{8,10},{10,12},{12... | collective-permute-start | bytes 1867784 | tf_op jit(solution)/shard_map/ppermute | solution.py:63
  294.0 20.1 %all-to-all-start.5 = ((bf16[16,256,128]{2,1,0:T(8,128)(2,1)}), bf16[16,256,128]{2,1,0:T(8,128)(2,1)S(1)}, u32[]{:S(2)}, u32[]{:S(2)}) async-start(bf16[16,256,128]{2,1,0:T(8,128)(2,1)} %fusion.1), calls=%async_computation.5 | async-start | bytes 2097152 | tf_op jit(solution)/shard_map/all_to_all | solution.py:55
  298.1 16.1 %collective-permute-start.24 = (bf16[128,2432]{1,0:T(8,128)(2,1)}, bf16[128,2432]{1,0:T(8,128)(2,1)}, u32[]{:S(2)}, u32[]{:S(2)}) collective-permute-start(bf16[128,2432]{1,0:T(8,128)(2,1)} %get-tuple-element.97), channel_id=1, source_target_pairs={{0,4},{2,6},{4,0},{6,2},{1,5},{3,7},{5,1},{7,3},{8,12},{10,14},{12... | collective-permute-start | bytes 1867784 | tf_op jit(solution)/shard_map/ppermute | solution.py:63
  320.6 4.0 collective-permute-start.25
  331.5 17.4 %all-to-all-start.6 = ((bf16[16,128,128]{2,1,0:T(8,128)(2,1)}), bf16[16,128,128]{2,1,0:T(8,128)(2,1)S(1)}, u32[]{:S(2)}, u32[]{:S(2)}) async-start(bf16[16,128,128]{2,1,0:T(8,128)(2,1)} %pack_kernel.1), calls=%async_computation.6 | async-start | bytes 1048576 | tf_op jit(solution)/shard_map/all_to_all | solution.py:55
  354.1 26.2 %all-to-all-start.7 = ((bf16[16,384,128]{2,1,0:T(8,128)(2,1)}), bf16[16,384,128]{2,1,0:T(8,128)(2,1)S(1)}, u32[]{:S(2)}, u32[]{:S(2)}) async-start(bf16[16,384,128]{2,1,0:T(8,128)(2,1)} %early_grads_kernel.1), calls=%async_computation.7 | async-start | bytes 3145728 | tf_op jit(solution)/shard_map/all_to_all | solution.py:55
  361.2 70.6 %collective-permute-start.21 = (bf16[128,2048]{1,0:T(8,128)(2,1)}, bf16[128,2048]{1,0:T(8,128)(2,1)}, u32[]{:S(2)}, u32[]{:S(2)}) collective-permute-start(bf16[128,2048]{1,0:T(8,128)(2,1)} %get-tuple-element.93.refs_9_), channel_id=1, source_target_pairs={{0,6},{2,0},{4,2},{6,4},{1,7},{3,1},{5,3},{7,5},{8,14},{10,8},{12,... | collective-permute-start | bytes 1572872 | tf_op jit(solution)/shard_map/ppermute | solution.py:63
  363.9 67.9 %collective-permute-start.22 = (bf16[128,2048]{1,0:T(8,128)(2,1)}, bf16[128,2048]{1,0:T(8,128)(2,1)}, u32[]{:S(2)}, u32[]{:S(2)}) collective-permute-start(bf16[128,2048]{1,0:T(8,128)(2,1)} %copy-done.66), channel_id=1, source_target_pairs={{0,2},{2,4},{4,6},{6,0},{1,3},{3,5},{5,7},{7,1},{8,10},{10,12},{12... | collective-permute-start | bytes 1572872 | tf_op jit(solution)/shard_map/ppermute | solution.py:63
  380.3 26.6 %all-to-all-start.8 = ((bf16[16,128,256]{2,1,0:T(8,128)(2,1)}), bf16[16,128,256]{2,1,0:T(8,128)(2,1)}, u32[]{:S(2)}, u32[]{:S(2)}) async-start(bf16[16,128,256]{2,1,0:T(8,128)(2,1)} %bitcast.284), calls=%async_computation.8 | async-start | bytes 2097152 | tf_op jit(solution)/shard_map/all_to_all | solution.py:55
  389.4 5.5 %collective-permute-start.37 = (f32[64,128]{1,0:T(8,128)S(1)}, f32[64,128]{1,0:T(8,128)S(1)}, u32[]{:S(2)}, u32[]{:S(2)}) collective-permute-start(f32[64,128]{1,0:T(8,128)S(1)} %dynamic-slice_bitcast_fusion.16), channel_id=1, source_target_pairs={{0,1},{1,0},{2,3},{3,2},{4,5},{5,4},{6,7},{7,6},{8,9},{9,8},{10,11... | collective-permute-start | bytes 98312 | tf_op jit(solution)/shard_map/ppermute | solution.py:59
  391.9 8.2 %collective-permute-start.33 = (f32[2,120,128]{2,1,0:T(8,128)S(1)}, f32[2,120,128]{2,1,0:T(8,128)S(1)}, u32[]{:S(2)}, u32[]{:S(2)}) collective-permute-start(f32[2,120,128]{2,1,0:T(8,128)S(1)} %get-tuple-element.170), channel_id=1, source_target_pairs={{0,6},{2,0},{4,2},{6,4},{1,7},{3,1},{5,3},{7,5},{8,14},{10,8},{12,... | collective-permute-start | bytes 368648 | tf_op jit(solution)/shard_map/ppermute | solution.py:63
  394.9 6.3 %collective-permute-start.32 = (f32[2,120,128]{2,1,0:T(8,128)S(1)}, f32[2,120,128]{2,1,0:T(8,128)S(1)}, u32[]{:S(2)}, u32[]{:S(2)}) collective-permute-start(f32[2,120,128]{2,1,0:T(8,128)S(1)} %get-tuple-element.171), channel_id=1, source_target_pairs={{0,4},{2,6},{4,0},{6,2},{1,5},{3,7},{5,1},{7,3},{8,12},{10,14},{12... | collective-permute-start | bytes 368648 | tf_op jit(solution)/shard_map/ppermute | solution.py:63
  394.9 8.9 %collective-permute-start.31 = (f32[2,120,128]{2,1,0:T(8,128)S(1)}, f32[2,120,128]{2,1,0:T(8,128)S(1)}, u32[]{:S(2)}, u32[]{:S(2)}) collective-permute-start(f32[2,120,128]{2,1,0:T(8,128)S(1)} %get-tuple-element.172), channel_id=1, source_target_pairs={{0,2},{2,4},{4,6},{6,0},{1,3},{3,5},{5,7},{7,1},{8,10},{10,12},{12... | collective-permute-start | bytes 368648 | tf_op jit(solution)/shard_map/ppermute | solution.py:63
  400.1 31.7 %collective-permute-start.23 = (bf16[128,2048]{1,0:T(8,128)(2,1)}, bf16[128,2048]{1,0:T(8,128)(2,1)}, u32[]{:S(2)}, u32[]{:S(2)}) collective-permute-start(bf16[128,2048]{1,0:T(8,128)(2,1)} %get-tuple-element.96), channel_id=1, source_target_pairs={{0,4},{2,6},{4,0},{6,2},{1,5},{3,7},{5,1},{7,3},{8,12},{10,14},{12... | collective-permute-start | bytes 1572872 | tf_op jit(solution)/shard_map/ppermute | solution.py:63
  409.1 3.7 collective-permute-start.35
  421.1 14.5 %collective-permute-start.36 = (bf16[128,2048]{1,0:T(8,128)(2,1)}, bf16[128,2048]{1,0:T(8,128)(2,1)}, u32[]{:S(2)}, u32[]{:S(2)}) collective-permute-start(bf16[128,2048]{1,0:T(8,128)(2,1)} %get-tuple-element.126), channel_id=1, source_target_pairs={{0,1},{1,0},{2,3},{3,2},{4,5},{5,4},{6,7},{7,6},{8,9},{9,8},{10,11... | collective-permute-start | bytes 1572872 | tf_op jit(solution)/shard_map/ppermute | solution.py:59
  421.3 27.0 %all-to-all-start.9 = ((bf16[128,16,256]{2,1,0:T(8,128)(2,1)}), bf16[128,16,256]{2,1,0:T(8,128)(2,1)S(1)}, u32[]{:S(2)}, u32[]{:S(2)}) async-start(bf16[128,16,256]{2,1,0:T(8,128)(2,1)} %bitcast.67), calls=%async_computation.9 | async-start | bytes 2097152 | tf_op jit(solution)/shard_map/all_to_all | solution.py:55
  (113 other events, 899.0 us)
Sparse Core Ops, SparseCore 0:
  10.3 35.6 all-gather.4
  53.9 56.2 all-gather.6
  112.6 117.9 all-gather.8
  232.6 62.5 all-gather.10
